TPU v7x, 32 devices: a whole 2x2x4 slice. The times are simulated.
32 devices in a mesh: rows: 16 (over z, y, x), tm: 2 (over core).
Axes of the slice: x: 2, y: 2, z: 4, core: 2. Of those that a mesh axis runs over, the one named last changes fastest.
Arguments:
- inputs: bfloat16 [16, 2048, 512], P('rows', 'tm'), may hold values from -6 to 6
- cotangent: bfloat16 [16, 2048, 512], P('rows', 'tm'), may hold values from -6 to 6
- segment_ids: int32 [16, 2048], P('rows', 'tm'), may hold values from 0 to 2047, as said below
- qkv_weight: float32 [512, 1536], P('rows', 'tm'), may hold values from -0.25 to 0.25
- out_weight: float32 [512, 512], P('rows', 'tm'), may hold values from -1 to 1
- up_weight: float32 [512, 2048], P('rows', 'tm'), may hold values from -0.25 to 0.25
- down_weight: float32 [2048, 512], P('rows', 'tm'), may hold values from -0.125 to 0.125
- norm_gain_one: float32 [512], P('tm'), may hold values from 0.5 to 1.5
- norm_bias_one: float32 [512], P('tm'), may hold values from -3 to 3
- attn_scale: float32 [512], P('tm'), may hold values from 0.5 to 1.5
- norm_gain_two: float32 [512], P('tm'), may hold values from 0.5 to 1.5
- norm_bias_two: float32 [512], P('tm'), may hold values from -3 to 3
- mlp_scale: float32 [512], P('tm'), may hold values from 0.5 to 1.5
Outputs:
- outputs: bfloat16 [16, 2048, 512], P('rows', 'tm')
- input_grad: bfloat16 [16, 2048, 512], P('rows', 'tm')
- qkv_grad: float32 [512, 1536], P('rows', 'tm')
- out_grad: float32 [512, 512], P('rows', 'tm')
- up_grad: float32 [512, 2048], P('rows', 'tm')
- down_grad: float32 [2048, 512], P('rows', 'tm')
- gain_one_grad: float32 [512], P('tm')
- bias_one_grad: float32 [512], P('tm')
- attn_scale_grad: float32 [512], P('tm')
- gain_two_grad: float32 [512], P('tm')
- bias_two_grad: float32 [512], P('tm')
- mlp_scale_grad: float32 [512], P('tm')
Inputs may be any that keep to these rules, and one draw needn't show every extreme that they name: `segment_ids`: in every row each frame holds the index of the last frame of its utterance, so values never fall from one frame to the next, frame 0 is an utterance of its own, and the last utterance ends at the row's last frame; one utterance of each row begins within the row's first 1024 frames and ends within its last 1024.
All inputs are finite; a program needn't handle non-finite values.
Results may differ from a plain program's by a relative error of at most 0.012.
The roundings to bfloat16 on the way count: a program that leaves them out, or rounds other values in their place, can miss the bound.
Values may be sent and summed in bfloat16 or wider, within the bound.
A program may use at most 192 MiB of HBM per device.

v0:
```python
import math

import jax
import jax.numpy as jnp
from jax import lax
from jax.sharding import PartitionSpec as P

H = 8
HD = 64
WINDOW = 250
REACH = 256
QBLOCK = 512


EPSILON = 1e-05
NEGATIVE = -1e30


def prefix(part, axis, combine, identity):
    place = lax.axis_index(axis)
    gathered = jax.tree.map(lambda a: lax.all_gather(a, axis), part)
    state = jax.tree.map(lambda a, e: jnp.zeros_like(a) + jnp.asarray(e, a.dtype), part, identity)

    def one(turn, state):
        return combine(
            state, jax.tree.map(lambda a: lax.dynamic_index_in_dim(a, turn, 0, False), gathered)
        )

    return lax.fori_loop(0, place, one, state)


def shifted(block, axis, distance):
    devices = range(lax.axis_size(axis))
    route = [(i - distance, i) for i in devices if i - distance in devices]
    return lax.ppermute(block, axis, route)


def layer_norm(values, gain_vec, bias_vec):
    average = jnp.mean(values, axis=-1, keepdims=True)
    centred = values - average
    variance = jnp.mean(centred * centred, axis=-1, keepdims=True)
    return centred * lax.rsqrt(variance + EPSILON) * gain_vec + bias_vec


def gelu_exact(values):
    return jax.nn.gelu(values, approximate=False)


def rotation_tables(positions):
    half_size = HD // 2
    ladder = jnp.arange(half_size, dtype=jnp.float32)
    frequency = jnp.exp(ladder * (-2.0 * math.log(10000.0) / HD))
    angles = positions.astype(jnp.float32)[:, None] * frequency[None, :]
    return (jnp.cos(angles)[:, None, :], jnp.sin(angles)[:, None, :])


def rotate(field, cosine, sine):
    half_size = field.shape[-1] // 2
    former = field[..., :half_size]
    latter = field[..., half_size:]
    return jnp.concatenate(
        [former * cosine - latter * sine, latter * cosine + former * sine], axis=-1
    )


def outer_sum(left, right):
    return lax.dot_general(
        left, right, (((0,), (0,)), ((), ())), preferred_element_type=jnp.float32
    )


def block_allowed(begin, segment, extended_segments, valid_keys):
    offsets = (
        jnp.arange(QBLOCK, dtype=jnp.int32)[:, None]
        - jnp.arange(QBLOCK + REACH, dtype=jnp.int32)[None, :]
        + REACH
    )
    near = (offsets >= 0) & (offsets < WINDOW)
    query_segments = segment[begin : begin + QBLOCK]
    key_segments = extended_segments[begin : begin + QBLOCK + REACH]
    key_valid = valid_keys[begin : begin + QBLOCK + REACH]
    return near & (query_segments[:, None] == key_segments[None, :]) & key_valid[None, :]


def block_scores(query_block, key_window, allowed):
    raw = jnp.einsum(
        "qhd,khd->hqk", query_block, key_window, preferred_element_type=jnp.float32
    ) * (1.0 / math.sqrt(HD))
    return jnp.where(allowed[None], raw, NEGATIVE)


def local(
    inputs,
    cotangent,
    segment_ids,
    qkv_weight,
    out_weight,
    up_weight,
    down_weight,
    norm_gain_one,
    norm_bias_one,
    attn_scale,
    norm_gain_two,
    norm_bias_two,
    mlp_scale,
):
    frames = inputs.shape[1]
    width = inputs.shape[2]
    low_type = jnp.bfloat16
    gathered = (
        lax.all_gather(qkv_weight.astype(low_type), "tm", axis=1, tiled=True),
        lax.all_gather(out_weight.astype(low_type), "tm", axis=1, tiled=True),
        lax.all_gather(up_weight.astype(low_type), "tm", axis=1, tiled=True),
        lax.all_gather(down_weight.astype(low_type), "tm", axis=1, tiled=True),
        lax.all_gather(norm_gain_one.astype(low_type), "tm", axis=0, tiled=True),
        lax.all_gather(norm_bias_one.astype(low_type), "tm", axis=0, tiled=True),
        lax.all_gather(attn_scale.astype(low_type), "tm", axis=0, tiled=True),
        lax.all_gather(norm_gain_two.astype(low_type), "tm", axis=0, tiled=True),
        lax.all_gather(norm_bias_two.astype(low_type), "tm", axis=0, tiled=True),
        lax.all_gather(mlp_scale.astype(low_type), "tm", axis=0, tiled=True),
    )
    w_qkv, w_out, w_up, w_down = (
        lax.all_gather(gathered[0], "rows", axis=0, tiled=True),
        lax.all_gather(gathered[1], "rows", axis=0, tiled=True),
        lax.all_gather(gathered[2], "rows", axis=0, tiled=True),
        lax.all_gather(gathered[3], "rows", axis=0, tiled=True),
    )
    gain_one, bias_one, scale_one, gain_two, bias_two, scale_two = [
        piece.astype(jnp.float32) for piece in gathered[4:]
    ]
    segment = segment_ids[0]
    index = jnp.arange(frames, dtype=jnp.int32)
    last_run = jnp.sum((segment == segment[frames - 1]).astype(jnp.int32), keepdims=True)

    def join_runs(earlier, later):
        extends = (later[1] == frames) & (later[0] == earlier[0])
        joined = jnp.where(extends, earlier[1] + later[1], later[1])
        vacant = later[0] < 0
        return (jnp.where(vacant, earlier[0], later[0]), jnp.where(vacant, earlier[1], joined))

    before_id, before_run = prefix(
        (segment[frames - 1 :], last_run),
        "tm",
        join_runs,
        (jnp.full((1,), -1, jnp.int32), jnp.zeros((1,), jnp.int32)),
    )
    change = jnp.concatenate([jnp.ones((1,), jnp.bool_), segment[1:] != segment[:-1]])
    starts = lax.cummax(jnp.where(change, index, jnp.zeros_like(index)), axis=0)
    positions = index - starts + jnp.where(segment == before_id[0], before_run[0], 0)
    cosine, sine = rotation_tables(positions)
    source = inputs[0].astype(jnp.float32)
    normed_one, norm_one_pull = jax.vjp(layer_norm, source, gain_one, bias_one)
    normed_one_low = normed_one.astype(low_type)
    projected = jnp.dot(normed_one_low, w_qkv, preferred_element_type=jnp.float32)
    queries = rotate(projected[:, :width].reshape(frames, H, HD), cosine, sine).astype(low_type)
    keys_flat = (
        rotate(projected[:, width : 2 * width].reshape(frames, H, HD), cosine, sine)
        .reshape(frames, width)
        .astype(low_type)
    )
    values_flat = projected[:, 2 * width :].astype(low_type)
    got_keys, got_values, got_segments = shifted((keys_flat, values_flat, segment), "tm", 1)
    got_keys = got_keys[frames - REACH :]
    got_values = got_values[frames - REACH :]
    got_segments = got_segments[frames - REACH :]
    extended_keys = jnp.concatenate([got_keys, keys_flat], axis=0).reshape(REACH + frames, H, HD)
    extended_values = jnp.concatenate([got_values, values_flat], axis=0).reshape(
        REACH + frames, H, HD
    )
    extended_segments = jnp.concatenate([got_segments, segment])
    valid_keys = (lax.axis_index("tm") > 0) | (jnp.arange(REACH + frames, dtype=jnp.int32) >= REACH)
    block_count = frames // QBLOCK
    mixed_parts = []
    log_sums = []
    for block in range(block_count):
        begin = block * QBLOCK
        allowed = block_allowed(begin, segment, extended_segments, valid_keys)
        scores = block_scores(
            queries[begin : begin + QBLOCK], extended_keys[begin : begin + QBLOCK + REACH], allowed
        )
        top = jnp.max(scores, axis=-1, keepdims=True)
        weights = jnp.exp(scores - top)
        total = jnp.sum(weights, axis=-1, keepdims=True)
        probs = (weights / total).astype(low_type)
        mixed_parts.append(
            jnp.einsum(
                "hqk,khd->qhd",
                probs,
                extended_values[begin : begin + QBLOCK + REACH],
                preferred_element_type=jnp.float32,
            )
        )
        log_sums.append(top + jnp.log(total))
    mixed_low = jnp.concatenate(mixed_parts, axis=0).reshape(frames, width).astype(low_type)
    branch = jnp.dot(mixed_low, w_out, preferred_element_type=jnp.float32)
    after = source + scale_one * branch
    normed_two, norm_two_pull = jax.vjp(layer_norm, after, gain_two, bias_two)
    normed_two_low = normed_two.astype(low_type)
    hidden = jnp.dot(normed_two_low, w_up, preferred_element_type=jnp.float32)
    active, gelu_pull = jax.vjp(gelu_exact, hidden)
    active_low = active.astype(low_type)
    branch_two = jnp.dot(active_low, w_down, preferred_element_type=jnp.float32)
    result = (after + scale_two * branch_two).astype(low_type)
    again = (
        lax.all_gather(qkv_weight.astype(low_type), "tm", axis=1, tiled=True),
        lax.all_gather(out_weight.astype(low_type), "tm", axis=1, tiled=True),
        lax.all_gather(up_weight.astype(low_type), "tm", axis=1, tiled=True),
        lax.all_gather(down_weight.astype(low_type), "tm", axis=1, tiled=True),
    )
    back_qkv, back_out, back_up, back_down = (
        lax.all_gather(again[0], "rows", axis=0, tiled=True),
        lax.all_gather(again[1], "rows", axis=0, tiled=True),
        lax.all_gather(again[2], "rows", axis=0, tiled=True),
        lax.all_gather(again[3], "rows", axis=0, tiled=True),
    )
    upstream = cotangent[0].astype(jnp.float32)
    grad_scale_two = jnp.sum(upstream * branch_two, axis=0)
    grad_branch_two = (upstream * scale_two).astype(low_type)
    grad_down = outer_sum(active_low, grad_branch_two)
    grad_active = lax.dot_general(
        grad_branch_two, back_down, (((1,), (1,)), ((), ())), preferred_element_type=jnp.float32
    )
    grad_hidden = gelu_pull(grad_active)[0].astype(low_type)
    grad_up = outer_sum(normed_two_low, grad_hidden)
    grad_normed_two = lax.dot_general(
        grad_hidden, back_up, (((1,), (1,)), ((), ())), preferred_element_type=jnp.float32
    )
    after_part, grad_gain_two, grad_bias_two = norm_two_pull(grad_normed_two)
    grad_after = upstream + after_part
    grad_scale_one = jnp.sum(grad_after * branch, axis=0)
    grad_branch = (grad_after * scale_one).astype(low_type)
    grad_out = outer_sum(mixed_low, grad_branch)
    grad_mixed = lax.dot_general(
        grad_branch, back_out, (((1,), (1,)), ((), ())), preferred_element_type=jnp.float32
    )
    grad_mixed = grad_mixed.astype(low_type).reshape(frames, H, HD)
    factor = 1.0 / math.sqrt(HD)
    grad_keys_ext = jnp.zeros((REACH + frames, H, HD), jnp.float32)
    grad_values_ext = jnp.zeros((REACH + frames, H, HD), jnp.float32)
    query_grads = []
    for block in range(block_count):
        begin = block * QBLOCK
        allowed = block_allowed(begin, segment, extended_segments, valid_keys)
        query_block = queries[begin : begin + QBLOCK]
        key_window = extended_keys[begin : begin + QBLOCK + REACH]
        value_window = extended_values[begin : begin + QBLOCK + REACH]
        scores = block_scores(query_block, key_window, allowed)
        probs_full = jnp.exp(scores - log_sums[block])
        probs_low = probs_full.astype(low_type)
        grad_out_block = grad_mixed[begin : begin + QBLOCK]
        grad_probs = jnp.einsum(
            "qhd,khd->hqk", grad_out_block, value_window, preferred_element_type=jnp.float32
        )
        grad_values_ext = grad_values_ext.at[begin : begin + QBLOCK + REACH].add(
            jnp.einsum(
                "hqk,qhd->khd", probs_low, grad_out_block, preferred_element_type=jnp.float32
            )
        )
        balance = jnp.sum(grad_probs * probs_full, axis=-1, keepdims=True)
        grad_scores = (probs_full * (grad_probs - balance)).astype(low_type)
        query_grads.append(
            jnp.einsum("hqk,khd->qhd", grad_scores, key_window, preferred_element_type=jnp.float32)
            * factor
        )
        grad_keys_ext = grad_keys_ext.at[begin : begin + QBLOCK + REACH].add(
            jnp.einsum("hqk,qhd->khd", grad_scores, query_block, preferred_element_type=jnp.float32)
            * factor
        )
    grad_keys_flat = grad_keys_ext.reshape(REACH + frames, width)
    grad_values_flat = grad_values_ext.reshape(REACH + frames, width)
    back_keys, back_values = (
        shifted(grad_keys_flat[:REACH].astype(jnp.bfloat16), "tm", -1).astype(jnp.float32),
        shifted(grad_values_flat[:REACH].astype(jnp.bfloat16), "tm", -1).astype(jnp.float32),
    )
    own_keys = grad_keys_flat[REACH:]
    own_values = grad_values_flat[REACH:]
    own_keys = jnp.concatenate(
        [own_keys[: frames - REACH], own_keys[frames - REACH :] + back_keys], axis=0
    )
    own_values = jnp.concatenate(
        [own_values[: frames - REACH], own_values[frames - REACH :] + back_values], axis=0
    )
    grad_queries = rotate(jnp.concatenate(query_grads, axis=0), cosine, -sine).reshape(
        frames, width
    )
    grad_keys = rotate(own_keys.reshape(frames, H, HD), cosine, -sine).reshape(frames, width)
    grad_projected = jnp.concatenate([grad_queries, grad_keys, own_values], axis=1).astype(low_type)
    grad_qkv = outer_sum(normed_one_low, grad_projected)
    grad_normed_one = lax.dot_general(
        grad_projected, back_qkv, (((1,), (1,)), ((), ())), preferred_element_type=jnp.float32
    )
    source_part, grad_gain_one, grad_bias_one = norm_one_pull(grad_normed_one)
    input_grad = (grad_after + source_part).astype(low_type)
    reduced = (
        lax.psum_scatter(grad_qkv, "tm", scatter_dimension=1, tiled=True),
        lax.psum_scatter(grad_out, "tm", scatter_dimension=1, tiled=True),
        lax.psum_scatter(grad_up, "tm", scatter_dimension=1, tiled=True),
        lax.psum_scatter(grad_down, "tm", scatter_dimension=1, tiled=True),
        lax.psum_scatter(grad_gain_one, "tm", scatter_dimension=0, tiled=True),
        lax.psum_scatter(grad_bias_one, "tm", scatter_dimension=0, tiled=True),
        lax.psum_scatter(grad_scale_one, "tm", scatter_dimension=0, tiled=True),
        lax.psum_scatter(grad_gain_two, "tm", scatter_dimension=0, tiled=True),
        lax.psum_scatter(grad_bias_two, "tm", scatter_dimension=0, tiled=True),
        lax.psum_scatter(grad_scale_two, "tm", scatter_dimension=0, tiled=True),
    )
    qkv_grad, out_grad, up_grad, down_grad = (
        lax.psum_scatter(reduced[0], "rows", scatter_dimension=0, tiled=True),
        lax.psum_scatter(reduced[1], "rows", scatter_dimension=0, tiled=True),
        lax.psum_scatter(reduced[2], "rows", scatter_dimension=0, tiled=True),
        lax.psum_scatter(reduced[3], "rows", scatter_dimension=0, tiled=True),
    )
    vector_sums = lax.psum(
        (reduced[4], reduced[5], reduced[6], reduced[7], reduced[8], reduced[9]), "rows"
    )
    return (
        result[None],
        input_grad[None],
        qkv_grad,
        out_grad,
        up_grad,
        down_grad,
        vector_sums[0],
        vector_sums[1],
        vector_sums[2],
        vector_sums[3],
        vector_sums[4],
        vector_sums[5],
    )


def solution(mesh):
    placed = (
        P("rows", "tm", None),
        P("rows", "tm", None),
        P("rows", "tm"),
        P("rows", "tm"),
        P("rows", "tm"),
        P("rows", "tm"),
        P("rows", "tm"),
        P("tm"),
        P("tm"),
        P("tm"),
        P("tm"),
        P("tm"),
        P("tm"),
    )
    return jax.shard_map(
        local,
        mesh=mesh,
        in_specs=placed,
        out_specs=(
            P("rows", "tm", None),
            P("rows", "tm", None),
            P("rows", "tm"),
            P("rows", "tm"),
            P("rows", "tm"),
            P("rows", "tm"),
            P("tm"),
            P("tm"),
            P("tm"),
            P("tm"),
            P("tm"),
            P("tm"),
        ),
        check_vma=False,
    )
```

profile of v0, /device:TPU:0, one launch (start us, length us, event | category | flops | bytes accessed | tf_op | source)
XLA Modules:
  0.0 712.0 jit_solution(14630788319898229120)
XLA Ops:
  13.4 2.3 collective-permute-start.1
  31.5 6.1 all_gather.64
  37.6 49.6 %all_gather.65 = bf16[512,512]{1,0:T(8,128)(2,1)} all-gather(bf16[32,512]{1,0:T(8,128)(2,1)S(1)} %all_gather.64), channel_id=1, replica_groups=mesh['rows'=16,'tm'=2] {'rows'}, dimensions={0}, use_global_device_ids=true | all-gather | bytes 557056 | tf_op jit(solution)/shard_map/all_gather | solution.py:124
  101.6 2.3 copy.63
  104.2 3.4 fusion.88
  108.8 2.4 fusion.83
  111.2 2.9 copy.60
  115.3 3.1 collective-permute-start
  118.3 2.9 copy.59
  121.2 2.9 add_convert_fusion.6
  125.3 2.5 collective-permute-start.2
  127.8 2.6 fusion.89
  130.4 3.1 fusion.1
  134.9 5.2 fusion.46
  145.5 3.7 fusion.90
  149.1 3.1 fusion
  153.6 4.3 fusion.45
  158.1 2.1 fusion.81
  161.9 24.8 %multiply_convert_fusion.2 = (bf16[1024,2048]{1,0:T(8,128)(2,1)}, f32[1024,2048]{1,0:T(8,128)}, f32[1024,2048]{1,0:T(8,128)}) fusion(bf16[512,2048]{1,0:T(8,128)(2,1)} %all-gather.12.cloned.1.call-done, f32[1024,512]{0,1:T(8,128)} %copy-done.2, f32[512]{0:T(512)S(1)} %bitcast.209, f32[512]{0:T(512)S(1)} %bitcast.194, f32[1024]{0:T(1024)S(1)} %fusion.65, ...), kind=kOutput, calls=%fused_computation.21 | convolution fusion | flops 2286419968 | bytes 25178112 | tf_op jit(solution)/shard_map/dot_general | solution.py:199
  186.7 10.9 %all-gather.14.cloned.1.call-done = bf16[2048,512]{1,0:T(8,128)(2,1)} async-done(((bf16[128,512]{1,0:T(8,128)(2,1)}), bf16[2048,512]{1,0:T(8,128)(2,1)}) %all-gather.14.cloned.1.call-update) | async-done | bytes 2097168 | tf_op jit(solution)/shard_map/all_gather | solution.py:126
  197.6 9.2 %add_convert_fusion = bf16[1024,2048]{1,0:T(8,128)(2,1)S(1)} fusion(f32[1024,2048]{1,0:T(8,128)} %get-tuple-element.167, f32[1024,2048]{1,0:T(8,128)} %get-tuple-element.206, bf16[2048,512]{1,0:T(8,128)(2,1)} %all-gather.14.cloned.1.call-done, bf16[1,1024,512]{1,2,0:T(8,128)(2,1)S(1)} %copy-done.20, f32[512]{0:T(512)S(1)} %bitcast.206), kind=kOutput, calls=%fused_computation.20 | convolution fusion | flops 2178416640 | bytes 24119296 | tf_op jit(solution)/shard_map/dot_general | solution.py:220
  206.9 3.8 fusion.92
  210.6 2.9 copy.64
  213.5 3.0 multiply_reduce_fusion.2
  224.0 7.0 fusion.36
  231.0 8.9 %multiply_reduce_fusion.1 = (f32[8,512]{1,0:T(8,128)S(1)}, f32[8,512,768]{2,1,0:T(8,128)}) fusion(f32[8,512,768]{2,1,0:T(8,128)} %copy-done, f32[8,512]{1,0:T(8,128)S(1)} %log_add_fusion.1, bf16[512,8,64]{0,2,1:T(8,128)(2,1)S(1)} %bitcast.169, bf16[768,8,64]{0,2,1:T(8,128)(2,1)S(1)} %bitcast.175), kind=kOutput, calls=%fused_computation.6 | convolution fusion | flops 412086272 | bytes 26509312 | tf_op jit(solution)/shard_map/qhd,khd->hqk/dot_general | solution.py:251
  241.7 11.0 %multiply_reduce_fusion = (f32[8,512]{1,0:T(8,128)S(1)}, f32[8,512,768]{2,1,0:T(8,128)}) fusion(f32[8,512,768]{2,1,0:T(8,128)} %copy-done.1, f32[8,512]{1,0:T(8,128)S(1)} %log_add_fusion, bf16[512,8,64]{0,2,1:T(8,128)(2,1)S(1)} %bitcast.166, bf16[768,8,64]{0,2,1:T(8,128)(2,1)S(1)} %bitcast.173), kind=kOutput, calls=%fused_computation.3 | convolution fusion | flops 412086272 | bytes 26509312 | tf_op jit(solution)/shard_map/qhd,khd->hqk/dot_general | solution.py:251
  252.7 7.4 %constant_dynamic-update-slice_fusion = (bf16[1280,8,64]{0,2,1:T(8,128)(2,1)S(1)}, f32[768,8,64]{0,2,1:T(8,128)}) fusion(bf16[1280,8,64]{0,2,1:T(8,128)(2,1)S(1)} %scatter-add.16, bf16[512,8,64]{0,2,1:T(8,128)(2,1)S(1)} %bitcast.167, f32[8,512,768]{2,1,0:T(8,128)} %copy-done.1, f32[8,512]{1,0:T(8,128)S(1)} %log_add_fusion, f32[768,8,64]{0,2,1:T(8,128)S(1)} %copy-done.7), kind=kOutput, calls=%fused_computation.157 | convolution fusion | flops 409337856 | bytes 17842176 | tf_op jit(solution)/shard_map/hqk,qhd->khd/dot_general | solution.py:255
  261.2 7.7 %multiply_convert_fusion.1 = bf16[8,512,768]{2,1,0:T(8,128)(2,1)S(1)} fusion(f32[8,512,768]{2,1,0:T(8,128)} %get-tuple-element.212, f32[8,512,768]{2,1,0:T(8,128)S(1)} %bitcast.159, f32[8,512]{1,0:T(8,128)S(1)} %get-tuple-element.211, f32[8,512]{1,0:T(8,128)S(1)} %log_add_fusion.1), kind=kLoop, calls=%fused_computation.5 | loop fusion | flops 12582912 | bytes 31490048 | tf_op jit(solution)/shard_map/convert_element_type | solution.py:260
  271.1 6.3 multiply_convert_fusion
  289.4 3.7 fusion.52
  293.4 7.2 %fusion.77 = f32[512,2048]{1,0:T(8,128)} fusion(bf16[1024,2048]{1,0:T(8,128)(2,1)} %copy-done.55, f32[1024,512]{0,1:T(8,128)} %copy-done.2, f32[512]{0:T(512)S(1)} %bitcast.210, f32[512]{0:T(512)S(1)} %bitcast.197, f32[1024]{0:T(1024)S(1)} %fusion.65, f32[1024]{0:T(1024)S(1)} %broadcast_multiply_fusion), kind=kOutput, calls=%fused_computation.166 | convolution fusion | flops 2150105088 | bytes 10498048 | tf_op jit(solution)/shard_map/dot_general | solution.py:67
  301.9 6.9 fusion.56
  310.3 8.4 %reduce-scatter.17.cloned.1.call-done = f32[512,1024]{1,0:T(8,128)} async-done(((f32[512,2048]{1,0:T(8,128)}), f32[512,1024]{1,0:T(8,128)}) %reduce-scatter.17.cloned.1.call-update) | async-done | bytes 2097168 | tf_op jit(solution)/shard_map/reduce_scatter | solution.py:297
  318.8 15.7 %reduce-scatter.21.cloned.1.call-done = f32[2048,256]{1,0:T(8,128)} async-done(((f32[2048,512]{1,0:T(8,128)}), f32[2048,256]{1,0:T(8,128)}) %reduce-scatter.21.cloned.1.call-update) | async-done | bytes 2097168 | tf_op jit(solution)/shard_map/reduce_scatter | solution.py:298
  335.2 5.2 fusion.91
  340.4 2.9 copy.65
  343.3 2.1 fusion.30
  345.5 2.8 fusion.28
  348.3 8.4 %fusion.32 = (f32[512]{0:T(512)S(1)}, f32[512]{0:T(512)S(1)}, bf16[1,1024,512]{1,2,0:T(8,128)(2,1)}, bf16[1,1024,512]{1,2,0:T(8,128)(2,1)}) fusion(bf16[1,1024,512]{1,2,0:T(8,128)(2,1)S(1)} %copy-done.21, f32[1024,512]{0,1:T(8,128)} %get-tuple-element.205, f32[1024,512]{0,1:T(8,128)S(1)} %copy-done.11, f32[1024]{0:T(1024)S(1)} %negate_multiply_fusion.2, ...), kind=kOutput, calls=%fused_computation.63 | convolution fusion | flops 2157968384 | bytes 18903040 | tf_op jit(solution)/shard_map/dot_general | solution.py:202
  356.7 3.5 all-reduce.12
  360.6 2.3 copy.70
  362.9 2.3 copy.69
  365.2 43.2 %all-reduce.11 = (f32[256]{0:T(256)}, f32[256]{0:T(256)}, f32[256]{0:T(256)}, f32[256]{0:T(256)}, f32[256]{0:T(256)}, /*index=5*/f32[256]{0:T(256)}) all-reduce(f32[256]{0:T(256)S(1)} %dynamic-slice.35, f32[256]{0:T(256)S(1)} %dynamic-slice.37, f32[256]{0:T(256)S(1)} %dynamic-slice.39, ...), channel_id=1, replica_groups=mesh['rows'=16,'tm'=2] {'rows'}, use_global_device_ids=true, to_apply=%region_29.30 | all-reduce | flops 1536 | bytes 12288 | tf_op jit(solution)/shard_map/psum | solution.py:312
  408.3 6.9 reduce-scatter.15.cloned.1.call-done
  415.3 127.1 %reduce-scatter.11.cloned.1.call-done = f32[32,768]{1,0:T(8,128)} async-done(((f32[512,768]{1,0:T(8,128)}), f32[32,768]{1,0:T(8,128)}) %reduce-scatter.11.cloned.1.call-update) | async-done | bytes 98320 | tf_op jit(solution)/shard_map/reduce_scatter | solution.py:307
  542.3 82.3 %reduce-scatter.19.cloned.1.call-done = f32[32,1024]{1,0:T(8,128)} async-done(((f32[512,1024]{1,0:T(8,128)}), f32[32,1024]{1,0:T(8,128)}) %reduce-scatter.19.cloned.1.call-update) | async-done | bytes 131088 | tf_op jit(solution)/shard_map/reduce_scatter | solution.py:309
  624.7 80.6 %reduce-scatter.23.cloned.1.call-done = f32[128,256]{1,0:T(8,128)} async-done(((f32[2048,256]{1,0:T(8,128)}), f32[128,256]{1,0:T(8,128)}) %reduce-scatter.23.cloned.1.call-update) | async-done | bytes 131088 | tf_op jit(solution)/shard_map/reduce_scatter | solution.py:310
  (267 shorter events, 77.4 us)
Async XLA Ops:
  7.2 80.1 %copy-start.31 = (bf16[1,1024,512]{2,1,0:T(8,128)(2,1)S(1)}, bf16[1,1024,512]{2,1,0:T(8,128)(2,1)}, u32[]{:S(2)}) copy-start(bf16[1,1024,512]{2,1,0:T(8,128)(2,1)} %param.23) | copy-start | bytes 3145732
  7.2 97.0 %all-gather.10.cloned.1.call-start = ((), (), s32[]{:S(2)}) async-start(), calls=%async_computation.8 | async-start | bytes 1671168 | tf_op jit(solution)/shard_map/all_gather | solution.py:123
  10.3 151.6 %all-gather.12.cloned.1.call-start = ((), (), s32[]{:S(2)}) async-start(), calls=%async_computation.9 | async-start | bytes 2228224 | tf_op jit(solution)/shard_map/all_gather | solution.py:125
  11.3 77.0 %copy-start.39 = (s32[1,1024]{1,0:T(1,128)S(1)}, s32[1,1024]{1,0:T(1,128)}, u32[]{:S(2)}) copy-start(s32[1,1024]{1,0:T(1,128)} %param.25) | copy-start | bytes 12292
  13.4 184.3 %all-gather.14.cloned.1.call-start = ((), (), s32[]{:S(2)}) async-start(), calls=%async_computation.10 | async-start | bytes 2228224 | tf_op jit(solution)/shard_map/all_gather | solution.py:126
  13.4 90.4 %collective-permute-start.1 = (s32[1024]{0:T(1024)}, s32[1024]{0:T(1024)S(1)}, u32[]{:S(2)}, u32[]{:S(2)}) collective-permute-start(s32[1024]{0:T(1024)} %bitcast.185), channel_id=1, source_target_pairs={{0,1},{2,3},{4,5},{6,7},{8,9},{10,11},{12,13},{14,15},{16,17},{18,... | collective-permute-start | bytes 12296 | tf_op jit(solution)/shard_map/ppermute | solution.py:35
  18.6 72.1 %copy-start.49 = (f32[256]{0:T(256)S(1)}, f32[256]{0:T(256)}, u32[]{:S(2)}) copy-start(f32[256]{0:T(256)} %param.30) | copy-start | bytes 3076
  18.6 72.1 %copy-start.50 = (f32[256]{0:T(256)S(1)}, f32[256]{0:T(256)}, u32[]{:S(2)}) copy-start(f32[256]{0:T(256)} %param.31) | copy-start | bytes 3076
  18.6 72.1 %copy-start.51 = (f32[256]{0:T(256)S(1)}, f32[256]{0:T(256)}, u32[]{:S(2)}) copy-start(f32[256]{0:T(256)} %param.32) | copy-start | bytes 3076
  18.6 72.1 %copy-start.52 = (f32[256]{0:T(256)S(1)}, f32[256]{0:T(256)}, u32[]{:S(2)}) copy-start(f32[256]{0:T(256)} %param.33) | copy-start | bytes 3076
  18.7 72.1 %copy-start.53 = (f32[256]{0:T(256)S(1)}, f32[256]{0:T(256)}, u32[]{:S(2)}) copy-start(f32[256]{0:T(256)} %param.34) | copy-start | bytes 3076
  18.7 72.2 %copy-start.54 = (f32[256]{0:T(256)S(1)}, f32[256]{0:T(256)}, u32[]{:S(2)}) copy-start(f32[256]{0:T(256)} %param.35) | copy-start | bytes 3076
  18.7 290.2 %reduce-scatter.13.cloned.1.call-start = ((), (), s32[]{:S(2)}) async-start(), calls=%async_computation.13 | async-start | bytes 1572864 | tf_op jit(solution)/shard_map/reduce_scatter | solution.py:296
  88.0 19.7 %copy-start.37 = (f32[1024]{0:T(1024)}, f32[1024]{0:T(1024)S(1)}, u32[]{:S(2)}) copy-start(f32[1024]{0:T(1024)S(1)} %broadcast_multiply_fusion.1) | copy-start | bytes 12292
  88.3 11.5 %copy-start.44 = (f32[1024]{0:T(1024)}, f32[1024]{0:T(1024)S(1)}, u32[]{:S(2)}) copy-start(f32[1024]{0:T(1024)S(1)} %fusion.29) | copy-start | bytes 12292
  89.6 31.6 %copy-start.28 = (f32[1024,32]{0,1:T(8,128)}, f32[1024,32]{0,1:T(8,128)S(1)}, u32[]{:S(2)}) copy-start(f32[1024,32]{0,1:T(8,128)S(1)} %get-tuple-element.192) | copy-start | bytes 393220
  90.7 17.0 %copy-start.40 = (f32[1024]{0:T(1024)}, f32[1024]{0:T(1024)S(1)}, u32[]{:S(2)}) copy-start(f32[1024]{0:T(1024)S(1)} %fusion.64) | copy-start | bytes 12292
  99.8 7.9 %copy-start.46 = (f32[2,1,256]{2,1,0:T(1,128)}, f32[2,1,256]{2,1,0:T(1,128)S(1)}, u32[]{:S(2)}) copy-start(f32[2,1,256]{2,1,0:T(1,128)S(1)} %convert_element_type.190) | copy-start | bytes 6148
  101.6 6.1 copy-start.42
  115.3 24.8 %collective-permute-start = (bf16[1024,512]{1,0:T(8,128)(2,1)}, bf16[1024,512]{1,0:T(8,128)(2,1)}, u32[]{:S(2)}, u32[]{:S(2)}) collective-permute-start(bf16[1024,512]{1,0:T(8,128)(2,1)} %slice.325), channel_id=1, source_target_pairs={{0,1},{2,3},{4,5},{6,7},{8,9},{10,11},{12,13},{14,15},{16,17},{18,... | collective-permute-start | bytes 3145736 | tf_op jit(solution)/shard_map/ppermute | solution.py:35
  121.2 6.6 copy-start.36
  124.1 6.2 copy-start.8
  124.1 6.2 copy-start.14
  124.1 6.2 copy-start.16
  125.3 18.1 %collective-permute-start.2 = (bf16[1024,512]{0,1:T(8,128)(2,1)}, bf16[1024,512]{0,1:T(8,128)(2,1)}, u32[]{:S(2)}, u32[]{:S(2)}) collective-permute-start(bf16[1024,512]{0,1:T(8,128)(2,1)} %bitcast.21), channel_id=1, source_target_pairs={{0,1},{2,3},{4,5},{6,7},{8,9},{10,11},{12,13},{14,15},{16,17},{18,... | collective-permute-start | bytes 3145736 | tf_op jit(solution)/shard_map/ppermute | solution.py:35
  161.9 35.7 %copy-start.20 = (bf16[1,1024,512]{1,2,0:T(8,128)(2,1)S(1)}, bf16[1,1024,512]{1,2,0:T(8,128)(2,1)}, u32[]{:S(2)}) copy-start(bf16[1,1024,512]{1,2,0:T(8,128)(2,1)} %copy.63) | copy-start | bytes 3145732
  197.6 9.2 %copy-start.48 = (bf16[512,2048]{1,0:T(8,128)(2,1)S(1)}, bf16[512,2048]{1,0:T(8,128)(2,1)}, u32[]{:S(2)}) copy-start(bf16[512,2048]{1,0:T(8,128)(2,1)} %all-gather.12.cloned.1.call-done) | copy-start | bytes 6291460
  224.0 7.1 copy-start.25
  240.0 69.6 %reduce-scatter.9.cloned.1.call-start = ((), (), s32[]{:S(2)}) async-start(), calls=%async_computation.11 | async-start | bytes 4718592 | tf_op jit(solution)/shard_map/reduce_scatter | solution.py:295
  241.6 11.1 %copy-start.7 = (f32[768,8,64]{0,2,1:T(8,128)S(1)}, f32[768,8,64]{0,2,1:T(8,128)}, u32[]{:S(2)}) copy-start(f32[768,8,64]{0,2,1:T(8,128)} %fusion.36) | copy-start | bytes 4718596
  241.6 19.5 %slice-start = ((s8[12582912]{0:T(1024)(128)(4,1)}), s8[4194304]{0:T(1024)(128)(4,1)S(1)}, s32[]{:S(2)}) async-start(s8[12582912]{0:T(1024)(128)(4,1)} %bitcast.158), calls=%async_computation.19 | async-start | bytes 8388608
  241.6 19.5 %slice-start.1 = ((s8[12582912]{0:T(1024)(128)(4,1)}), s8[4194304]{0:T(1024)(128)(4,1)S(1)}, s32[]{:S(2)}) async-start(s8[12582912]{0:T(1024)(128)(4,1)} %bitcast.158), calls=%async_computation.20 | async-start | bytes 8388608
  252.7 8.4 %slice-start.2 = ((s8[12582912]{0:T(1024)(128)(4,1)}), s8[4194304]{0:T(1024)(128)(4,1)S(1)}, s32[]{:S(2)}) async-start(s8[12582912]{0:T(1024)(128)(4,1)} %bitcast.158), calls=%async_computation.21 | async-start | bytes 8388608
  261.1 7.8 %copy-start.9 = (bf16[1024,8,32]{0,2,1:T(8,128)(2,1)S(1)}, bf16[1024,8,32]{0,2,1:T(8,128)(2,1)}, u32[]{:S(2)}) copy-start(bf16[1024,8,32]{0,2,1:T(8,128)(2,1)} %copy-done.8) | copy-start | bytes 1572868
  261.1 9.2 %slice-start.3 = ((s8[12582912]{0:T(1024)(128)(4,1)}), s8[4194304]{0:T(1024)(128)(4,1)S(1)}, s32[]{:S(2)}) async-start(s8[12582912]{0:T(1024)(128)(4,1)} %bitcast.160), calls=%async_computation.22 | async-start | bytes 8388608
  261.1 9.2 %slice-start.4 = ((s8[12582912]{0:T(1024)(128)(4,1)}), s8[4194304]{0:T(1024)(128)(4,1)S(1)}, s32[]{:S(2)}) async-start(s8[12582912]{0:T(1024)(128)(4,1)} %bitcast.160), calls=%async_computation.23 | async-start | bytes 8388608
  282.1 6.0 collective-permute-start.4
  283.5 3.6 collective-permute-start.3
  293.1 25.7 %reduce-scatter.17.cloned.1.call-start = ((), (), s32[]{:S(2)}) async-start(), calls=%async_computation.15 | async-start | bytes 6291456 | tf_op jit(solution)/shard_map/reduce_scatter | solution.py:297
  300.6 33.9 %reduce-scatter.21.cloned.1.call-start = ((), (), s32[]{:S(2)}) async-start(), calls=%async_computation.17 | async-start | bytes 6291456 | tf_op jit(solution)/shard_map/reduce_scatter | solution.py:298
  308.8 106.5 %reduce-scatter.15.cloned.1.call-start = ((), (), s32[]{:S(2)}) async-start(), calls=%async_computation.14 | async-start | bytes 557056 | tf_op jit(solution)/shard_map/reduce_scatter | solution.py:308
  309.6 232.8 %reduce-scatter.11.cloned.1.call-start = ((), (), s32[]{:S(2)}) async-start(), calls=%async_computation.12 | async-start | bytes 1671168 | tf_op jit(solution)/shard_map/reduce_scatter | solution.py:307
  310.3 314.4 %reduce-scatter.19.cloned.1.call-start = ((), (), s32[]{:S(2)}) async-start(), calls=%async_computation.16 | async-start | bytes 2228224 | tf_op jit(solution)/shard_map/reduce_scatter | solution.py:309
  318.8 386.5 %reduce-scatter.23.cloned.1.call-start = ((), (), s32[]{:S(2)}) async-start(), calls=%async_computation.18 | async-start | bytes 2228224 | tf_op jit(solution)/shard_map/reduce_scatter | solution.py:310
  340.4 5.0 copy-start.45
  343.3 5.0 copy-start.4
  343.3 5.0 copy-start.5
  343.3 5.0 copy-start.11
  (30 other events, 75.6 us)
Sparse Core Ops, SparseCore 0:
  10.8 63.0 all-gather.9
  76.6 58.7 all-gather.11
  138.2 59.3 all-gather.13
  240.1 7.1 reduce-scatter.12
  293.2 10.1 reduce-scatter.8
  305.5 13.1 reduce-scatter.16
  321.2 13.3 reduce-scatter.20
  337.3 77.8 reduce-scatter.14
  421.4 120.9 reduce-scatter.10
  545.1 79.4 reduce-scatter.18
  627.6 77.6 reduce-scatter.22
where the time goes:
time: 720 us; the launch traced here: 712 us
  waiting for transfers between devices  334 us (46%)
  matrix products  135 us (19%)
  blocking collectives  121 us (17%)
  local copies, waits for them, and re-layouts  48.8 us (7%)
  other arithmetic  46.8 us (6%)
  between operations  15.8 us (2%)
  starting transfers between devices  11.2 us (2%)
    reduce_scatter x1, waiting for transfers between devices, local(): lax.psum_scatter(reduced[0], 'rows', scatter_dimension=0, tiled=True)  127 us
    reduce_scatter x1, waiting for transfers between devices, local(): lax.psum_scatter(reduced[2], 'rows', scatter_dimension=0, tiled=True)  82.3 us
    reduce_scatter x1, waiting for transfers between devices, local(): lax.psum_scatter(reduced[3], 'rows', scatter_dimension=0, tiled=True)  80.6 us
    all_gather x1, blocking collectives, local(): lax.all_gather(gathered[1], 'rows', axis=0, tiled=True)  49.6 us
    psum x1, blocking collectives, local(): lax.psum((reduced[4], reduced[5], reduced[6], reduced[7], reduced[8], red...  43.2 us
    dot_general x1, matrix products, local(): hidden = jnp.dot(normed_two_low, w_up, preferred_element_type=jnp.float32)  24.8 us
    unnamed x145, local copies, waits for them, and re-layouts  23.2 us
    dot_general x2, matrix products, local(): jnp.einsum('qhd,khd->hqk', grad_out_block, value_window, preferred_elemen...  20 us
  transfers between devices with their start and end apart: 16, of which 8 were waited for; matrix products, arithmetic and copies ran while one was open for 25% of the time, Pallas kernels for 0%

commit v1 on v0

--- a/solution.py
+++ b/solution.py
@@ -3,6 +3,8 @@
 import jax
 import jax.numpy as jnp
 from jax import lax
+from jax.experimental import pallas as pl
+from jax.experimental.pallas import tpu as pltpu
 from jax.sharding import PartitionSpec as P
 
 H = 8
@@ -89,7 +91,498 @@
     return jnp.where(allowed[None], raw, NEGATIVE)
 
 
+MESH_IDS = pl.DeviceIdType.MESH
+
+
+def coordinates():
+    row, core = lax.axis_index("rows"), lax.axis_index("tm")
+    return row, core, lax.rem(row, 2), lax.rem(lax.div(row, 2), 2), lax.div(row, 4)
+
+
+def peers_of(at):
+    row, core, x, y, z = at
+    found = {
+        "x": (row + 1 - 2 * x, core),
+        "y": (row + 2 - 4 * y, core),
+        "s": (row, 1 - core),
+    }
+    for k in (1, 2, 3):
+        found[k] = (lax.rem(z + k, 4) * 4 + lax.rem(row, 4), core)
+    return found
+
+
+def enter(peers):
+    barrier = pltpu.get_barrier_semaphore()
+    for peer in peers.values():
+        pl.semaphore_signal(barrier, inc=1, device_id=peer, device_id_type=MESH_IDS)
+    pl.semaphore_wait(barrier, len(peers))
+
+
+def gather_copies(full, base, sems, at, peers):
+    row, core, x, y, z = at
+    half = full.shape[4] // 2
+    low, high = pl.ds(0, half), pl.ds(half, half)
+    every = slice(None)
+    send, recv = sems
+    table = [
+        ("a1", (core, z, y, x), 1),
+        ("a2", (core, z, y, x), 2),
+        ("a3", (core, z, y, x), 3),
+        ("b1", (core, every, y, x, low), "x"),
+        ("b2", (core, every, y, x, high), "y"),
+        ("c1", (core, every, y, every, low), "y"),
+        ("c2", (core, every, every, x, high), "x"),
+        ("da", (core, every, y, x), "s"),
+        ("db1", (core, every, y, 1 - x, low), "s"),
+        ("db2", (core, every, 1 - y, x, high), "s"),
+        ("dc1", (core, every, 1 - y, every, low), "s"),
+        ("dc2", (core, every, every, 1 - x, high), "s"),
+    ]
+    out = {}
+    for offset, (name, where, peer) in enumerate(table):
+        view = full.at[where]
+        out[name] = pltpu.make_async_remote_copy(
+            src_ref=view,
+            dst_ref=view,
+            send_sem=send.at[base + offset],
+            recv_sem=recv.at[base + offset],
+            device_id=peers[peer],
+            device_id_type=MESH_IDS,
+        )
+    return out
+
+
+GATHER_STEPS = (
+    ((), ("a1", "a2", "a3")),
+    (("a1", "a2", "a3"), ("b1", "b2", "da")),
+    (("b1", "b2"), ("c1", "c2", "db1", "db2")),
+    (("c1", "c2"), ("dc1", "dc2")),
+    (("da", "db1", "db2", "dc1", "dc2"), ()),
+)
+
+
+def gather_step(copies, step):
+    waits, starts = GATHER_STEPS[step]
+    for name in waits:
+        copies[name].wait_recv()
+    for name in starts:
+        copies[name].start()
+
+
+def drain(copies):
+    for copy in copies.values():
+        copy.wait_send()
+
+
+def gather_kernel(*refs):
+    shards, fulls, sems = refs[:4], refs[4:8], refs[8:]
+    at = coordinates()
+    peers = peers_of(at)
+    row, core, x, y, z = at
+    for shard, full in zip(shards, fulls):
+        full[core, z, y, x] = shard[...].astype(jnp.bfloat16)
+    enter(peers)
+    copies = [gather_copies(full, 12 * i, sems, at, peers) for i, full in enumerate(fulls)]
+    for step in range(5):
+        for each in copies:
+            gather_step(each, step)
+    for each in copies:
+        drain(each)
+
+
+def gather_weights(*shards):
+    return pl.pallas_call(
+        gather_kernel,
+        out_shape=[
+            jax.ShapeDtypeStruct((2, 4, 2, 2) + s.shape, jnp.bfloat16) for s in shards
+        ],
+        in_specs=[pl.BlockSpec(memory_space=pltpu.VMEM)] * 4,
+        out_specs=[pl.BlockSpec(memory_space=pltpu.VMEM)] * 4,
+        scratch_shapes=[pltpu.SemaphoreType.DMA((48,)), pltpu.SemaphoreType.DMA((48,))],
+        compiler_params=pltpu.CompilerParams(
+            collective_id=0, has_side_effects=True, vmem_limit_bytes=50 * 2**20
+        ),
+    )(*shards)
+
+
+SCATTER_SLOTS = 8
+
+
+def scatter_shapes(rows, columns):
+    half = rows // 2
+    low = jnp.bfloat16
+    return [
+        pltpu.VMEM((4, 2, 2, rows, columns), low),
+        pltpu.VMEM((4, 2, 2, rows, columns), low),
+        pltpu.VMEM((2, 4, 2, half, columns), low),
+        pltpu.VMEM((2, 4, 2, half, columns), low),
+        pltpu.VMEM((2, 4, half, columns), low),
+        pltpu.VMEM((2, 4, half, columns), low),
+        pltpu.VMEM((3, rows, columns), low),
+        pltpu.VMEM((3, rows, columns), low),
+    ]
+
+
+def scatter_copies(bufs, base, sems, peers):
+    s_out, s_in, c_out, c_in, b_out, b_in, a_out, a_in = bufs
+    send, recv = sems
+    table = [
+        ("d", s_out, s_in, "s"),
+        ("c1", c_out.at[0], c_in.at[0], "y"),
+        ("c2", c_out.at[1], c_in.at[1], "x"),
+        ("b1", b_out.at[0], b_in.at[0], "x"),
+        ("b2", b_out.at[1], b_in.at[1], "y"),
+        ("a1", a_out.at[0], a_in.at[0], 1),
+        ("a2", a_out.at[1], a_in.at[1], 2),
+        ("a3", a_out.at[2], a_in.at[2], 3),
+    ]
+    return {
+        name: pltpu.make_async_remote_copy(
+            src_ref=src,
+            dst_ref=dst,
+            send_sem=send.at[base + offset],
+            recv_sem=recv.at[base + offset],
+            device_id=peers[peer],
+            device_id_type=MESH_IDS,
+        )
+        for offset, (name, src, dst, peer) in enumerate(table)
+    }
+
+
+def scatter_step(step, copies, own, bufs, result, at):
+    s_out, s_in, c_out, c_in, b_out, b_in, a_out, a_in = bufs
+    row, core, x, y, z = at
+    half = own.shape[3] // 2
+    low, high = pl.ds(0, half), pl.ds(half, half)
+    f32, bf16 = jnp.float32, jnp.bfloat16
+    if step == 0:
+        copies["d"].start()
+    if step == 1:
+        copies["d"].wait_recv()
+        for k in range(4):
+            for i in range(2):
+                c_out[0, k, i] = (
+                    own[k, 1 - y, i, low] + s_in[k, 1 - y, i, low].astype(f32)
+                ).astype(bf16)
+        copies["c1"].start()
+        for k in range(4):
+            for i in range(2):
+                c_out[1, k, i] = (
+                    own[k, i, 1 - x, high] + s_in[k, i, 1 - x, high].astype(f32)
+                ).astype(bf16)
+        copies["c2"].start()
+    if step == 2:
+        copies["c1"].wait_recv()
+        for k in range(4):
+            b_out[0, k] = (
+                own[k, y, 1 - x, low]
+                + s_in[k, y, 1 - x, low].astype(f32)
+                + c_in[0, k, 1 - x].astype(f32)
+            ).astype(bf16)
+        copies["b1"].start()
+        copies["c2"].wait_recv()
+        for k in range(4):
+            b_out[1, k] = (
+                own[k, 1 - y, x, high]
+                + s_in[k, 1 - y, x, high].astype(f32)
+                + c_in[1, k, 1 - y].astype(f32)
+            ).astype(bf16)
+        copies["b2"].start()
+    def summed(k):
+        one = (
+            own[k, y, x, low]
+            + s_in[k, y, x, low].astype(f32)
+            + c_in[0, k, x].astype(f32)
+            + b_in[0, k].astype(f32)
+        )
+        two = (
+            own[k, y, x, high]
+            + s_in[k, y, x, high].astype(f32)
+            + c_in[1, k, y].astype(f32)
+            + b_in[1, k].astype(f32)
+        )
+        return jnp.concatenate([one, two], axis=0)
+
+    if step == 3:
+        copies["b1"].wait_recv()
+        copies["b2"].wait_recv()
+        for k in (1, 2, 3):
+            a_out[k - 1] = summed(lax.rem(z + k, 4)).astype(bf16)
+            copies["a%d" % k].start()
+        result[...] = summed(z)
+    if step == 4:
+        for k in (1, 2, 3):
+            copies["a%d" % k].wait_recv()
+        result[...] = result[...] + (
+            a_in[0].astype(f32) + a_in[1].astype(f32) + a_in[2].astype(f32)
+        )
+
+
+def scatter_kernel(*refs):
+    owns, others, results = refs[:4], refs[4:8], refs[8:12]
+    bufs = [refs[12 + 8 * i : 20 + 8 * i] for i in range(4)]
+    sems = refs[44:]
+    at = coordinates()
+    peers = peers_of(at)
+    for other, each in zip(others, bufs):
+        each[0][...] = other[...]
+    enter(peers)
+    copies = [scatter_copies(each, 8 * i, sems, peers) for i, each in enumerate(bufs)]
+    for step in range(5):
+        for i in range(4):
+            scatter_step(step, copies[i], owns[i], bufs[i], results[i], at)
+    for each in copies:
+        drain(each)
+
+
+def scatter_grads(owns, others):
+    shapes = [o.shape[3:] for o in owns]
+    return pl.pallas_call(
+        scatter_kernel,
+        out_shape=[jax.ShapeDtypeStruct(s, jnp.float32) for s in shapes],
+        in_specs=[pl.BlockSpec(memory_space=pltpu.VMEM)] * 8,
+        out_specs=[pl.BlockSpec(memory_space=pltpu.VMEM)] * 4,
+        scratch_shapes=[b for s in shapes for b in scatter_shapes(*s)]
+        + [pltpu.SemaphoreType.DMA((32,)), pltpu.SemaphoreType.DMA((32,))],
+        compiler_params=pltpu.CompilerParams(
+            collective_id=1, has_side_effects=True, vmem_limit_bytes=56 * 2**20
+        ),
+    )(*owns, *others)
+
+
+def whole_weight(blocks):
+    columns = blocks.shape[-1]
+    flat = blocks.reshape(2, -1, columns)
+    return jnp.concatenate([flat[0], flat[1]], axis=1)
+
+
+def split_grad(grad):
+    rows, columns = grad.shape
+    core = lax.axis_index("tm")
+    pieces = grad.reshape(4, 2, 2, rows // 16, 2, columns // 2)
+    own = lax.dynamic_index_in_dim(pieces, core, 4, False)
+    other = lax.dynamic_index_in_dim(pieces, 1 - core, 4, False).astype(jnp.bfloat16)
+    return own, other
+
+
 def local(
+    inputs,
+    cotangent,
+    segment_ids,
+    qkv_weight,
+    out_weight,
+    up_weight,
+    down_weight,
+    norm_gain_one,
+    norm_bias_one,
+    attn_scale,
+    norm_gain_two,
+    norm_bias_two,
+    mlp_scale,
+):
+    frames = inputs.shape[1]
+    width = inputs.shape[2]
+    low_type = jnp.bfloat16
+    gathered = (
+        None, None, None, None,
+        lax.all_gather(norm_gain_one.astype(low_type), "tm", axis=0, tiled=True),
+        lax.all_gather(norm_bias_one.astype(low_type), "tm", axis=0, tiled=True),
+        lax.all_gather(attn_scale.astype(low_type), "tm", axis=0, tiled=True),
+        lax.all_gather(norm_gain_two.astype(low_type), "tm", axis=0, tiled=True),
+        lax.all_gather(norm_bias_two.astype(low_type), "tm", axis=0, tiled=True),
+        lax.all_gather(mlp_scale.astype(low_type), "tm", axis=0, tiled=True),
+    )
+    w_qkv, w_out, w_up, w_down = [
+        whole_weight(w) for w in gather_weights(qkv_weight, out_weight, up_weight, down_weight)
+    ]
+    gain_one, bias_one, scale_one, gain_two, bias_two, scale_two = [
+        piece.astype(jnp.float32) for piece in gathered[4:]
+    ]
+    segment = segment_ids[0]
+    index = jnp.arange(frames, dtype=jnp.int32)
+    last_run = jnp.sum((segment == segment[frames - 1]).astype(jnp.int32), keepdims=True)
+
+    def join_runs(earlier, later):
+        extends = (later[1] == frames) & (later[0] == earlier[0])
+        joined = jnp.where(extends, earlier[1] + later[1], later[1])
+        vacant = later[0] < 0
+        return (jnp.where(vacant, earlier[0], later[0]), jnp.where(vacant, earlier[1], joined))
+
+    before_id, before_run = prefix(
+        (segment[frames - 1 :], last_run),
+        "tm",
+        join_runs,
+        (jnp.full((1,), -1, jnp.int32), jnp.zeros((1,), jnp.int32)),
+    )
+    change = jnp.concatenate([jnp.ones((1,), jnp.bool_), segment[1:] != segment[:-1]])
+    starts = lax.cummax(jnp.where(change, index, jnp.zeros_like(index)), axis=0)
+    positions = index - starts + jnp.where(segment == before_id[0], before_run[0], 0)
+    cosine, sine = rotation_tables(positions)
+    source = inputs[0].astype(jnp.float32)
+    normed_one, norm_one_pull = jax.vjp(layer_norm, source, gain_one, bias_one)
+    normed_one_low = normed_one.astype(low_type)
+    projected = jnp.dot(normed_one_low, w_qkv, preferred_element_type=jnp.float32)
+    queries = rotate(projected[:, :width].reshape(frames, H, HD), cosine, sine).astype(low_type)
+    keys_flat = (
+        rotate(projected[:, width : 2 * width].reshape(frames, H, HD), cosine, sine)
+        .reshape(frames, width)
+        .astype(low_type)
+    )
+    values_flat = projected[:, 2 * width :].astype(low_type)
+    got_keys, got_values, got_segments = shifted((keys_flat, values_flat, segment), "tm", 1)
+    got_keys = got_keys[frames - REACH :]
+    got_values = got_values[frames - REACH :]
+    got_segments = got_segments[frames - REACH :]
+    extended_keys = jnp.concatenate([got_keys, keys_flat], axis=0).reshape(REACH + frames, H, HD)
+    extended_values = jnp.concatenate([got_values, values_flat], axis=0).reshape(
+        REACH + frames, H, HD
+    )
+    extended_segments = jnp.concatenate([got_segments, segment])
+    valid_keys = (lax.axis_index("tm") > 0) | (jnp.arange(REACH + frames, dtype=jnp.int32) >= REACH)
+    block_count = frames // QBLOCK
+    mixed_parts = []
+    log_sums = []
+    for block in range(block_count):
+        begin = block * QBLOCK
+        allowed = block_allowed(begin, segment, extended_segments, valid_keys)
+        scores = block_scores(
+            queries[begin : begin + QBLOCK], extended_keys[begin : begin + QBLOCK + REACH], allowed
+        )
+        top = jnp.max(scores, axis=-1, keepdims=True)
+        weights = jnp.exp(scores - top)
+        total = jnp.sum(weights, axis=-1, keepdims=True)
+        probs = (weights / total).astype(low_type)
+        mixed_parts.append(
+            jnp.einsum(
+                "hqk,khd->qhd",
+                probs,
+                extended_values[begin : begin + QBLOCK + REACH],
+                preferred_element_type=jnp.float32,
+            )
+        )
+        log_sums.append(top + jnp.log(total))
+    mixed_low = jnp.concatenate(mixed_parts, axis=0).reshape(frames, width).astype(low_type)
+    branch = jnp.dot(mixed_low, w_out, preferred_element_type=jnp.float32)
+    after = source + scale_one * branch
+    normed_two, norm_two_pull = jax.vjp(layer_norm, after, gain_two, bias_two)
+    normed_two_low = normed_two.astype(low_type)
+    hidden = jnp.dot(normed_two_low, w_up, preferred_element_type=jnp.float32)
+    active, gelu_pull = jax.vjp(gelu_exact, hidden)
+    active_low = active.astype(low_type)
+    branch_two = jnp.dot(active_low, w_down, preferred_element_type=jnp.float32)
+    result = (after + scale_two * branch_two).astype(low_type)
+    back_qkv, back_out, back_up, back_down = w_qkv, w_out, w_up, w_down
+    upstream = cotangent[0].astype(jnp.float32)
+    grad_scale_two = jnp.sum(upstream * branch_two, axis=0)
+    grad_branch_two = (upstream * scale_two).astype(low_type)
+    grad_down = outer_sum(active_low, grad_branch_two)
+    grad_active = lax.dot_general(
+        grad_branch_two, back_down, (((1,), (1,)), ((), ())), preferred_element_type=jnp.float32
+    )
+    grad_hidden = gelu_pull(grad_active)[0].astype(low_type)
+    grad_up = outer_sum(normed_two_low, grad_hidden)
+    grad_normed_two = lax.dot_general(
+        grad_hidden, back_up, (((1,), (1,)), ((), ())), preferred_element_type=jnp.float32
+    )
+    after_part, grad_gain_two, grad_bias_two = norm_two_pull(grad_normed_two)
+    grad_after = upstream + after_part
+    grad_scale_one = jnp.sum(grad_after * branch, axis=0)
+    grad_branch = (grad_after * scale_one).astype(low_type)
+    grad_out = outer_sum(mixed_low, grad_branch)
+    grad_mixed = lax.dot_general(
+        grad_branch, back_out, (((1,), (1,)), ((), ())), preferred_element_type=jnp.float32
+    )
+    grad_mixed = grad_mixed.astype(low_type).reshape(frames, H, HD)
+    factor = 1.0 / math.sqrt(HD)
+    grad_keys_ext = jnp.zeros((REACH + frames, H, HD), jnp.float32)
+    grad_values_ext = jnp.zeros((REACH + frames, H, HD), jnp.float32)
+    query_grads = []
+    for block in range(block_count):
+        begin = block * QBLOCK
+        allowed = block_allowed(begin, segment, extended_segments, valid_keys)
+        query_block = queries[begin : begin + QBLOCK]
+        key_window = extended_keys[begin : begin + QBLOCK + REACH]
+        value_window = extended_values[begin : begin + QBLOCK + REACH]
+        scores = block_scores(query_block, key_window, allowed)
+        probs_full = jnp.exp(scores - log_sums[block])
+        probs_low = probs_full.astype(low_type)
+        grad_out_block = grad_mixed[begin : begin + QBLOCK]
+        grad_probs = jnp.einsum(
+            "qhd,khd->hqk", grad_out_block, value_window, preferred_element_type=jnp.float32
+        )
+        grad_values_ext = grad_values_ext.at[begin : begin + QBLOCK + REACH].add(
+            jnp.einsum(
+                "hqk,qhd->khd", probs_low, grad_out_block, preferred_element_type=jnp.float32
+            )
+        )
+        balance = jnp.sum(grad_probs * probs_full, axis=-1, keepdims=True)
+        grad_scores = (probs_full * (grad_probs - balance)).astype(low_type)
+        query_grads.append(
+            jnp.einsum("hqk,khd->qhd", grad_scores, key_window, preferred_element_type=jnp.float32)
+            * factor
+        )
+        grad_keys_ext = grad_keys_ext.at[begin : begin + QBLOCK + REACH].add(
+            jnp.einsum("hqk,qhd->khd", grad_scores, query_block, preferred_element_type=jnp.float32)
+            * factor
+        )
+    grad_keys_flat = grad_keys_ext.reshape(REACH + frames, width)
+    grad_values_flat = grad_values_ext.reshape(REACH + frames, width)
+    back_keys, back_values = (
+        shifted(grad_keys_flat[:REACH].astype(jnp.bfloat16), "tm", -1).astype(jnp.float32),
+        shifted(grad_values_flat[:REACH].astype(jnp.bfloat16), "tm", -1).astype(jnp.float32),
+    )
+    own_keys = grad_keys_flat[REACH:]
+    own_values = grad_values_flat[REACH:]
+    own_keys = jnp.concatenate(
+        [own_keys[: frames - REACH], own_keys[frames - REACH :] + back_keys], axis=0
+    )
+    own_values = jnp.concatenate(
+        [own_values[: frames - REACH], own_values[frames - REACH :] + back_values], axis=0
+    )
+    grad_queries = rotate(jnp.concatenate(query_grads, axis=0), cosine, -sine).reshape(
+        frames, width
+    )
+    grad_keys = rotate(own_keys.reshape(frames, H, HD), cosine, -sine).reshape(frames, width)
+    grad_projected = jnp.concatenate([grad_queries, grad_keys, own_values], axis=1).astype(low_type)
+    grad_qkv = outer_sum(normed_one_low, grad_projected)
+    grad_normed_one = lax.dot_general(
+        grad_projected, back_qkv, (((1,), (1,)), ((), ())), preferred_element_type=jnp.float32
+    )
+    source_part, grad_gain_one, grad_bias_one = norm_one_pull(grad_normed_one)
+    input_grad = (grad_after + source_part).astype(low_type)
+    reduced = (
+        None, None, None, None,
+        lax.psum_scatter(grad_gain_one, "tm", scatter_dimension=0, tiled=True),
+        lax.psum_scatter(grad_bias_one, "tm", scatter_dimension=0, tiled=True),
+        lax.psum_scatter(grad_scale_one, "tm", scatter_dimension=0, tiled=True),
+        lax.psum_scatter(grad_gain_two, "tm", scatter_dimension=0, tiled=True),
+        lax.psum_scatter(grad_bias_two, "tm", scatter_dimension=0, tiled=True),
+        lax.psum_scatter(grad_scale_two, "tm", scatter_dimension=0, tiled=True),
+    )
+    halves = [split_grad(g) for g in (grad_qkv, grad_out, grad_up, grad_down)]
+    qkv_grad, out_grad, up_grad, down_grad = scatter_grads(
+        [h[0] for h in halves], [h[1] for h in halves]
+    )
+    vector_sums = lax.psum(
+        (reduced[4], reduced[5], reduced[6], reduced[7], reduced[8], reduced[9]), "rows"
+    )
+    return (
+        result[None],
+        input_grad[None],
+        qkv_grad,
+        out_grad,
+        up_grad,
+        down_grad,
+        vector_sums[0],
+        vector_sums[1],
+        vector_sums[2],
+        vector_sums[3],
+        vector_sums[4],
+        vector_sums[5],
+    )
+
+
+def local_plain(
     inputs,
     cotangent,
     segment_ids,
@@ -344,8 +837,9 @@
         P("tm"),
         P("tm"),
     )
+    staged = mesh.shape["rows"] == 16 and mesh.shape["tm"] == 2
     return jax.shard_map(
-        local,
+        local if staged else local_plain,
         mesh=mesh,
         in_specs=placed,
         out_specs=(

time: 720 us -> 460 us (0.64)
  waiting for transfers between devices: 334 us -> 0.01 us
  Pallas kernels: 0 us -> 97.7 us
  blocking collectives: 121 us -> 57.6 us
  local copies, waits for them, and re-layouts: 48.8 us -> 83.7 us
  other arithmetic: 46.8 us -> 66.5 us
  between operations: 15.8 us -> 2.91 us
    reduce_scatter x8 -> x0, waiting for transfers between devices: 321 us -> none  [the longest x1 127 us: local(): lax.psum_scatter(reduced[0], 'rows', scatter_dimension=0, tiled=True)]
    pallas_call x0 -> x2, Pallas kernels: none -> 97.7 us  [the longest x1 50 us: scatter_grads(): pl.pallas_call(scatter_kernel, out_shape=[jax.ShapeDtypeStruct(s, jnp.flo...]
    all_gather x5 -> x0, blocking collectives: 61.9 us -> none  [the longest x1 49.6 us: local(): lax.all_gather(gathered[1], 'rows', axis=0, tiled=True)]
    convert_element_type x4 -> x3, other arithmetic: 3.57 us -> 22 us  [the longest x1 20.4 us: local(): active_low = active.astype(low_type)]
    all_gather x3 -> x0, waiting for transfers between devices: 11 us -> none  [the longest x1 10.9 us: local(): lax.all_gather(gathered[3], 'rows', axis=0, tiled=True)]
    dot_general x2, matrix products: 14.4 us -> 6.38 us  [local(): jnp.einsum('hqk,qhd->khd', probs_low, grad_out_block, preferred_element_t...]
    unnamed x145 -> x203, local copies, waits for them, and re-layouts: 23.2 us -> 23.9 us
  transfers between devices with their start and end apart: 16 -> 5, of which waited for: 8 -> 0; matrix products, arithmetic and copies ran while one was open for 25% -> 22% of each run, Pallas kernels for 0% -> 11%
where the time goes in v1:
time: 460 us; the launch traced here: 453 us
  matrix products  128 us (28%)
  Pallas kernels  97.7 us (21%)
  local copies, waits for them, and re-layouts  83.7 us (18%)
  other arithmetic  66.5 us (14%)
  blocking collectives  57.6 us (13%)
  starting transfers between devices  16.2 us (4%)
    pallas_call x1, Pallas kernels, scatter_grads(): pl.pallas_call(scatter_kernel, out_shape=[jax.ShapeDtypeStruct(s, jnp.flo...  50 us
    pallas_call x1, Pallas kernels, gather_weights(): pl.pallas_call(gather_kernel, out_shape=[jax.ShapeDtypeStruct((2, 4, 2, 2...  47.7 us
    psum x1, blocking collectives, local(): lax.psum((reduced[4], reduced[5], reduced[6], reduced[7], reduced[8], red...  40.9 us
    unnamed x203, local copies, waits for them, and re-layouts  23.9 us
    dot_general x1, matrix products, local(): hidden = jnp.dot(normed_two_low, w_up, preferred_element_type=jnp.float32)  21.8 us
    convert_element_type x1, other arithmetic, local(): active_low = active.astype(low_type)  20.4 us
    ppermute x5, starting transfers between devices, shifted(): return lax.ppermute(block, axis, route)  16.2 us
    dot_general x2, matrix products, local(): jnp.einsum('qhd,khd->hqk', grad_out_block, value_window, preferred_elemen...  13.7 us
  transfers between devices with their start and end apart: 5, of which 0 were waited for; matrix products, arithmetic and copies ran while one was open for 22% of the time, Pallas kernels for 11%

profile of v1, /device:TPU:0, one launch (start us, length us, event | category | flops | bytes accessed | tf_op | source)
XLA Modules:
  0.0 452.9 jit_solution(5551033625113185500)
XLA Ops:
  0.7 2.5 collective-permute-start.1
  10.2 47.7 %shard_map.220 = (bf16[2,4,2,2,32,768]{5,4,3,2,1,0:T(8,128)(2,1)S(1)}, bf16[2,4,2,2,32,256]{5,4,3,2,1,0:T(8,128)(2,1)S(1)}, bf16[2,4,2,2,32,1024]{5,4,3,2,1,0:T(8,128)(2,1)}, bf16[2,4,2,2,128,256]{5,4,3,2,1,0:T(8,128)(2,1)}) custom-call(f32[32,768]{1,0:T(8,128)S(1)} %copy-done.2, f32[32,256]{1,0:T(8,128)S(1)} %copy-done.3, f32[32,1024]{1,0:T(8,128)S(1)} %copy-done, ...), custom_call_target="tpu_custom_call" | custom-call | tf_op jit(solution)/shard_map/pallas_call | solution.py:194
  58.5 4.5 %fusion.117 = (bf16[1024,1536]{1,0:T(8,128)(2,1)S(1)}, f32[1024,1536]{1,0:T(8,128)}) fusion(bf16[1024,512]{0,1:T(8,128)(2,1)S(1)} %fusion.46, bf16[512,768]{1,0:T(8,128)(2,1)S(1)} %bitcast.321, bf16[512,768]{1,0:T(8,128)(2,1)S(1)} %bitcast.319), kind=kOutput, calls=%fused_computation.228 | convolution fusion | flops 1615331328 | bytes 12058624 | tf_op jit(solution)/shard_map/dot_general | solution.py:424
  65.8 3.3 collective-permute-start
  76.9 4.7 %fusion.108 = (f32[1024,512]{1,0:T(8,128)}, f32[1024,512]{1,0:T(8,128)}) fusion(f32[1024,1536]{1,0:T(8,128)} %get-tuple-element.223), kind=kLoop, calls=%fused_computation.219 | loop fusion | bytes 8388608 | tf_op jit(solution)/shard_map/slice | solution.py:427
  81.5 2.9 copy.65
  84.5 2.9 copy.64
  88.6 3.7 add_convert_fusion.6
  93.5 7.5 %collective-permute-start.2 = (bf16[1024,512]{0,1:T(8,128)(2,1)}, bf16[1024,512]{0,1:T(8,128)(2,1)}, u32[]{:S(2)}, u32[]{:S(2)}) collective-permute-start(bf16[1024,512]{0,1:T(8,128)(2,1)} %bitcast.23), channel_id=1, source_target_pairs={{0,1},{2,3},{4,5},{6,7},{8,9},{10,11},{12,13},{14,15},{16,17},{18,... | collective-permute-start | bytes 3145736 | tf_op jit(solution)/shard_map/ppermute | solution.py:37
  101.7 2.1 slice.378
  108.0 3.5 fusion.110
  111.5 2.3 copy.66
  115.4 8.1 %fusion.118 = (f32[8,512]{1,0:T(8,128)S(1)}, f32[8,512,768]{2,1,0:T(8,128)}) fusion(bf16[1024,8,32]{0,2,1:T(8,128)(2,1)} %copy-done.24, bf16[1024,8,32]{0,2,1:T(8,128)(2,1)} %copy-done.22, bf16[1024,8,32]{0,2,1:T(8,128)(2,1)S(1)} %get-tuple-element.211, bf16[1024,8,32]{0,2,1:T(8,128)(2,1)} %get-tuple-element.212, pred[512,768]{1,0:T(8,128)(4,1)S(1)} %and_and_fusion), kind=kOutput, calls=%fused_computation.229 | convolution fusion | flops 414707712 | bytes 15089664 | tf_op jit(solution)/shard_map/qhd,khd->hqk/dot_general | solution.py:88
  123.5 7.0 %fusion.1 = f32[8,512]{1,0:T(8,128)S(1)} fusion(f32[8,512,768]{2,1,0:T(8,128)} %get-tuple-element.225, f32[8,512]{1,0:T(8,128)S(1)} %get-tuple-element.224), kind=kLoop, calls=%fused_computation.17 | loop fusion | flops 6287360 | bytes 12615680 | tf_op jit(solution)/shard_map/reduce_sum | solution.py:453
  130.5 7.1 %fusion.67 = bf16[512,8,64]{0,2,1:T(8,128)(2,1)} fusion(bf16[768,8,64]{0,2,1:T(8,128)(2,1)S(1)} %bitcast.312, f32[8,512,768]{2,1,0:T(8,128)} %get-tuple-element.225, f32[8,512]{1,0:T(8,128)S(1)} %fusion.1, f32[8,512]{1,0:T(8,128)S(1)} %get-tuple-element.224), kind=kOutput, calls=%fused_computation.129 | convolution fusion | flops 412352512 | bytes 13926400 | tf_op jit(solution)/shard_map/hqk,khd->qhd/dot_general | solution.py:456
  144.7 2.3 all-gather
  154.0 4.3 fusion.119
  158.3 3.1 fusion
  161.4 3.9 fusion.66
  165.6 2.1 fusion.106
  168.1 21.8 %fusion.4 = (f32[1024,2048]{1,0:T(8,128)}, f32[1024,2048]{1,0:T(8,128)S(1)}) fusion(bf16[512,1024]{1,0:T(8,128)(2,1)S(1)} %bitcast.333, bf16[512,1024]{1,0:T(8,128)(2,1)S(1)} %bitcast.331, f32[1024,512]{0,1:T(8,128)S(1)} %get-tuple-element.184, f32[512]{0:T(512)S(1)} %bitcast.357, f32[512]{0:T(512)S(1)} %bitcast.350, f32[1024]{0:T(1024)S(1)} %fusion.88, ...), kind=kOutput, calls=%fused_computation.20 | convolution fusion | flops 2284322816 | bytes 20983808 | tf_op jit(solution)/shard_map/dot_general | solution.py:469
  189.9 12.1 %add_convert_fusion = bf16[1024,2048]{1,0:T(8,128)(2,1)} fusion(f32[1024,2048]{1,0:T(8,128)} %get-tuple-element.229, f32[1024,2048]{1,0:T(8,128)S(1)} %get-tuple-element.230, bf16[1024,512]{0,1:T(8,128)(2,1)} %fusion.50, bf16[2048,256]{1,0:T(8,128)(2,1)} %bitcast.304, bf16[2048,256]{1,0:T(8,128)(2,1)S(1)} %bitcast.303), kind=kOutput, calls=%fused_computation.41 | convolution fusion | flops 2181038080 | bytes 24117248 | tf_op jit(solution)/shard_map/dot_general | solution.py:479
  202.0 5.8 %multiply_reduce_fusion.2 = (f32[512]{0:T(512)S(1)}, f32[1024]{0:T(1024)S(1)}, f32[512]{0:T(512)S(1)}, f32[1024,512]{0,1:T(8,128)S(1)}) fusion(f32[1024,512]{0,1:T(8,128)S(1)} %get-tuple-element.184, f32[1024]{0:T(1024)S(1)} %fusion.88, f32[1024]{0:T(1024)S(1)} %broadcast_multiply_fusion, f32[512]{0:T(512)S(1)} %bitcast.351, ...), kind=kOutput, calls=%fused_computation.97 | convolution fusion | flops 2155870208 | bytes 10504192 | tf_op jit(solution)/shard_map/dot_general | solution.py:484
  207.8 4.4 fusion.104
  216.3 3.0 fusion.55
  219.7 3.4 constant_dynamic-update-slice_fusion
  224.7 20.4 %fusion.7 = bf16[2048,1024]{0,1:T(8,128)(2,1)} fusion(f32[1024,2048]{1,0:T(8,128)} %copy-done.8), kind=kLoop, calls=%fused_computation.23 | loop fusion | flops 136314880 | bytes 12582912 | tf_op jit(solution)/shard_map/convert_element_type | solution.py:471
  245.1 6.2 %multiply_reduce_fusion = (f32[8,512]{1,0:T(8,128)S(1)}, f32[8,512,768]{2,1,0:T(8,128)}) fusion(f32[8,512,768]{2,1,0:T(8,128)S(1)} %bitcast.287, f32[8,512]{1,0:T(8,128)S(1)} %log_add_fusion, bf16[512,8,64]{0,2,1:T(8,128)(2,1)S(1)} %bitcast.298, bf16[768,8,64]{0,2,1:T(8,128)(2,1)S(1)} %bitcast.313), kind=kOutput, calls=%fused_computation.4 | convolution fusion | flops 412086272 | bytes 26509312 | tf_op jit(solution)/shard_map/qhd,khd->hqk/dot_general | solution.py:510
  251.3 7.5 %multiply_reduce_fusion.1 = (f32[8,512]{1,0:T(8,128)S(1)}, f32[8,512,768]{2,1,0:T(8,128)}) fusion(f32[8,512,768]{2,1,0:T(8,128)S(1)} %get-tuple-element.227, f32[8,512]{1,0:T(8,128)S(1)} %log_add_fusion.1, bf16[512,8,64]{0,2,1:T(8,128)(2,1)S(1)} %bitcast.296, bf16[768,8,64]{0,2,1:T(8,128)(2,1)} %bitcast.314), kind=kOutput, calls=%fused_computation.7 | convolution fusion | flops 412086272 | bytes 26509312 | tf_op jit(solution)/shard_map/qhd,khd->hqk/dot_general | solution.py:510
  258.8 6.4 %multiply_convert_fusion.1 = bf16[8,512,768]{2,1,0:T(8,128)(2,1)S(1)} fusion(f32[8,512,768]{2,1,0:T(8,128)} %get-tuple-element.237, f32[8,512,768]{2,1,0:T(8,128)S(1)} %get-tuple-element.227, f32[8,512]{1,0:T(8,128)S(1)} %get-tuple-element.236, f32[8,512]{1,0:T(8,128)S(1)} %log_add_fusion.1), kind=kLoop, calls=%fused_computation.6 | loop fusion | flops 12582912 | bytes 31490048 | tf_op jit(solution)/shard_map/convert_element_type | solution.py:519
  265.3 3.0 fusion.61
  268.3 2.3 multiply_bitcast_fusion
  270.7 2.6 multiply_convert_fusion
  273.4 3.0 fusion.60
  279.8 6.8 %reshape.560 = f32[4,2,2,32,2,1024]{5,4,3,2,1,0:T(2,128)} reshape(f32[512,2048]{1,0:T(8,128)} %fusion.104) | data formatting | bytes 8388608 | tf_op jit(solution)/shard_map/reshape | solution.py:362
  293.1 2.2 constant_dynamic-slice_fusion.3
  295.3 2.2 constant_dynamic-slice_fusion.2
  300.7 6.5 %copy.86 = bf16[2048,1024]{1,0:T(8,128)(2,1)} copy(bf16[2048,1024]{0,1:T(8,128)(2,1)} %fusion.7) | data formatting | bytes 8388608 | tf_op jit(solution)/shard_map/dot_general | solution.py:69
  307.2 4.7 %fusion.123 = f32[4,2,2,128,2,256]{5,3,4,2,1,0:T(8,128)S(1)} fusion(bf16[4,2,2,128,1024,1]{4,3,5,2,1,0:T(8,128)(2,1)} %bitcast.301, bf16[2,256,1024,1,1,1]{2,1,0,5,4,3:T(8,128)(2,1)S(1)} %bitcast.325), kind=kOutput, calls=%fused_computation.234 | convolution fusion | flops 2147483648 | bytes 9437184 | tf_op jit(solution)/shard_map/dot_general | solution.py:69
  320.6 3.2 fusion.120
  323.8 6.1 %maximum_maximum_fusion = bf16[1024,1536]{0,1:T(8,128)(2,1)S(1)} fusion(bf16[256,512]{0,1:T(8,128)(2,1)S(1)} %fusion.79, bf16[768,512]{0,1:T(8,128)(2,1)S(1)} %bitcast.317, bf16[1024,512]{0,1:T(8,128)(2,1)S(1)} %bitcast.311, bf16[1024,512]{0,1:T(8,128)(2,1)S(1)} %bitcast.309), kind=kLoop, calls=%fused_computation.65 | loop fusion | flops 12582912 | bytes 6291456 | tf_op jit(solution)/shard_map/concatenate | solution.py:546
  333.9 50.0 %shard_map.221 = (f32[32,768]{1,0:T(8,128)}, f32[32,256]{1,0:T(8,128)}, f32[32,1024]{1,0:T(8,128)}, f32[128,256]{1,0:T(8,128)}) custom-call(f32[4,2,2,32,768]{4,3,2,1,0:T(8,128)} %dynamic-slice_bitcast_fusion.1.refs_0_, f32[4,2,2,32,256]{4,3,2,1,0:T(8,128)} %dynamic-slice_bitcast_fusion.2.refs_1_, f32[4,2,2,32,1024]{4,3,2,1,0:T(8,128)} %bitcast.292, ...), custom_call_target="tpu_custom_call" | custom-call | tf_op jit(solution)/shard_map/pallas_call | solution.py:340
  384.0 2.3 copy.69
  388.5 12.2 %fusion.51 = (f32[512]{0:T(512)S(1)}, f32[512]{0:T(512)S(1)}, bf16[1,1024,512]{1,2,0:T(8,128)(2,1)}, bf16[1,1024,512]{1,2,0:T(8,128)(2,1)}) fusion(bf16[1,1024,512]{1,2,0:T(8,128)(2,1)} %copy-done.12, f32[1024,512]{0,1:T(8,128)} %get-tuple-element.228, f32[1024,512]{0,1:T(8,128)S(1)} %copy-done.11, f32[1024]{0:T(1024)S(1)} %negate_multiply_fusion.2, ...), kind=kOutput, calls=%fused_computation.87 | convolution fusion | flops 2168454144 | bytes 31485952 | tf_op jit(solution)/shard_map/dot_general | solution.py:472
  400.8 3.4 all-reduce.12
  404.6 2.3 copy.78
  406.9 2.3 copy.77
  409.2 40.9 %all-reduce.11 = (f32[256]{0:T(256)}, f32[256]{0:T(256)}, f32[256]{0:T(256)}, f32[256]{0:T(256)}, f32[256]{0:T(256)}, /*index=5*/f32[256]{0:T(256)}) all-reduce(f32[256]{0:T(256)S(1)} %dynamic-slice.35, f32[256]{0:T(256)S(1)} %dynamic-slice.37, f32[256]{0:T(256)S(1)} %dynamic-slice.39, ...), channel_id=1, replica_groups=mesh['rows'=16,'tm'=2] {'rows'}, use_global_device_ids=true, to_apply=%region_21.22 | all-reduce | flops 1536 | bytes 12288 | tf_op jit(solution)/shard_map/psum | solution.py:566
  (301 shorter events, 77.6 us)
Async XLA Ops:
  0.6 9.5 %copy-start.1 = (f32[128,256]{1,0:T(8,128)S(1)}, f32[128,256]{1,0:T(8,128)}, u32[]{:S(2)}) copy-start(f32[128,256]{1,0:T(8,128)} %refs_3_.1) | copy-start | bytes 393220
  0.7 9.5 %copy-start = (f32[32,1024]{1,0:T(8,128)S(1)}, f32[32,1024]{1,0:T(8,128)}, u32[]{:S(2)}) copy-start(f32[32,1024]{1,0:T(8,128)} %refs_2_.1) | copy-start | bytes 393220
  0.7 9.5 %copy-start.3 = (f32[32,256]{1,0:T(8,128)S(1)}, f32[32,256]{1,0:T(8,128)}, u32[]{:S(2)}) copy-start(f32[32,256]{1,0:T(8,128)} %refs_1_.1) | copy-start | bytes 98308
  0.7 9.5 %copy-start.2 = (f32[32,768]{1,0:T(8,128)S(1)}, f32[32,768]{1,0:T(8,128)}, u32[]{:S(2)}) copy-start(f32[32,768]{1,0:T(8,128)} %refs_0_.1) | copy-start | bytes 294916
  0.7 147.6 %collective-permute-start.1 = (s32[1024]{0:T(1024)}, s32[1024]{0:T(1024)S(1)}, u32[]{:S(2)}, u32[]{:S(2)}) collective-permute-start(s32[1024]{0:T(1024)} %bitcast.336), channel_id=1, source_target_pairs={{0,1},{2,3},{4,5},{6,7},{8,9},{10,11},{12,13},{14,15},{16,17},{18,... | collective-permute-start | bytes 12296 | tf_op jit(solution)/shard_map/ppermute | solution.py:37
  8.1 50.4 %copy-start.64 = (f32[2,1,256]{2,1,0:T(1,128)}, f32[2,1,256]{2,1,0:T(1,128)S(1)}, u32[]{:S(2)}) copy-start(f32[2,1,256]{2,1,0:T(1,128)S(1)} %convert_element_type.201) | copy-start | bytes 6148
  9.6 155.9 %copy-start.4 = (bf16[1,1024,512]{1,2,0:T(8,128)(2,1)}, bf16[1,1024,512]{1,2,0:T(8,128)(2,1)S(1)}, u32[]{:S(2)}) copy-start(bf16[1,1024,512]{1,2,0:T(8,128)(2,1)S(1)} %copy.62) | copy-start | bytes 3145732
  9.8 53.3 %copy-start.56 = (f32[1024]{0:T(1024)}, f32[1024]{0:T(1024)S(1)}, u32[]{:S(2)}) copy-start(f32[1024]{0:T(1024)S(1)} %broadcast_multiply_fusion.1) | copy-start | bytes 12292
  10.1 52.9 %copy-start.66 = (f32[1024]{0:T(1024)}, f32[1024]{0:T(1024)S(1)}, u32[]{:S(2)}) copy-start(f32[1024]{0:T(1024)S(1)} %fusion.48) | copy-start | bytes 12292
  10.2 52.9 %copy-start.62 = (f32[1024]{0:T(1024)}, f32[1024]{0:T(1024)S(1)}, u32[]{:S(2)}) copy-start(f32[1024]{0:T(1024)S(1)} %fusion.87) | copy-start | bytes 12292
  58.5 10.7 %copy-start.55 = (s32[1,1024]{1,0:T(1,128)S(1)}, s32[1,1024]{1,0:T(1,128)}, u32[]{:S(2)}) copy-start(s32[1,1024]{1,0:T(1,128)} %param.25) | copy-start | bytes 12292
  58.5 12.6 %copy-start.75 = (u32[32]{0:T(128)S(1)}, u32[32]{0:T(128)}, u32[]{:S(2)}) copy-start(u32[32]{0:T(128)} %constant.255) | copy-start | bytes 388
  65.8 82.8 %collective-permute-start = (bf16[1024,512]{1,0:T(8,128)(2,1)}, bf16[1024,512]{1,0:T(8,128)(2,1)}, u32[]{:S(2)}, u32[]{:S(2)}) collective-permute-start(bf16[1024,512]{1,0:T(8,128)(2,1)} %slice.365), channel_id=1, source_target_pairs={{0,1},{2,3},{4,5},{6,7},{8,9},{10,11},{12,13},{14,15},{16,17},{18,... | collective-permute-start | bytes 3145736 | tf_op jit(solution)/shard_map/ppermute | solution.py:37
  88.6 15.1 %copy-start.77 = (f32[256]{0:T(256)S(1)}, f32[256]{0:T(256)}, u32[]{:S(2)}) copy-start(f32[256]{0:T(256)} %param.35) | copy-start | bytes 3076
  92.3 13.5 %copy-start.22 = (bf16[1024,8,32]{0,2,1:T(8,128)(2,1)}, bf16[1024,8,32]{0,2,1:T(8,128)(2,1)S(1)}, u32[]{:S(2)}) copy-start(bf16[1024,8,32]{0,2,1:T(8,128)(2,1)S(1)} %get-tuple-element.194) | copy-start | bytes 1572868
  92.3 13.6 %copy-start.24 = (bf16[1024,8,32]{0,2,1:T(8,128)(2,1)}, bf16[1024,8,32]{0,2,1:T(8,128)(2,1)S(1)}, u32[]{:S(2)}) copy-start(bf16[1024,8,32]{0,2,1:T(8,128)(2,1)S(1)} %get-tuple-element.195) | copy-start | bytes 1572868
  92.3 61.7 %copy-start.15 = (bf16[1024,8,32]{0,2,1:T(8,128)(2,1)}, bf16[1024,8,32]{0,2,1:T(8,128)(2,1)S(1)}, u32[]{:S(2)}) copy-start(bf16[1024,8,32]{0,2,1:T(8,128)(2,1)S(1)} %get-tuple-element.211) | copy-start | bytes 1572868
  93.5 58.4 %collective-permute-start.2 = (bf16[1024,512]{0,1:T(8,128)(2,1)}, bf16[1024,512]{0,1:T(8,128)(2,1)}, u32[]{:S(2)}, u32[]{:S(2)}) collective-permute-start(bf16[1024,512]{0,1:T(8,128)(2,1)} %bitcast.23), channel_id=1, source_target_pairs={{0,1},{2,3},{4,5},{6,7},{8,9},{10,11},{12,13},{14,15},{16,17},{18,... | collective-permute-start | bytes 3145736 | tf_op jit(solution)/shard_map/ppermute | solution.py:37
  105.9 9.2 %copy-start.69 = (f32[2,1,256]{2,1,0:T(1,128)}, f32[2,1,256]{2,1,0:T(1,128)S(1)}, u32[]{:S(2)}) copy-start(f32[2,1,256]{2,1,0:T(1,128)S(1)} %convert_element_type.203) | copy-start | bytes 6148
  107.9 15.5 %copy-start.12 = (bf16[1,1024,512]{1,2,0:T(8,128)(2,1)}, bf16[1,1024,512]{1,2,0:T(8,128)(2,1)S(1)}, u32[]{:S(2)}) copy-start(bf16[1,1024,512]{1,2,0:T(8,128)(2,1)S(1)} %copy.68) | copy-start | bytes 3145732
  123.5 7.0 %copy-start.33 = (bf16[768,512]{0,1:T(8,128)(2,1)S(1)}, bf16[768,512]{0,1:T(8,128)(2,1)}, u32[]{:S(2)}) copy-start(bf16[768,512]{0,1:T(8,128)(2,1)} %copy.66) | copy-start | bytes 2359300
  130.4 8.0 %copy-start.41 = (bf16[2,4,2,2,128,256]{5,4,3,2,1,0:T(8,128)(2,1)S(1)}, bf16[2,4,2,2,128,256]{5,4,3,2,1,0:T(8,128)(2,1)}, u32[]{:S(2)}) copy-start(bf16[2,4,2,2,128,256]{5,4,3,2,1,0:T(8,128)(2,1)} %get-tuple-element.107) | copy-start | bytes 6291460
  137.5 10.8 %copy-start.73 = (s32[1,512]{1,0:T(1,128)S(1)}, s32[1,512]{1,0:T(1,128)}, u32[]{:S(2)}) copy-start(s32[1,512]{1,0:T(1,128)} %get-tuple-element.216) | copy-start | bytes 6148
  137.6 10.8 %copy-start.74 = (pred[768]{0:T(1024)(128)(4,1)S(1)}, pred[768]{0:T(1024)(128)(4,1)}, u32[]{:S(2)}) copy-start(pred[768]{0:T(1024)(128)(4,1)} %get-tuple-element.218) | copy-start | bytes 2308
  167.8 44.5 %copy-start.6 = (f32[1024,512]{0,1:T(8,128)}, f32[1024,512]{0,1:T(8,128)S(1)}, u32[]{:S(2)}) copy-start(f32[1024,512]{0,1:T(8,128)S(1)} %get-tuple-element.184) | copy-start | bytes 6291460
  168.1 21.8 %copy-start.28 = (bf16[1,4,2,2,128,256]{5,4,3,2,1,0:T(8,128)(2,1)S(1)}, bf16[1,4,2,2,128,256]{5,4,3,2,1,0:T(8,128)(2,1)}, u32[]{:S(2)}) copy-start(bf16[1,4,2,2,128,256]{5,4,3,2,1,0:T(8,128)(2,1)} %get-tuple-element.199) | copy-start | bytes 3145732
  189.9 12.1 %copy-start.8 = (f32[1024,2048]{1,0:T(8,128)}, f32[1024,2048]{1,0:T(8,128)S(1)}, u32[]{:S(2)}) copy-start(f32[1024,2048]{1,0:T(8,128)S(1)} %get-tuple-element.230) | copy-start | bytes 25165828
  224.7 20.4 %copy-start.34 = (bf16[768,512]{0,1:T(8,128)(2,1)S(1)}, bf16[768,512]{0,1:T(8,128)(2,1)}, u32[]{:S(2)}) copy-start(bf16[768,512]{0,1:T(8,128)(2,1)} %copy.66) | copy-start | bytes 2359300
  258.8 6.4 %copy-start.20 = (bf16[768,512]{0,1:T(8,128)(2,1)S(1)}, bf16[768,512]{0,1:T(8,128)(2,1)}, u32[]{:S(2)}) copy-start(bf16[768,512]{0,1:T(8,128)(2,1)} %copy-done.19) | copy-start | bytes 2359300
  258.8 9.4 %copy-start.16 = (bf16[1024,8,32]{0,2,1:T(8,128)(2,1)S(1)}, bf16[1024,8,32]{0,2,1:T(8,128)(2,1)}, u32[]{:S(2)}) copy-start(bf16[1024,8,32]{0,2,1:T(8,128)(2,1)} %copy-done.15) | copy-start | bytes 1572868
  258.8 9.4 %copy-start.17 = (bf16[1024,8,32]{0,2,1:T(8,128)(2,1)S(1)}, bf16[1024,8,32]{0,2,1:T(8,128)(2,1)}, u32[]{:S(2)}) copy-start(bf16[1024,8,32]{0,2,1:T(8,128)(2,1)} %get-tuple-element.212) | copy-start | bytes 1572868
  279.8 8.1 %copy-start.53 = (bf16[256,8,64]{0,2,1:T(8,128)(2,1)S(1)}, bf16[256,8,64]{0,2,1:T(8,128)(2,1)}, u32[]{:S(2)}) copy-start(bf16[256,8,64]{0,2,1:T(8,128)(2,1)} %slice.393) | copy-start | bytes 786436
  279.8 9.5 %copy-start.30 = (bf16[1024,8,64]{0,2,1:T(8,128)(2,1)S(1)}, bf16[1024,8,64]{0,2,1:T(8,128)(2,1)}, u32[]{:S(2)}) copy-start(bf16[1024,8,64]{0,2,1:T(8,128)(2,1)} %copy-done.29) | copy-start | bytes 3145732
  286.6 6.5 %copy-start.14 = (f32[4,2,2,32,2,1024]{5,4,3,2,1,0:T(2,128)S(1)}, f32[4,2,2,32,2,1024]{5,4,3,2,1,0:T(2,128)}, u32[]{:S(2)}) copy-start(f32[4,2,2,32,2,1024]{5,4,3,2,1,0:T(2,128)} %reshape.560) | copy-start | bytes 12582916
  287.8 31.2 %collective-permute-start.4 = (bf16[256,512]{0,1:T(8,128)(2,1)S(1)}, bf16[256,512]{0,1:T(8,128)(2,1)}, u32[]{:S(2)}, u32[]{:S(2)}) collective-permute-start(bf16[256,512]{0,1:T(8,128)(2,1)S(1)} %bitcast.334), channel_id=1, source_target_pairs={{1,0},{3,2},{5,4},{7,6},{9,8},{11,10},{13,12},{15,14},{17,16},{19,... | collective-permute-start | bytes 786440 | tf_op jit(solution)/shard_map/ppermute | solution.py:37
  300.7 6.5 %copy-start.45 = (bf16[1024,512]{0,1:T(8,128)(2,1)S(1)}, bf16[1024,512]{0,1:T(8,128)(2,1)}, u32[]{:S(2)}) copy-start(bf16[1024,512]{0,1:T(8,128)(2,1)} %fusion.50) | copy-start | bytes 3145732
  307.2 6.0 %copy-start.54 = (bf16[256,8,64]{0,2,1:T(8,128)(2,1)S(1)}, bf16[256,8,64]{0,2,1:T(8,128)(2,1)}, u32[]{:S(2)}) copy-start(bf16[256,8,64]{0,2,1:T(8,128)(2,1)} %slice.457) | copy-start | bytes 786436
  311.9 6.0 %copy-start.21 = (f32[768,8,64]{0,2,1:T(8,128)S(1)}, f32[768,8,64]{0,2,1:T(8,128)}, u32[]{:S(2)}) copy-start(f32[768,8,64]{0,2,1:T(8,128)} %slice.386) | copy-start | bytes 4718596
  311.9 6.0 %copy-start.31 = (f32[512,8,64]{0,2,1:T(8,128)S(1)}, f32[512,8,64]{0,2,1:T(8,128)}, u32[]{:S(2)}) copy-start(f32[512,8,64]{0,2,1:T(8,128)} %fusion.61) | copy-start | bytes 3145732
  311.9 6.0 %copy-start.32 = (f32[512,8,64]{0,2,1:T(8,128)S(1)}, f32[512,8,64]{0,2,1:T(8,128)}, u32[]{:S(2)}) copy-start(f32[512,8,64]{0,2,1:T(8,128)} %fusion.60) | copy-start | bytes 3145732
  311.9 6.0 %copy-start.43 = (f32[1024,32]{0,1:T(8,128)S(1)}, f32[1024,32]{0,1:T(8,128)}, u32[]{:S(2)}) copy-start(f32[1024,32]{0,1:T(8,128)} %copy-done.42) | copy-start | bytes 393220
  312.0 6.0 %copy-start.51 = (f32[1024,32]{0,1:T(8,128)S(1)}, f32[1024,32]{0,1:T(8,128)}, u32[]{:S(2)}) copy-start(f32[1024,32]{0,1:T(8,128)} %get-tuple-element.213) | copy-start | bytes 393220
  313.2 4.7 %collective-permute-start.3 = (bf16[256,512]{0,1:T(8,128)(2,1)S(1)}, bf16[256,512]{0,1:T(8,128)(2,1)S(1)}, u32[]{:S(2)}, u32[]{:S(2)}) collective-permute-start(bf16[256,512]{0,1:T(8,128)(2,1)S(1)} %bitcast.335), channel_id=1, source_target_pairs={{1,0},{3,2},{5,4},{7,6},{9,8},{11,10},{13,12},{15,14},{17,16},{19,... | collective-permute-start | bytes 786440 | tf_op jit(solution)/shard_map/ppermute | solution.py:37
  323.8 6.1 %copy-start.27 = (bf16[1024,512]{0,1:T(8,128)(2,1)S(1)}, bf16[1024,512]{0,1:T(8,128)(2,1)}, u32[]{:S(2)}) copy-start(bf16[1024,512]{0,1:T(8,128)(2,1)} %copy-done.26) | copy-start | bytes 3145732
  400.7 49.4 %copy-start.61 = (f32[32,768]{1,0:T(8,128)S(1)}, f32[32,768]{1,0:T(8,128)}, u32[]{:S(2)}) copy-start(f32[32,768]{1,0:T(8,128)} %get-tuple-element.333) | copy-start | bytes 294916
  400.7 50.0 %copy-start.68 = (f32[32,256]{1,0:T(8,128)S(1)}, f32[32,256]{1,0:T(8,128)}, u32[]{:S(2)}) copy-start(f32[32,256]{1,0:T(8,128)} %get-tuple-element.334) | copy-start | bytes 98308
  400.7 50.6 %copy-start.60 = (f32[32,1024]{1,0:T(8,128)S(1)}, f32[32,1024]{1,0:T(8,128)}, u32[]{:S(2)}) copy-start(f32[32,1024]{1,0:T(8,128)} %get-tuple-element.335) | copy-start | bytes 393220
  400.7 51.3 %copy-start.59 = (f32[128,256]{1,0:T(8,128)S(1)}, f32[128,256]{1,0:T(8,128)}, u32[]{:S(2)}) copy-start(f32[128,256]{1,0:T(8,128)} %get-tuple-element.336) | copy-start | bytes 393220
  (45 other events, 135.1 us)

commit v2 on v0

--- a/solution.py
+++ b/solution.py
@@ -1,8 +1,11 @@
+import functools
 import math
 
 import jax
 import jax.numpy as jnp
 from jax import lax
+from jax.experimental import pallas as pl
+from jax.experimental.pallas import tpu as pltpu
 from jax.sharding import PartitionSpec as P
 
 H = 8
@@ -328,6 +331,774 @@
     )
 
 
+MESH_IDS = pl.DeviceIdType.MESH
+F32 = jnp.float32
+BF16 = jnp.bfloat16
+
+
+def dot(left, right, contract=((1,), (0,))):
+    return lax.dot_general(left, right, (contract, ((), ())), preferred_element_type=F32)
+
+
+def dot_t(left, right):
+    return dot(left, right, ((1,), (1,)))
+
+
+def start_of(index, size):
+    return pl.ds(pl.multiple_of(index * size, size), size)
+
+
+def coordinates():
+    row, core = lax.axis_index("rows"), lax.axis_index("tm")
+    return row, core, lax.rem(row, 2), lax.rem(lax.div(row, 2), 2), lax.div(row, 4)
+
+
+def peers_of(at):
+    row, core, x, y, z = at
+    found = {
+        "x": (row + 1 - 2 * x, core),
+        "y": (row + 2 - 4 * y, core),
+        "s": (row, 1 - core),
+    }
+    for k in (1, 2, 3):
+        found[k] = (lax.rem(z + k, 4) * 4 + lax.rem(row, 4), core)
+    return found
+
+
+def enter(peers):
+    barrier = pltpu.get_barrier_semaphore()
+    for peer in peers.values():
+        pl.semaphore_signal(barrier, inc=1, device_id=peer, device_id_type=MESH_IDS)
+    pl.semaphore_wait(barrier, len(peers))
+
+
+class Links:
+    def __init__(self, sems, peers):
+        self.send, self.recv = sems
+        self.peers = peers
+        self.used = 0
+        self.started = []
+
+    def copy(self, src, dst, peer):
+        slot = self.used
+        self.used += 1
+        made = pltpu.make_async_remote_copy(
+            src_ref=src,
+            dst_ref=dst,
+            send_sem=self.send.at[slot],
+            recv_sem=self.recv.at[slot],
+            device_id=self.peers[peer],
+            device_id_type=MESH_IDS,
+        )
+        self.started.append(made)
+        return made
+
+    def drain(self, skip=()):
+        for made in self.started:
+            if not any(made is s for s in skip):
+                made.wait_send()
+
+
+def gather_copies(full, links, at):
+    row, core, x, y, z = at
+    half = full.shape[4] // 2
+    low, high = pl.ds(0, half), pl.ds(half, half)
+    every = slice(None)
+    table = [
+        ("a1", (core, z, y, x), 1),
+        ("a2", (core, z, y, x), 2),
+        ("a3", (core, z, y, x), 3),
+        ("b1", (core, every, y, x, low), "x"),
+        ("b2", (core, every, y, x, high), "y"),
+        ("c1", (core, every, y, every, low), "y"),
+        ("c2", (core, every, every, x, high), "x"),
+        ("da", (core, every, y, x), "s"),
+        ("db1", (core, every, y, 1 - x, low), "s"),
+        ("db2", (core, every, 1 - y, x, high), "s"),
+        ("dc1", (core, every, 1 - y, every, low), "s"),
+        ("dc2", (core, every, every, 1 - x, high), "s"),
+    ]
+    return {
+        name: links.copy(full.at[where], full.at[where], peer) for name, where, peer in table
+    }
+
+
+GATHER_STEPS = (
+    ((), ("a1", "a2", "a3")),
+    (("a1", "a2", "a3"), ("b1", "b2", "da")),
+    (("b1", "b2"), ("c1", "c2", "db1", "db2")),
+    (("c1", "c2"), ("dc1", "dc2")),
+    (("da", "db1", "db2", "dc1", "dc2"), ()),
+)
+
+
+def gather_step(copies, step):
+    waits, starts = GATHER_STEPS[step]
+    for name in waits:
+        copies[name].wait_recv()
+    for name in starts:
+        copies[name].start()
+
+
+def scatter_buffers(rows, columns):
+    half = rows // 2
+    return [
+        ((4, 2, 2, rows, columns), BF16),
+        ((4, 2, 2, rows, columns), BF16),
+        ((2, 4, 2, half, columns), BF16),
+        ((2, 4, half, columns), BF16),
+        ((3, rows, columns), BF16),
+    ]
+
+
+class Scatter:
+    def __init__(self, own, bufs, result, rows, links, at):
+        self.own, self.result, self.rows, self.at = own, result, rows, at
+        self.out, self.s_in, self.c_in, self.b_in, self.a_in = bufs
+        row, core, x, y, z = at
+        half = rows // 2
+        self.half = half
+        self.low, self.high = pl.ds(0, half), pl.ds(half, half)
+        every = slice(None)
+        low, high, out = self.low, self.high, self.out
+        self.d = links.copy(out, self.s_in, "s")
+        self.c1 = links.copy(out.at[every, 1 - y, every, low], self.c_in.at[0], "y")
+        self.c2 = links.copy(out.at[every, every, 1 - x, high], self.c_in.at[1], "x")
+        self.b1 = links.copy(out.at[every, y, 1 - x, low], self.b_in.at[0], "x")
+        self.b2 = links.copy(out.at[every, 1 - y, x, high], self.b_in.at[1], "y")
+        self.a = [
+            links.copy(out.at[lax.rem(z + k, 4), y, x], self.a_in.at[k - 1], k) for k in (1, 2, 3)
+        ]
+
+    def mine(self, k, y, x, part):
+        begin = ((k * 2 + y) * 2 + x) * self.rows + part * self.half
+        return self.own[pl.ds(pl.multiple_of(begin, self.half), self.half), :] + self.s_in[
+            k, y, x, pl.ds(part * self.half, self.half)
+        ].astype(F32)
+
+    def step(self, number):
+        row, core, x, y, z = self.at
+        low, high, out = self.low, self.high, self.out
+        c_in, b_in = self.c_in, self.b_in
+        if number == 0:
+            self.d.start()
+        if number == 1:
+            self.d.wait()
+            for k in range(4):
+                for i in range(2):
+                    out[k, 1 - y, i, low] = self.mine(k, 1 - y, i, 0).astype(BF16)
+            self.c1.start()
+            for k in range(4):
+                for i in range(2):
+                    out[k, i, 1 - x, high] = self.mine(k, i, 1 - x, 1).astype(BF16)
+            self.c2.start()
+        if number == 2:
+            self.c1.wait_recv()
+            for k in range(4):
+                out[k, y, 1 - x, low] = (
+                    self.mine(k, y, 1 - x, 0) + c_in[0, k, 1 - x].astype(F32)
+                ).astype(BF16)
+            self.b1.start()
+            self.c2.wait_recv()
+            for k in range(4):
+                out[k, 1 - y, x, high] = (
+                    self.mine(k, 1 - y, x, 1) + c_in[1, k, 1 - y].astype(F32)
+                ).astype(BF16)
+            self.b2.start()
+        if number == 3:
+            self.b1.wait_recv()
+            self.b2.wait_recv()
+            for k in (1, 2, 3):
+                there = lax.rem(z + k, 4)
+                out[there, y, x, low] = self.column(there, 0).astype(BF16)
+                out[there, y, x, high] = self.column(there, 1).astype(BF16)
+                self.a[k - 1].start()
+            self.result[low, :] = self.column(z, 0)
+            self.result[high, :] = self.column(z, 1)
+        if number == 4:
+            for k in range(3):
+                self.a[k].wait_recv()
+            self.result[...] = self.result[...] + (
+                self.a_in[0].astype(F32) + self.a_in[1].astype(F32) + self.a_in[2].astype(F32)
+            )
+
+    def column(self, k, part):
+        row, core, x, y, z = self.at
+        place = x if part == 0 else y
+        return (
+            self.mine(k, y, x, part)
+            + self.c_in[part, k, place].astype(F32)
+            + self.b_in[part, k].astype(F32)
+        )
+
+
+def normal_tail(values):
+    t = 1.0 / (1.0 + TAIL_P * jnp.abs(values))
+    e = jnp.exp(-0.5 * (values * values))
+    series = jnp.full_like(values, TAIL[-1])
+    for term in TAIL[-2::-1]:
+        series = series * t + term
+    return series * t * e, e
+
+
+TAIL_P = 0.4 / math.sqrt(2.0)
+TAIL = (
+    0.11283793097319604,
+    0.11283480301555754,
+    0.10392122984713166,
+    0.08427214046581868,
+    0.0707105879765068,
+    -0.002791732410193116,
+    0.08452735931959071,
+    -0.09144066126533841,
+    0.025128404380787478,
+)
+
+
+def lane_pattern(shape, size):
+    return lax.rem(lax.broadcasted_iota(jnp.int32, shape, len(shape) - 1), size)
+
+
+def turned(values, cosine, sine):
+    first = lane_pattern(values.shape, HD) < HD // 2
+    swapped = jnp.where(first, pltpu.roll(values, 96, 1), pltpu.roll(values, 32, 1))
+    return values * cosine + swapped * sine
+
+
+TILE = 256
+BLOCK = 128
+SPAN = BLOCK + REACH
+PAIRS = H // 2
+
+NAMES = [
+    "y", "ig", "gq", "go", "gu", "gd", "gv",
+]
+
+
+def scratch_list(frames, width, hidden):
+    blocks = frames // BLOCK
+    ext = REACH + frames
+    items = [
+        ("wq", (2, 4, 2, 2, width // 16, 3 * width // 2), BF16),
+        ("wo", (2, 4, 2, 2, width // 16, width // 2), BF16),
+        ("wu", (2, 4, 2, 2, width // 16, hidden // 2), BF16),
+        ("wd", (2, 4, 2, 2, hidden // 16, width // 2), BF16),
+        ("vecs", (2, 8, width // 2), F32),
+        ("segs", (2, 8, frames), F32),
+        ("n1t", (width, frames), BF16),
+        ("cos", (frames, 128), F32),
+        ("sin", (frames, 128), F32),
+        ("bias", (blocks, SPAN, BLOCK), BF16),
+        ("qm", (PAIRS, 2 * frames, 128), BF16),
+        ("kx", (PAIRS, ext, 128), BF16),
+        ("vx", (PAIRS, ext, 128), BF16),
+        ("kt", (PAIRS, 128, ext), BF16),
+        ("vt", (PAIRS, 128, ext), BF16),
+        ("probs", (PAIRS, blocks, SPAN, 2 * BLOCK), BF16),
+        ("ot", (width, frames), BF16),
+        ("n2t", (width, frames), BF16),
+        ("act", (frames, hidden), BF16),
+        ("du", (2, frames, hidden // 2), BF16),
+        ("own_u", (width, hidden // 2), F32),
+        ("own_d", (hidden * 2, 128), F32),
+        ("own_o", (width, width // 2), F32),
+        ("own_q", (width, 3 * width // 2), F32),
+        ("dbmt", (width, frames), BF16),
+        ("dba", (2, frames, width // 2), BF16),
+        ("dom", (PAIRS, 2 * frames, 128), BF16),
+        ("dx1", (frames, width), F32),
+        ("dkx", (ext, 128), F32),
+        ("dvx", (ext, 128), F32),
+        ("h_out", (PAIRS, 2, REACH, 128), BF16),
+        ("h_in", (PAIRS, 2, REACH, 128), BF16),
+        ("acc", (8, width), F32),
+        ("v_out", (3, 8, width // 2), F32),
+        ("v_in", (3, 8, width // 2), F32),
+        ("v_z", (4, 8, width // 2), F32),
+        ("down_t", (width // 2, hidden // 16), F32),
+    ]
+    for name, rows, columns in (
+        ("q", width // 16, 3 * width // 2),
+        ("o", width // 16, width // 2),
+        ("u", width // 16, hidden // 2),
+        ("d", width // 2, hidden // 16),
+    ):
+        for i, (shape, kind) in enumerate(scatter_buffers(rows, columns)):
+            if i > 0 or name in "qd":
+                items.append(("s_%s%d" % (name, i), shape, kind))
+    return items
+
+
+SLOTS = 120
+
+
+def layer_kernel(names, *refs):
+    x_ref, dy_ref, seg_ref = refs[:3]
+    shards, vectors = refs[3:7], refs[7:13]
+    y_ref, ig_ref, gq, go, gu, gd, gv = refs[13:20]
+    m = dict(zip(names, refs[20:-2]))
+    at = coordinates()
+    row, core, x, y, z = at
+    peers = peers_of(at)
+    links = Links(refs[-2:], peers)
+    frames, width = x_ref.shape[1:]
+    hidden = m["act"].shape[1]
+    blocks, tiles = frames // BLOCK, frames // TILE
+    factor = 1.0 / math.sqrt(HD)
+    wq, wo, wu, wd = m["wq"], m["wo"], m["wu"], m["wd"]
+    other = 1 - core
+
+    for shard, full in zip(shards, (wq, wo, wu, wd)):
+        full[core, z, y, x] = shard[...].astype(BF16)
+    m["vecs"][core] = jnp.concatenate(
+        [v[...].astype(BF16).astype(F32) for v in vectors]
+        + [jnp.zeros((2, width // 2), F32)],
+        axis=0,
+    )
+    m["segs"][core] = jnp.broadcast_to(seg_ref[...].astype(F32), (8, frames))
+    enter(peers)
+    vec_copy = links.copy(m["vecs"].at[core], m["vecs"].at[core], "s")
+    seg_copy = links.copy(m["segs"].at[core], m["segs"].at[core], "s")
+    gathers = [gather_copies(full, links, at) for full in (wq, wo, wu, wd)]
+    vec_copy.start()
+    seg_copy.start()
+    for each in gathers:
+        gather_step(each, 0)
+
+    def vector(i):
+        return jnp.concatenate([m["vecs"][0, i : i + 1, :], m["vecs"][1, i : i + 1, :]], axis=1)
+
+    def normalized(values):
+        average = jnp.mean(values, axis=-1, keepdims=True)
+        centred = values - average
+        variance = jnp.mean(centred * centred, axis=-1, keepdims=True)
+        scale = lax.rsqrt(variance + EPSILON)
+        return centred * scale, scale
+
+    vec_copy.wait_recv()
+    n1 = y_ref
+    gain_one, bias_one = vector(0), vector(1)
+
+    def norm_one(t, _):
+        rows = start_of(t, TILE)
+        unit, _scale = normalized(x_ref[0, rows, :].astype(F32))
+        low = (unit * gain_one + bias_one).astype(BF16)
+        n1[0, rows, :] = low
+        m["n1t"][:, rows] = low.T
+        return 0
+
+    lax.fori_loop(0, tiles, norm_one, 0)
+    gather_step(gathers[0], 1)
+
+    seg_copy.wait_recv()
+    segs = m["segs"]
+    segc = m["own_d"]
+
+    def spread(which, begin):
+        line = segs[which, 0:1, pl.ds(pl.multiple_of(begin, BLOCK), BLOCK)]
+        return jnp.broadcast_to(line, (BLOCK, BLOCK)).T
+
+    for e in range(REACH // BLOCK):
+        halo = spread(other, frames - REACH + e * BLOCK)
+        segc[e * BLOCK : (e + 1) * BLOCK, :] = jnp.where(core > 0, halo, -1.0)
+
+    lanes = lane_pattern((1, 128), HD // 2).astype(F32)
+    frequency = jnp.exp(lanes * (-2.0 * math.log(10000.0) / HD))
+    first_half = lane_pattern((BLOCK, 128), HD) < HD // 2
+
+    def tables(b, _):
+        rows = start_of(b, BLOCK)
+        here = spread(core, b * BLOCK)
+        segc[pl.ds(pl.multiple_of(REACH + b * BLOCK, BLOCK), BLOCK), :] = here
+        count = jnp.zeros((BLOCK, BLOCK), F32)
+        for which in range(2):
+            for k in range(blocks):
+                line = segs[which, 0:1, k * BLOCK : (k + 1) * BLOCK]
+                count = count + jnp.where(line < here, 1.0, 0.0)
+        began = jnp.sum(count, axis=1, keepdims=True)
+        frame = lax.broadcasted_iota(jnp.int32, (BLOCK, 1), 0) + (core * frames + b * BLOCK)
+        angle = (frame.astype(F32) - began) * frequency
+        m["cos"][rows, :] = jnp.cos(angle)
+        sine = jnp.sin(angle)
+        m["sin"][rows, :] = jnp.where(first_half, -sine, sine)
+        return 0
+
+    lax.fori_loop(0, blocks, tables, 0)
+    gather_step(gathers[0], 2)
+
+    distance = (
+        lax.broadcasted_iota(jnp.int32, (SPAN, BLOCK), 1)
+        - lax.broadcasted_iota(jnp.int32, (SPAN, BLOCK), 0)
+        + REACH
+    )
+    near = (distance >= 0) & (distance < WINDOW)
+
+    def masks(b, _):
+        keys = segc[pl.ds(pl.multiple_of(b * BLOCK, BLOCK), SPAN), :]
+        line = segs[core, 0:1, start_of(b, BLOCK)]
+        m["bias"][b] = jnp.where(near & (keys == line), 0.0, NEGATIVE).astype(BF16)
+        return 0
+
+    lax.fori_loop(0, blocks, masks, 0)
+    gather_step(gathers[0], 3)
+    gather_step(gathers[0], 4)
+    for each in gathers[1:]:
+        gather_step(each, 1)
+
+    low_lanes = lane_pattern((1, 128), 128) < HD
+
+    def two_heads(ref, p, b, value):
+        zero = jnp.zeros_like(value)
+        ref[p, pl.ds(pl.multiple_of(b * 2 * BLOCK, BLOCK), BLOCK), :] = jnp.where(
+            low_lanes, value, zero
+        )
+        ref[p, pl.ds(pl.multiple_of((b * 2 + 1) * BLOCK, BLOCK), BLOCK), :] = jnp.where(
+            low_lanes, zero, value
+        )
+
+    def project(t, _):
+        rows = start_of(t, TILE)
+        placed = pl.ds(pl.multiple_of(REACH + t * TILE, TILE), TILE)
+        left = n1[0, rows, :]
+        cosine, sine = m["cos"][rows, :], m["sin"][rows, :]
+        for half in range(2):
+            wide = dot(left, wq[half].reshape(width, -1))
+            for j in range(6):
+                chunk = wide[:, j * 128 : (j + 1) * 128]
+                kind, p = divmod(half * 6 + j, PAIRS)
+                if kind == 0:
+                    value = (turned(chunk, cosine, sine).astype(BF16) * factor).astype(BF16)
+                    for i in range(TILE // BLOCK):
+                        two_heads(
+                            m["qm"], p, t * (TILE // BLOCK) + i, value[i * BLOCK : (i + 1) * BLOCK]
+                        )
+                elif kind == 1:
+                    value = turned(chunk, cosine, sine).astype(BF16)
+                    m["kx"][p, placed, :] = value
+                    m["kt"][p, :, placed] = value.T
+                else:
+                    value = chunk.astype(BF16)
+                    m["vx"][p, placed, :] = value
+                    m["vt"][p, :, placed] = value.T
+        return 0
+
+    lax.fori_loop(0, tiles, project, 0)
+    tail, head = pl.ds(frames, REACH), pl.ds(0, REACH)
+    halo_copies = [
+        links.copy(m[r].at[:, tail], m[r].at[:, head], "s") for r in ("kx", "vx")
+    ]
+    for each in halo_copies:
+        each.start()
+    for each in gathers[1:]:
+        gather_step(each, 2)
+    for each in halo_copies:
+        each.wait_recv()
+    for p in range(PAIRS):
+        m["kt"][p, :, 0:REACH] = m["kx"][p, 0:REACH, :].T
+        m["vt"][p, :, 0:REACH] = m["vx"][p, 0:REACH, :].T
+
+    mixed = ig_ref
+
+    def heads_joined(both):
+        return jnp.concatenate([both[:HD, :BLOCK], both[HD:, BLOCK:]], axis=0)
+
+    def attend(b, _):
+        rows = start_of(b, BLOCK)
+        window = pl.ds(pl.multiple_of(b * BLOCK, BLOCK), SPAN)
+        mask = m["bias"][b].astype(F32)
+        mask = jnp.concatenate([mask, mask], axis=1)
+        for p in range(PAIRS):
+            scores = dot_t(m["kx"][p, window, :], m["qm"][p, start_of(b, 2 * BLOCK), :]) + mask
+            top = jnp.max(scores, axis=0, keepdims=True)
+            weights = jnp.exp(scores - top)
+            total = jnp.sum(weights, axis=0, keepdims=True)
+            probs = (weights * (1.0 / total)).astype(BF16)
+            m["probs"][p, b] = probs
+            joined = heads_joined(dot(m["vt"][p, :, window], probs))
+            m["ot"][p * 128 : (p + 1) * 128, rows] = joined.astype(BF16)
+            mixed[0, rows, p * 128 : (p + 1) * 128] = joined.T.astype(BF16)
+        return 0
+
+    lax.fori_loop(0, blocks, attend, 0)
+    for each in gathers[1:]:
+        gather_step(each, 3)
+    for each in gathers[1:]:
+        gather_step(each, 4)
+
+    m["acc"][...] = jnp.zeros_like(m["acc"])
+    acc = m["acc"]
+
+    def add_to(i, values):
+        acc[i : i + 1, :] = acc[i : i + 1, :] + jnp.sum(values, axis=0, keepdims=True)
+
+    scale_one, gain_two, bias_two, scale_two = vector(2), vector(3), vector(4), vector(5)
+    slope = m["own_u"]
+    part = hidden // 4
+
+    def norm_back(unit, scale, gain, grad):
+        inner = grad * gain
+        return scale * (
+            inner
+            - jnp.mean(inner, axis=-1, keepdims=True)
+            - unit * jnp.mean(inner * unit, axis=-1, keepdims=True)
+        )
+
+    def middle(t, _):
+        rows = start_of(t, TILE)
+        both = mixed[0, rows, :]
+        branch = jnp.concatenate(
+            [dot(both, wo[h].reshape(width, -1)) for h in range(2)], axis=1
+        )
+        after = x_ref[0, rows, :].astype(F32) + scale_one * branch
+        unit, scale = normalized(after)
+        n2 = (unit * gain_two + bias_two).astype(BF16)
+        m["n2t"][:, rows] = n2.T
+        for n in range(4):
+            half, columns = n // 2, pl.ds((n % 2) * part, part)
+            up = dot(n2, wu[half, :, :, :, :, columns].reshape(width, part))
+            tail_value, bell = normal_tail(up)
+            cdf = jnp.where(up >= 0.0, 1.0 - tail_value, tail_value)
+            m["act"][rows, n * part : (n + 1) * part] = (up * cdf).astype(BF16)
+            slope[half * TILE : (half + 1) * TILE, columns] = cdf + up * (
+                bell * (1.0 / math.sqrt(2.0 * math.pi))
+            )
+        act = m["act"][rows, :]
+        branch_two = jnp.concatenate(
+            [dot(act, wd[h].reshape(hidden, -1)) for h in range(2)], axis=1
+        )
+        y_ref[0, rows, :] = (after + scale_two * branch_two).astype(BF16)
+        upstream = dy_ref[0, rows, :].astype(F32)
+        add_to(5, upstream * branch_two)
+        dbm = (upstream * scale_two).astype(BF16)
+        m["dbmt"][:, rows] = dbm.T
+        grad = jnp.zeros((TILE, width), F32)
+        for n in range(4):
+            half, columns = n // 2, pl.ds((n % 2) * part, part)
+            back = dot_t(dbm[:, : width // 2], wd[0, n].reshape(part, -1)) + dot_t(
+                dbm[:, width // 2 :], wd[1, n].reshape(part, -1)
+            )
+            du = (back * slope[half * TILE : (half + 1) * TILE, columns]).astype(BF16)
+            m["du"][half, rows, columns] = du
+            grad = grad + dot_t(du, wu[half, :, :, :, :, columns].reshape(width, part))
+        add_to(3, grad * unit)
+        add_to(4, grad)
+        dx1 = upstream + norm_back(unit, scale, gain_two, grad)
+        m["dx1"][rows, :] = dx1
+        add_to(2, dx1 * branch)
+        dba = (dx1 * scale_one).astype(BF16)
+        m["dba"][0, rows, :] = dba[:, : width // 2]
+        m["dba"][1, rows, :] = dba[:, width // 2 :]
+        dmixed = (
+            dot_t(dba[:, : width // 2], wo[0].reshape(width, -1))
+            + dot_t(dba[:, width // 2 :], wo[1].reshape(width, -1))
+        ).astype(BF16)
+        for p in range(PAIRS):
+            for i in range(TILE // BLOCK):
+                two_heads(
+                    m["dom"],
+                    p,
+                    t * (TILE // BLOCK) + i,
+                    dmixed[i * BLOCK : (i + 1) * BLOCK, p * 128 : (p + 1) * 128],
+                )
+        return 0
+
+    lax.fori_loop(0, tiles, middle, 0)
+
+    for each in gathers:
+        for made in each.values():
+            made.wait_send()
+    m["s_u0"], m["s_o0"] = wu.at[0], wo.at[0]
+
+    def scatter(name, own, result, rows):
+        bufs = [m["s_%s%d" % (name, i)] for i in range(5)]
+        return Scatter(own, bufs, result, rows, links, at)
+
+    sum_u = scatter("u", m["own_u"], gu, width // 16)
+    sum_d = scatter("d", m["own_d"], m["down_t"], width // 2)
+    sum_o = scatter("o", m["own_o"], go, width // 16)
+    sum_q = scatter("q", m["own_q"], gq, width // 16)
+
+    def down_grads(k, _):
+        right = m["act"][:, start_of(k, hidden // 4)]
+        for which, side in ((0, core), (1, other)):
+            made = dot(m["dbmt"][start_of(side, width // 2), :], right)
+            for i in range(4):
+                piece = made[:, i * 128 : (i + 1) * 128]
+                if which == 0:
+                    m["own_d"][start_of(k * 4 + i, width // 2), :] = piece
+                else:
+                    sum_d.out[k, i // 2, i % 2] = piece.astype(BF16)
+        return 0
+
+    lax.fori_loop(0, 4, down_grads, 0)
+    sum_d.step(0)
+
+    def columns_of(sum_x, left, right_ref, step):
+        def one(n, _):
+            columns = start_of(n, step)
+            sum_x.own[:, columns] = dot(left[...], right_ref[core, :, columns])
+            made = dot(left[...], right_ref[other, :, columns]).astype(BF16)
+            sum_x.out[:, :, :, :, columns] = made.reshape(4, 2, 2, -1, step)
+            return 0
+
+        lax.fori_loop(0, sum_x.own.shape[1] // step, one, 0)
+        sum_x.step(0)
+
+    columns_of(sum_u, m["n2t"], m["du"], 256)
+    columns_of(sum_o, m["ot"], m["dba"], 256)
+    dp = m["du"]
+
+    plan = [
+        [(sum_d, 1), (sum_u, 1)],
+        [(sum_o, 1), (sum_d, 2), (sum_u, 2)],
+        [(sum_o, 2), (sum_d, 3), (sum_u, 3)],
+        [(sum_o, 3), (sum_d, 4), (sum_u, 4)],
+    ]
+    for p in range(PAIRS):
+        dkx, dvx = m["dkx"], m["dvx"]
+        dkx[...] = jnp.zeros_like(dkx)
+        dvx[...] = jnp.zeros_like(dvx)
+
+        def attend_back(b, _, p=p):
+            rows = start_of(b, BLOCK)
+            window = pl.ds(pl.multiple_of(b * BLOCK, BLOCK), SPAN)
+            queries = m["qm"][p, start_of(b, 2 * BLOCK), :]
+            dmixed = m["dom"][p, start_of(b, 2 * BLOCK), :]
+            low = m["probs"][p, b]
+            probs = low.astype(F32)
+            dprobs = dot_t(m["vx"][p, window, :], dmixed)
+            balance = jnp.sum(dprobs * probs, axis=0, keepdims=True)
+            dscores = (probs * (dprobs - balance)).astype(BF16)
+            dvx[window, :] = dvx[window, :] + dot(low, dmixed)
+            dkx[window, :] = dkx[window, :] + dot(dscores, queries)
+            joined = heads_joined(dot(m["kt"][p, :, window], dscores)).T * factor
+            m["du"][0, rows, p * 128 : (p + 1) * 128] = turned(
+                joined, m["cos"][rows, :], -m["sin"][rows, :]
+            ).astype(BF16)
+            return 0
+
+        lax.fori_loop(0, 2, attend_back, 0)
+        h_out, h_in = m["h_out"], m["h_in"]
+        h_out[p, 0] = dkx[0:REACH, :].astype(BF16)
+        h_out[p, 1] = dvx[0:REACH, :].astype(BF16)
+        halo_back = links.copy(h_out.at[p], h_in.at[p], "s")
+        halo_back.start()
+        for one, step in plan[p]:
+            one.step(step)
+        lax.fori_loop(2, blocks, attend_back, 0)
+        halo_back.wait_recv()
+        dkx[tail, :] = dkx[tail, :] + h_in[p, 0].astype(F32)
+        dvx[tail, :] = dvx[tail, :] + h_in[p, 1].astype(F32)
+        k_half, k_at = divmod(PAIRS + p, 6)
+        v_half, v_at = divmod(2 * PAIRS + p, 6)
+
+        def finish(t, _, k_half=k_half, k_at=k_at, v_half=v_half, v_at=v_at):
+            rows = start_of(t, TILE)
+            placed = pl.ds(pl.multiple_of(REACH + t * TILE, TILE), TILE)
+            dp[k_half, rows, k_at * 128 : (k_at + 1) * 128] = turned(
+                dkx[placed, :], m["cos"][rows, :], -m["sin"][rows, :]
+            ).astype(BF16)
+            dp[v_half, rows, v_at * 128 : (v_at + 1) * 128] = dvx[placed, :].astype(BF16)
+            return 0
+
+        lax.fori_loop(0, tiles, finish, 0)
+
+    sum_o.step(4)
+    columns_of(sum_q, m["n1t"], dp, 256)
+
+    def first(t, _):
+        rows = start_of(t, TILE)
+        grad = dot_t(dp[0, rows, : 3 * width // 2], wq[0].reshape(width, -1)) + dot_t(
+            dp[1, rows, : 3 * width // 2], wq[1].reshape(width, -1)
+        )
+        unit, scale = normalized(x_ref[0, rows, :].astype(F32))
+        add_to(0, grad * unit)
+        add_to(1, grad)
+        ig_ref[0, rows, :] = (
+            m["dx1"][rows, :] + norm_back(unit, scale, gain_one, grad)
+        ).astype(BF16)
+        return 0
+
+    lax.fori_loop(0, tiles, first, 0)
+
+    v_out, v_in, v_z = m["v_out"], m["v_in"], m["v_z"]
+    here, there = start_of(core, width // 2), start_of(other, width // 2)
+    v_out[0] = acc[:, there]
+    hops = [links.copy(v_out.at[i], v_in.at[i], peer) for i, peer in enumerate(("s", "y", "x"))]
+    hops[0].start()
+    sum_q.step(1)
+    hops[0].wait_recv()
+    v_out[1] = acc[:, here] + v_in[0]
+    hops[1].start()
+    sum_q.step(2)
+    hops[1].wait_recv()
+    v_out[2] = v_out[1] + v_in[1]
+    hops[2].start()
+    sum_q.step(3)
+    hops[2].wait_recv()
+    v_z[z] = v_out[2] + v_in[2]
+    spreads = [links.copy(v_z.at[z], v_z.at[z], k) for k in (1, 2, 3)]
+    for each in spreads:
+        each.start()
+    sum_q.step(4)
+    gd[...] = m["down_t"][...].T
+    for each in spreads:
+        each.wait_recv()
+    gv[...] = (v_z[0] + v_z[1]) + (v_z[2] + v_z[3])
+    gathered = [made for each in gathers for made in each.values()]
+    links.drain(skip=gathered + [one.d for one in (sum_u, sum_d, sum_o, sum_q)])
+
+
+def local_staged(
+    inputs,
+    cotangent,
+    segment_ids,
+    qkv_weight,
+    out_weight,
+    up_weight,
+    down_weight,
+    *vectors,
+):
+    frames, width = inputs.shape[1:]
+    hidden = up_weight.shape[1] * 2
+    items = scratch_list(frames, width, hidden)
+    whole = pl.BlockSpec(memory_space=pltpu.VMEM)
+    outs = [
+        jax.ShapeDtypeStruct(inputs.shape, BF16),
+        jax.ShapeDtypeStruct(inputs.shape, BF16),
+        *[
+            jax.ShapeDtypeStruct(w.shape, F32)
+            for w in (qkv_weight, out_weight, up_weight, down_weight)
+        ],
+        jax.ShapeDtypeStruct((8, width // 2), F32),
+    ]
+    results = pl.pallas_call(
+        functools.partial(layer_kernel, [name for name, _, _ in items]),
+        out_shape=outs,
+        in_specs=[whole] * 13,
+        out_specs=[whole] * 7,
+        scratch_shapes=[pltpu.VMEM(shape, kind) for _, shape, kind in items]
+        + [pltpu.SemaphoreType.DMA((SLOTS,)), pltpu.SemaphoreType.DMA((SLOTS,))],
+        compiler_params=pltpu.CompilerParams(
+            collective_id=0, has_side_effects=True, vmem_limit_bytes=VMEM_LIMIT
+        ),
+    )(
+        inputs,
+        cotangent,
+        segment_ids,
+        qkv_weight,
+        out_weight,
+        up_weight,
+        down_weight,
+        *[v.reshape(1, -1) for v in vectors],
+    )
+    sums = results[6]
+    return (*results[:6], *[sums[i] for i in range(6)])
+
+
+VMEM_LIMIT = 64 * 2**20
+
+
 def solution(mesh):
     placed = (
         P("rows", "tm", None),
@@ -344,8 +1115,9 @@
         P("tm"),
         P("tm"),
     )
+    staged = mesh.shape["rows"] == 16 and mesh.shape["tm"] == 2
     return jax.shard_map(
-        local,
+        local_staged if staged else local,
         mesh=mesh,
         in_specs=placed,
         out_specs=(

time: 720 us -> 150 us (0.21); the launches traced: 712 us -> 149 us
  waiting for transfers between devices: 334 us -> 0 us
  Pallas kernels: 0 us -> 141 us
  matrix products: 135 us -> 0 us
  blocking collectives: 121 us -> 0 us
  other arithmetic: 46.8 us -> 0 us
  local copies, waits for them, and re-layouts: 48.8 us -> 7.81 us
  between operations: 15.8 us -> 0.67 us
  starting transfers between devices: 11.2 us -> 0 us
    reduce_scatter x8 -> x0, waiting for transfers between devices: 321 us -> none  [the longest x1 127 us: local(): lax.psum_scatter(reduced[0], 'rows', scatter_dimension=0, tiled=True)]
    pallas_call x0 -> x1, Pallas kernels: none -> 141 us  [local_staged(): pl.pallas_call(functools.partial(layer_kernel, [name for name, _, _ in it...]
    dot_general x24 -> x0, matrix products: 135 us -> none  [the longest x1 24.8 us: local(): hidden = jnp.dot(normed_two_low, w_up, preferred_element_type=jnp.float32)]
    all_gather x11 -> x0, blocking collectives: 72.6 us -> none  [the longest x1 49.6 us: local(): lax.all_gather(gathered[1], 'rows', axis=0, tiled=True)]
    psum x1 -> x0, blocking collectives: 43.2 us -> none  [local(): lax.psum((reduced[4], reduced[5], reduced[6], reduced[7], reduced[8], red...]
    convert_element_type x20 -> x0, other arithmetic: 18.1 us -> none  [the longest x2 14 us: local(): grad_scores = (probs_full * (grad_probs - balance)).astype(low_type)]
    reduce_sum x10 -> x0, other arithmetic: 17.5 us -> none  [the longest x3 7.98 us: layer_norm(): return centred * lax.rsqrt(variance + EPSILON) * gain_vec + bias_vec]
    unnamed x145 -> x16, local copies, waits for them, and re-layouts: 23.2 us -> 6.31 us
  transfers between devices with their start and end apart: 16 -> 0, of which waited for: 8 -> 0; matrix products, arithmetic and copies ran while one was open for 25% -> 0% of each run, Pallas kernels for 0% -> 0%
where the time goes in v2:
time: 150 us; the launch traced here: 149 us
  Pallas kernels  141 us (94%)
  local copies, waits for them, and re-layouts  7.81 us (5%)
    pallas_call x1, Pallas kernels, local_staged(): pl.pallas_call(functools.partial(layer_kernel, [name for name, _, _ in it...  141 us
    unnamed x16, local copies, waits for them, and re-layouts  6.31 us

profile of v2, /device:TPU:0, one launch (start us, length us, event | category | flops | bytes accessed | tf_op | source)
XLA Modules:
  0.0 149.5 jit_solution(4978997512708737246)
XLA Ops:
  0.6 141.0 %shard_map.220 = (bf16[1,1024,512]{2,1,0:T(8,128)(2,1)}, bf16[1,1024,512]{2,1,0:T(8,128)(2,1)}, f32[32,768]{1,0:T(8,128)}, f32[32,256]{1,0:T(8,128)}, f32[32,102...) custom-call(bf16[1,1024,512]{2,1,0:T(8,128)(2,1)} %refs_0_.1, bf16[1,1024,512]{2,1,0:T(8,128)(2,1)} %refs_1_.1, ...), custom_call_target="tpu_custom_call" | custom-call | tf_op jit(solution)/shard_map/pallas_call | solution.py:1075
  141.6 1.5 %fusion = (f32[1,256]{1,0:T(1,128)}, f32[1,256]{1,0:T(1,128)}, f32[1,256]{1,0:T(1,128)}, f32[1,256]{1,0:T(1,128)}, f32[1,256]{1,0:T(1,128)}, /*index=5*/f32[1,256]{1,0:T(1,128)}) fusion(f32[8,256]{1,0:T(8,128)} %get-tuple-element.25), kind=kLoop, calls=%fused_computation | loop fusion | bytes 12288 | tf_op jit(solution)/shard_map/slice | solution.py:1096
  143.1 0.0 copy-start
  143.1 2.4 %copy.31 = bf16[1,1024,512]{2,1,0:T(8,128)(2,1)} copy(bf16[1,1024,512]{2,1,0:T(8,128)(2,1)} %get-tuple-element.44) | data formatting | bytes 2097152
  145.5 0.0 copy-done
  145.5 0.0 copy-start.3
  145.5 1.0 copy.32
  146.5 0.0 copy-done.3
  146.5 0.0 copy-start.4
  146.5 0.0 copy-start.2
  146.5 0.6 copy.33
  147.1 0.1 copy-done.4
  147.2 0.6 copy.34
  147.8 0.0 copy-done.2
  147.8 0.0 copy-start.1
  147.8 0.7 copy.35
  148.5 0.3 copy-done.1
  148.8 0.7 copy.36
Async XLA Ops:
  143.1 2.4 %copy-start = (bf16[1,1024,512]{2,1,0:T(8,128)(2,1)S(1)}, bf16[1,1024,512]{2,1,0:T(8,128)(2,1)}, u32[]{:S(2)}) copy-start(bf16[1,1024,512]{2,1,0:T(8,128)(2,1)} %get-tuple-element.45) | copy-start | bytes 3145732
  145.5 1.0 copy-start.3
  146.5 0.8 copy-start.4
  146.5 1.4 copy-start.2
  147.8 1.0 copy-start.1

commit v3 on v0

--- a/solution.py
+++ b/solution.py
@@ -1,8 +1,11 @@
+import functools
 import math
 
 import jax
 import jax.numpy as jnp
 from jax import lax
+from jax.experimental import pallas as pl
+from jax.experimental.pallas import tpu as pltpu
 from jax.sharding import PartitionSpec as P
 
 H = 8
@@ -328,6 +331,925 @@
     )
 
 
+MESH_IDS = pl.DeviceIdType.MESH
+F32 = jnp.float32
+BF16 = jnp.bfloat16
+
+
+def dot(left, right, contract=((1,), (0,))):
+    return lax.dot_general(left, right, (contract, ((), ())), preferred_element_type=F32)
+
+
+def dot_t(left, right):
+    return dot(left, right, ((1,), (1,)))
+
+
+def start_of(index, size):
+    return pl.ds(pl.multiple_of(index * size, size), size)
+
+
+def coordinates():
+    row, core = lax.axis_index("rows"), lax.axis_index("tm")
+    return row, core, lax.rem(row, 2), lax.rem(lax.div(row, 2), 2), lax.div(row, 4)
+
+
+def peers_of(at):
+    row, core, x, y, z = at
+    found = {
+        "x": (row + 1 - 2 * x, core),
+        "y": (row + 2 - 4 * y, core),
+        "s": (row, 1 - core),
+    }
+    for k in (1, 2, 3):
+        found[k] = (lax.rem(z + k, 4) * 4 + lax.rem(row, 4), core)
+    return found
+
+
+def enter(peers):
+    barrier = pltpu.get_barrier_semaphore()
+    for peer in peers.values():
+        pl.semaphore_signal(barrier, inc=1, device_id=peer, device_id_type=MESH_IDS)
+    pl.semaphore_wait(barrier, len(peers))
+
+
+class Links:
+    def __init__(self, sems, peers):
+        self.sems, self.peers, self.used = sems, peers, 0
+
+    def slot(self):
+        self.used += 1
+        return self.sems.at[self.used - 1]
+
+    def copy(self, src, dst, peer, send, recv):
+        return pltpu.make_async_remote_copy(
+            src_ref=src,
+            dst_ref=dst,
+            send_sem=send,
+            recv_sem=recv,
+            device_id=self.peers[peer],
+            device_id_type=MESH_IDS,
+        )
+
+    def single(self, src, dst, peer):
+        return self.copy(src, dst, peer, self.slot(), self.slot())
+
+
+def await_bytes(like, sem):
+    pltpu.make_async_copy(like, like, sem).wait()
+
+
+class Gather:
+    def __init__(self, units, i, links, at):
+        full = units.at[i]
+        row, core, x, y, z = at
+        half = full.shape[4] // 2
+        low, high = pl.ds(0, half), pl.ds(half, half)
+        every = slice(None)
+        near, far = links.slot(), links.slot()
+        got = [links.slot() for _ in range(4)]
+
+        def copy(where, peer, send, recv):
+            return links.copy(full.at[where], full.at[where], peer, send, recv)
+
+        self.starts = (
+            [copy((core, z, y, x), k, near, got[0]) for k in (1, 2, 3)],
+            [
+                copy((core, every, y, x, low), "x", far, got[1]),
+                copy((core, every, y, x, high), "y", far, got[1]),
+                copy((core, every, y, x), "s", far, got[3]),
+            ],
+            [
+                copy((core, every, y, every, low), "y", far, got[2]),
+                copy((core, every, every, x, high), "x", far, got[2]),
+                copy((core, every, y, 1 - x, low), "s", far, got[3]),
+                copy((core, every, 1 - y, x, high), "s", far, got[3]),
+            ],
+            [
+                copy((core, every, 1 - y, every, low), "s", far, got[3]),
+                copy((core, every, every, 1 - x, high), "s", far, got[3]),
+            ],
+            [],
+        )
+        self.waits = (
+            None,
+            (full.at[core, 0:3, y, x], got[0]),
+            (full.at[core, :, y, x], got[1]),
+            (full.at[core, :, y], got[2]),
+            (full.at[1 - core], got[3]),
+        )
+        self.sent = ((full.at[core, 0:3, y, x], near), (units.at[0:7, 0, 0], far))
+
+    def step(self, number):
+        if number > 0:
+            await_bytes(*self.waits[number])
+        for copy in self.starts[number]:
+            copy.start()
+
+    def drain(self):
+        for like, sem in self.sent:
+            await_bytes(like, sem)
+
+
+class Scatter:
+    def __init__(self, own, out, arrived, result, links, at, units):
+        self.own, self.out, self.result, self.at = own, out, result, at
+        self.s_in, self.c_in, self.b_in, self.a_in = arrived
+        row, core, x, y, z = at
+        self.rows = out.shape[3]
+        half = self.half = self.rows // 2
+        low, high = self.low, self.high = pl.ds(0, half), pl.ds(half, half)
+        every = slice(None)
+        self.d = links.single(out, self.s_in, "s")
+        self.far = links.slot()
+        self.got = [links.slot() for _ in range(3)]
+        self.units = units
+
+        def copy(src, dst, peer, which):
+            return links.copy(src, dst, peer, self.far, self.got[which])
+
+        self.c1 = copy(out.at[every, 1 - y, every, low], self.c_in.at[0], "y", 0)
+        self.c2 = copy(out.at[every, every, 1 - x, high], self.c_in.at[1], "x", 0)
+        self.b1 = copy(out.at[every, y, 1 - x, low], self.b_in.at[0], "x", 1)
+        self.b2 = copy(out.at[every, 1 - y, x, high], self.b_in.at[1], "y", 1)
+        self.a = [
+            copy(out.at[lax.rem(z + k, 4), y, x], self.a_in.at[k - 1], k, 2) for k in (1, 2, 3)
+        ]
+
+    def mine(self, k, y, x, part):
+        begin = ((k * 2 + y) * 2 + x) * self.rows + part * self.half
+        return self.own[pl.ds(pl.multiple_of(begin, self.half), self.half), :] + self.s_in[
+            k, y, x, pl.ds(part * self.half, self.half)
+        ].astype(F32)
+
+    def column(self, k, part):
+        row, core, x, y, z = self.at
+        place = x if part == 0 else y
+        return (
+            self.mine(k, y, x, part)
+            + self.c_in[part, k, place].astype(F32)
+            + self.b_in[part, k].astype(F32)
+        )
+
+    def step(self, number):
+        row, core, x, y, z = self.at
+        low, high, out = self.low, self.high, self.out
+        c_in = self.c_in
+        if number == 0:
+            self.d.start()
+        if number == 1:
+            self.d.wait()
+            for k in range(4):
+                for i in range(2):
+                    out[k, 1 - y, i, low] = self.mine(k, 1 - y, i, 0).astype(BF16)
+            self.c1.start()
+            for k in range(4):
+                for i in range(2):
+                    out[k, i, 1 - x, high] = self.mine(k, i, 1 - x, 1).astype(BF16)
+            self.c2.start()
+        if number == 2:
+            await_bytes(c_in, self.got[0])
+            for k in range(4):
+                out[k, y, 1 - x, low] = (
+                    self.mine(k, y, 1 - x, 0) + c_in[0, k, 1 - x].astype(F32)
+                ).astype(BF16)
+            self.b1.start()
+            for k in range(4):
+                out[k, 1 - y, x, high] = (
+                    self.mine(k, 1 - y, x, 1) + c_in[1, k, 1 - y].astype(F32)
+                ).astype(BF16)
+            self.b2.start()
+        if number == 3:
+            await_bytes(self.b_in, self.got[1])
+            for k in (1, 2, 3):
+                there = lax.rem(z + k, 4)
+                out[there, y, x, low] = self.column(there, 0).astype(BF16)
+                out[there, y, x, high] = self.column(there, 1).astype(BF16)
+                self.a[k - 1].start()
+            self.own[low, :] = self.column(z, 0)
+            self.own[high, :] = self.column(z, 1)
+        if number == 4:
+            await_bytes(self.a_in, self.got[2])
+            self.result(
+                self.own[: self.rows, :]
+                + (self.a_in[0].astype(F32) + self.a_in[1].astype(F32) + self.a_in[2].astype(F32))
+            )
+
+    def drain(self):
+        await_bytes(self.units.at[0:5, 0:3, 0, 0], self.far)
+
+
+def gelu_and_slope(values):
+    cdf = 0.5 + 0.5 * lax.erf(values * math.sqrt(0.5))
+    bell = jnp.exp2((values * values) * (-0.5 * math.log2(math.e)))
+    return values * cdf, cdf + (values * (1.0 / math.sqrt(2.0 * math.pi))) * bell
+
+
+def lane_pattern(shape, size):
+    return lax.rem(lax.broadcasted_iota(jnp.int32, shape, len(shape) - 1), size)
+
+
+def turned(values, cosine, sine):
+    first = lane_pattern(values.shape, HD) < HD // 2
+    swapped = jnp.where(first, pltpu.roll(values, 96, 1), pltpu.roll(values, 32, 1))
+    return values * cosine + swapped * sine
+
+
+TILE = 256
+BLOCK = 128
+SPAN = BLOCK + REACH
+PAIRS = H // 2
+COLUMNS = 256
+UNITS = 12
+GROUP, OUT, DOWN, UP = 0, 3, (4, 6, 8, 10), (5, 7, 9, 11)
+OFFSETS = (0, 2, 4, 6, 7)
+CHUNKS = (
+    (((0, 0), (1, 0)), ((2, 0), (2, 1))),
+    (((0, 1), (1, 1)), ((2, 2), (1, 2))),
+    (((0, 2), (0, 3)), ((2, 3), (1, 3))),
+)
+
+
+def place_of(kind, p):
+    for g, cores in enumerate(CHUNKS):
+        for c, pair in enumerate(cores):
+            if (kind, p) in pair:
+                return g, c, pair.index((kind, p))
+
+
+def run(begin, end, body, events=None):
+    def with_events(i, carried):
+        for when, actions in sorted((events or {}).items()):
+
+            @pl.when(i == when)
+            def _(actions=actions):
+                for action in actions:
+                    action()
+
+        body(i, carried)
+        return 0
+
+    lax.fori_loop(begin, end, with_events, 0)
+
+
+def in_turn(count, stages, events):
+    for i in range(count + len(stages) - 1):
+        for action in events.get(i, []):
+            action()
+        for late, stage in enumerate(stages):
+            if 0 <= i - late < count:
+                stage(i - late)
+
+
+def regroup(tiles, quarter, back=False):
+    group = lax.broadcasted_iota(jnp.int32, (1, 128), 1) // 32
+    out = jnp.zeros_like(tiles[0])
+    for a in range(4):
+        out = jnp.where(group == a, pltpu.roll(tiles[a], (a - quarter) * 32 % 128, 1), out)
+    return out
+
+
+def scratch_list(frames, width):
+    blocks = frames // BLOCK
+    ext = REACH + frames
+    unit = (4, 2, 2, width // 16, COLUMNS)
+    half = width // 32
+    return [
+        ("w", (UNITS, 2) + unit, BF16),
+        ("vecs", (2, 8, width // 2), F32),
+        ("segs", (2, 8, frames), F32),
+        ("n1t", (width, frames), BF16),
+        ("cos", (frames, 128), F32),
+        ("sin", (frames, 128), F32),
+        ("bias", (blocks, SPAN, BLOCK), BF16),
+        ("qx", (PAIRS, frames, 128), BF16),
+        ("kx", (PAIRS, ext, 128), BF16),
+        ("vx", (PAIRS, ext, 128), BF16),
+        ("kt", (PAIRS, 128, ext), BF16),
+        ("vt", (PAIRS, 128, ext), BF16),
+        ("probs", (PAIRS, blocks, SPAN, 2 * BLOCK), BF16),
+        ("ot", (width, frames), BF16),
+        ("n2t", (width, frames), BF16),
+        ("actt", (2 * COLUMNS, frames), BF16),
+        ("du", (2, frames, COLUMNS), BF16),
+        ("after", (frames, width), F32),
+        ("branch", (frames, width), BF16),
+        ("branch_two", (frames, width), F32),
+        ("dx1", (frames, width), F32),
+        ("dba", (2, frames, width // 2), BF16),
+        ("dox", (PAIRS, frames, 128), BF16),
+        ("dp", (3, 2, frames, COLUMNS), BF16),
+        ("dkx", (ext, 128), F32),
+        ("dvx", (ext, 128), F32),
+        ("h_out", (PAIRS, 2, REACH, 128), BF16),
+        ("h_in", (PAIRS, 2, REACH, 128), BF16),
+        ("acc", (8, width), F32),
+        ("v_out", (3, 8, width // 2), F32),
+        ("v_in", (3, 8, width // 2), F32),
+        ("v_z", (4, 8, width // 2), F32),
+        ("own", (UNITS - 3, width, COLUMNS), F32),
+        ("up_sums", (4, width // 16, COLUMNS), F32),
+        ("s_in", (UNITS,) + unit, BF16),
+        ("c_in", (UNITS, 2, 4, 2, half, COLUMNS), BF16),
+        ("b_in", (UNITS, 2, 4, half, COLUMNS), BF16),
+        ("a_in", (UNITS, 3, width // 16, COLUMNS), BF16),
+    ]
+
+
+SLOTS = 12 * UNITS + 2 * (2 + 2 * PAIRS + PAIRS + 3) + 4
+
+
+def layer_kernel(names, *refs):
+    x_ref, dy_ref, seg_ref = refs[:3]
+    wq_shard, wo_shard, wu_shard, wd_shard = refs[3:7]
+    vectors = refs[7:13]
+    y_ref, ig_ref, gq, go, gu, gd, gv = refs[13:20]
+    m = dict(zip(names, refs[20:-1]))
+    at = coordinates()
+    row, core, x, y, z = at
+    peers = peers_of(at)
+    links = Links(refs[-1], peers)
+    frames, width = x_ref.shape[1:]
+    piece = width // 16
+    blocks, tiles = frames // BLOCK, frames // TILE
+    factor = 1.0 / math.sqrt(HD)
+    w = m["w"]
+    other = 1 - core
+
+    def chunk_columns(g, j):
+        offsets = []
+        for c in range(2):
+            kind, p = CHUNKS[g][c][j]
+            offsets.append((kind * PAIRS + p - 6 * c) * 128)
+        begin = offsets[0] + core * (offsets[1] - offsets[0])
+        return pl.ds(pl.multiple_of(begin, 128), 128)
+
+    for g in range(3):
+        for j in range(2):
+            w[g, core, z, y, x, :, j * 128 : (j + 1) * 128] = wq_shard[
+                :, chunk_columns(g, j)
+            ].astype(BF16)
+    m["vecs"][core] = jnp.concatenate(
+        [v[...].astype(BF16).astype(F32) for v in vectors]
+        + [jnp.zeros((2, width // 2), F32)],
+        axis=0,
+    )
+    m["segs"][core] = jnp.broadcast_to(seg_ref[...].astype(F32), (8, frames))
+    enter(peers)
+    vec_copy = links.single(m["vecs"].at[core], m["vecs"].at[core], "s")
+    seg_copy = links.single(m["segs"].at[core], m["segs"].at[core], "s")
+    gathers = [Gather(w, i, links, at) for i in range(UNITS)]
+
+    def tick(k):
+        for step in (4, 3, 2, 1, 0):
+            if 0 <= k - OFFSETS[step] < UNITS:
+                gathers[k - OFFSETS[step]].step(step)
+
+    vec_copy.start()
+    seg_copy.start()
+    tick(0)
+    w[OUT, core, z, y, x] = wo_shard[...].astype(BF16)
+    for q in range(4):
+        w[DOWN[q], core, z, y, x] = wd_shard[q * piece : (q + 1) * piece, :].astype(BF16)
+    for q in range(4):
+        for j in range(2):
+            made = regroup(
+                [wu_shard[:, (4 * j + a) * 128 : (4 * j + a + 1) * 128] for a in range(4)], q
+            )
+            w[UP[q], core, z, y, x, :, j * 128 : (j + 1) * 128] = made.astype(BF16)
+
+    def vector(i):
+        return jnp.concatenate([m["vecs"][0, i : i + 1, :], m["vecs"][1, i : i + 1, :]], axis=1)
+
+    def normalized(values):
+        average = jnp.mean(values, axis=-1, keepdims=True)
+        centred = values - average
+        variance = jnp.mean(centred * centred, axis=-1, keepdims=True)
+        scale = lax.rsqrt(variance + EPSILON)
+        return centred * scale, scale
+
+    vec_copy.wait_recv()
+    n1 = y_ref
+    gain_one, bias_one = vector(0), vector(1)
+
+    def norm_one(t, _):
+        rows = start_of(t, TILE)
+        unit, _scale = normalized(x_ref[0, rows, :].astype(F32))
+        low = (unit * gain_one + bias_one).astype(BF16)
+        n1[0, rows, :] = low
+        m["n1t"][:, rows] = low.T
+
+    tick(1)
+    run(0, tiles, norm_one)
+    tick(2)
+
+    seg_copy.wait_recv()
+    segs = m["segs"]
+
+    def spread(which, begin):
+        line = segs[which, 0:1, pl.ds(pl.multiple_of(begin, BLOCK), BLOCK)]
+        return jnp.broadcast_to(line, (BLOCK, BLOCK)).T
+
+    seg_blocks = m["own"]
+
+    def seg_place(e):
+        return (e // 8, pl.ds((e % 8) // 2 * BLOCK, BLOCK), pl.ds(e % 2 * BLOCK, BLOCK))
+
+    for e in range(REACH // BLOCK):
+        halo = spread(other, frames - REACH + e * BLOCK)
+        seg_blocks[seg_place(e)] = jnp.where(core > 0, halo, -1.0)
+
+    lanes = lane_pattern((1, 128), HD // 2).astype(F32)
+    frequency = jnp.exp(lanes * (-2.0 * math.log(10000.0) / HD))
+    first_half = lane_pattern((BLOCK, 128), HD) < HD // 2
+
+    def tables(b, _):
+        rows = start_of(b, BLOCK)
+        here = spread(core, b * BLOCK)
+        count = jnp.zeros((BLOCK, BLOCK), F32)
+        for which in range(2):
+            for k in range(blocks):
+                line = segs[which, 0:1, k * BLOCK : (k + 1) * BLOCK]
+                count = count + jnp.where(line < here, 1.0, 0.0)
+        began = jnp.sum(count, axis=1, keepdims=True)
+        frame = lax.broadcasted_iota(jnp.int32, (BLOCK, 1), 0) + (core * frames + b * BLOCK)
+        angle = (frame.astype(F32) - began) * frequency
+        m["cos"][rows, :] = jnp.cos(angle)
+        sine = jnp.sin(angle)
+        m["sin"][rows, :] = jnp.where(first_half, -sine, sine)
+
+    run(0, blocks, tables, {blocks // 2: [lambda: tick(3)]})
+    tick(4)
+
+    for b in range(blocks):
+        seg_blocks[seg_place(REACH // BLOCK + b)] = spread(core, b * BLOCK)
+    distance = (
+        lax.broadcasted_iota(jnp.int32, (SPAN, BLOCK), 1)
+        - lax.broadcasted_iota(jnp.int32, (SPAN, BLOCK), 0)
+        + REACH
+    )
+    near = (distance >= 0) & (distance < WINDOW)
+    for b in range(blocks):
+        keys = jnp.concatenate([seg_blocks[seg_place(b + i)] for i in range(SPAN // BLOCK)], axis=0)
+        line = segs[core, 0:1, b * BLOCK : (b + 1) * BLOCK]
+        m["bias"][b] = jnp.where(near & (keys == line), 0.0, NEGATIVE).astype(BF16)
+    for k in (5, 6, 7):
+        tick(k)
+
+    low_lanes = lane_pattern((1, 128), 128) < HD
+
+    def two_heads(value):
+        zero = jnp.zeros_like(value)
+        return jnp.concatenate(
+            [jnp.where(low_lanes, value, zero), jnp.where(low_lanes, zero, value)], axis=0
+        )
+
+    def projection(g):
+        def project(t, _):
+            rows = start_of(t, TILE)
+            placed = pl.ds(pl.multiple_of(REACH + t * TILE, TILE), TILE)
+            left = n1[0, rows, :]
+            cosine, sine = m["cos"][rows, :], m["sin"][rows, :]
+            for c in range(2):
+                wide = dot(left, w[g, c].reshape(width, COLUMNS))
+                for j in range(2):
+                    chunk = wide[:, j * 128 : (j + 1) * 128]
+                    kind, p = CHUNKS[g][c][j]
+                    if kind == 0:
+                        turn = turned(chunk, cosine, sine).astype(BF16)
+                        m["qx"][p, rows, :] = (turn * factor).astype(BF16)
+                    elif kind == 1:
+                        value = turned(chunk, cosine, sine).astype(BF16)
+                        m["kx"][p, placed, :] = value
+                        m["kt"][p, :, placed] = value.T
+                    else:
+                        value = chunk.astype(BF16)
+                        m["vx"][p, placed, :] = value
+                        m["vt"][p, :, placed] = value.T
+
+        return project
+
+    tail, head = pl.ds(frames, REACH), pl.ds(0, REACH)
+    mixed = ig_ref
+
+    def heads_joined(both):
+        return jnp.concatenate([both[:HD, :BLOCK], both[HD:, BLOCK:]], axis=0)
+
+    unit_rows = lax.broadcasted_iota(jnp.int32, (2 * BLOCK, BLOCK), 0)
+    unit_lanes = lax.broadcasted_iota(jnp.int32, (2 * BLOCK, BLOCK), 1)
+    picks = (lax.rem(unit_rows, BLOCK) == unit_lanes).astype(F32).astype(BF16)
+
+    def block_rows(b):
+        return pl.ds(b * BLOCK, BLOCK)
+
+    def block_window(b):
+        return pl.ds(b * BLOCK, SPAN)
+
+    def spare(i):
+        return m["after"].at[pl.ds(i // 2 * SPAN, SPAN), pl.ds(i % 2 * 2 * BLOCK, 2 * BLOCK)]
+
+    def spare_low(i):
+        return m["branch"].at[pl.ds(i // 2 * SPAN, SPAN), pl.ds(i % 2 * 2 * BLOCK, 2 * BLOCK)]
+
+    def attend(p, events):
+        def score(b):
+            left = jnp.concatenate([m["kx"][p, block_window(b), :], m["bias"][b]], axis=1)
+            right = jnp.concatenate([two_heads(m["qx"][p, block_rows(b), :]), picks], axis=1)
+            spare(b % 4)[...] = dot_t(left, right)
+
+        def soften(b):
+            scores = spare(b % 4)[...]
+            top = jnp.max(scores, axis=0, keepdims=True)
+            weights = jnp.exp(scores - top)
+            total = jnp.sum(weights, axis=0, keepdims=True)
+            m["probs"][p, b] = (weights * (1.0 / total)).astype(BF16)
+
+        def mix(b):
+            joined = heads_joined(dot(m["vt"][p, :, block_window(b)], m["probs"][p, b]))
+            m["ot"][p * 128 : (p + 1) * 128, block_rows(b)] = joined.astype(BF16)
+            mixed[0, block_rows(b), p * 128 : (p + 1) * 128] = joined.T.astype(BF16)
+
+        in_turn(blocks, (score, soften, mix), events)
+
+    halos = {}
+
+    def send_halo(kind, p):
+        ref = m["kx"] if kind == 1 else m["vx"]
+        halos[kind, p] = links.single(ref.at[p, tail], ref.at[p, head], "s")
+        halos[kind, p].start()
+
+    def take_halo(p):
+        for kind, flat, turned_ref in ((1, m["kx"], m["kt"]), (2, m["vx"], m["vt"])):
+            halos[kind, p].wait_recv()
+            turned_ref[p, :, 0:REACH] = flat[p, 0:REACH, :].T
+
+    for p in range(PAIRS):
+        if p < 3:
+            run(0, tiles, projection(p))
+            for pair in CHUNKS[p]:
+                for kind, q in pair:
+                    if kind > 0:
+                        send_halo(kind, q)
+        take_halo(p)
+        due = {
+            2: [functools.partial(tick, 8 + 2 * p)],
+            6: [functools.partial(tick, 9 + 2 * p)],
+        }
+        attend(p, due)
+
+    m["acc"][...] = jnp.zeros_like(m["acc"])
+    acc = m["acc"]
+
+    def add_to(i, values):
+        acc[i : i + 1, :] = acc[i : i + 1, :] + jnp.sum(values, axis=0, keepdims=True)
+
+    scale_one, gain_two, bias_two, scale_two = vector(2), vector(3), vector(4), vector(5)
+    n2 = y_ref
+    dba = m["dba"]
+
+    def norm_back(unit, scale, gain, grad):
+        inner = grad * gain
+        return scale * (
+            inner
+            - jnp.mean(inner, axis=-1, keepdims=True)
+            - unit * jnp.mean(inner * unit, axis=-1, keepdims=True)
+        )
+
+    def norm_two(t, _):
+        rows = start_of(t, TILE)
+        both = mixed[0, rows, :]
+        branch = jnp.concatenate(
+            [dot(both, w[OUT, c].reshape(width, COLUMNS)) for c in range(2)], axis=1
+        )
+        m["branch"][rows, :] = branch.astype(BF16)
+        after = x_ref[0, rows, :].astype(F32) + scale_one * branch
+        m["after"][rows, :] = after
+        unit, _scale = normalized(after)
+        low = (unit * gain_two + bias_two).astype(BF16)
+        n2[0, rows, :] = low
+        m["n2t"][:, rows] = low.T
+        dbm = (dy_ref[0, rows, :].astype(F32) * scale_two).astype(BF16)
+        dba[0, rows, :] = dbm[:, : width // 2]
+        dba[1, rows, :] = dbm[:, width // 2 :]
+
+    run(0, tiles, norm_two)
+
+    def result_of(i):
+        def keep(value):
+            if i < OUT:
+                for j in range(2):
+                    gq[:, chunk_columns(i, j)] = value[:, j * 128 : (j + 1) * 128]
+            elif i == OUT:
+                go[...] = value
+            elif i in DOWN:
+                q = DOWN.index(i)
+                gd[q * piece : (q + 1) * piece, :] = value
+            else:
+                m["up_sums"][UP.index(i)] = value
+
+        return keep
+
+    sums = {}
+
+    def unit_grads(i, left, right):
+        gathers[i].drain()
+        if i < OUT:
+            sums[DOWN[i]].drain()
+        place = DOWN[i] if i < OUT else i
+        out, own = w.at[place, 0], m["own"].at[place - 3]
+        arrived = [m[name].at[i] for name in ("s_in", "c_in", "b_in", "a_in")]
+        sums[i] = Scatter(own, out, arrived, result_of(i), links, at, m["s_in"])
+        own[...] = dot(left[...], right[core])
+        out[...] = dot(left[...], right[other]).astype(BF16).reshape(4, 2, 2, piece, COLUMNS)
+        sums[i].step(0)
+
+    def step_of(i, number):
+        return lambda: sums[i].step(number)
+
+    def feed(q):
+        def middle(t, _):
+            rows = start_of(t, TILE)
+            ups = [w[UP[q], h].reshape(width, COLUMNS) for h in range(2)]
+            dbm = jnp.concatenate([dba[c, rows, :] for c in range(2)], axis=1)
+            acts, dus = [], []
+            for h in range(2):
+                value, slope = gelu_and_slope(dot(n2[0, rows, :], ups[h]))
+                act = value.astype(BF16)
+                m["actt"][h * COLUMNS : (h + 1) * COLUMNS, rows] = act.T
+                down = jnp.concatenate(
+                    [w[DOWN[q], c, 2 * h : 2 * h + 2].reshape(COLUMNS, COLUMNS) for c in range(2)],
+                    axis=1,
+                )
+                du = (dot_t(dbm, down) * slope).astype(BF16)
+                m["du"][h, rows, :] = du
+                acts.append(act)
+                dus.append(du)
+            act = jnp.concatenate(acts, axis=1)
+            for c in range(2):
+                columns = pl.ds(c * COLUMNS, COLUMNS)
+                total = dot(act, w[DOWN[q], c].reshape(2 * COLUMNS, COLUMNS))
+                if q > 0:
+                    total = total + m["branch_two"][rows, columns]
+                m["branch_two"][rows, columns] = total
+            grad = dot_t(jnp.concatenate(dus, axis=1), jnp.concatenate(ups, axis=1))
+            if q > 0:
+                grad = grad + m["dx1"][rows, :]
+            m["dx1"][rows, :] = grad
+
+        return middle
+
+    def steps_of(q, number):
+        return [step_of(DOWN[q], number), step_of(UP[q], number)]
+
+    def do(actions):
+        for action in actions:
+            action()
+
+    for q in range(4):
+        events = {i: [] for i in range(tiles)}
+        if q == 0:
+            events[1] += [functools.partial(tick, 16)]
+            events[3] += [functools.partial(tick, 17)]
+        if q == 1:
+            events[2] += [functools.partial(tick, 18)]
+        if q > 0:
+            events[1] += steps_of(q - 1, 1)
+        if q > 1:
+            events[0] += steps_of(q - 2, 2)
+        if q > 2:
+            events[2] += steps_of(q - 3, 4)
+        run(0, tiles, feed(q), events)
+        if q > 1:
+            do(steps_of(q - 2, 3))
+        unit_grads(DOWN[q], m["actt"], dba)
+        unit_grads(UP[q], m["n2t"], m["du"])
+
+    def norm_two_back(t, _):
+        rows = start_of(t, TILE)
+        after, branch_two = m["after"][rows, :], m["branch_two"][rows, :]
+        y_ref[0, rows, :] = (after + scale_two * branch_two).astype(BF16)
+        upstream = dy_ref[0, rows, :].astype(F32)
+        add_to(5, upstream * branch_two)
+        unit, scale = normalized(after)
+        grad = m["dx1"][rows, :]
+        add_to(3, grad * unit)
+        add_to(4, grad)
+        dx1 = upstream + norm_back(unit, scale, gain_two, grad)
+        m["dx1"][rows, :] = dx1
+        add_to(2, dx1 * m["branch"][rows, :].astype(F32))
+        low = (dx1 * scale_one).astype(BF16)
+        sides = [low[:, : width // 2], low[:, width // 2 :]]
+        for c in range(2):
+            dba[c, rows, :] = sides[c]
+        dmixed = (
+            dot_t(sides[0], w[OUT, 0].reshape(width, COLUMNS))
+            + dot_t(sides[1], w[OUT, 1].reshape(width, COLUMNS))
+        ).astype(BF16)
+        m["n2t"][:, rows] = dmixed.T
+        for p in range(PAIRS):
+            m["dox"][p, rows, :] = dmixed[:, p * 128 : (p + 1) * 128]
+
+    run(
+        0,
+        tiles,
+        norm_two_back,
+        {0: steps_of(2, 2), 1: steps_of(3, 1)},
+    )
+    unit_grads(OUT, m["ot"], dba)
+
+    dp = m["dp"]
+    plan = [
+        {2: steps_of(2, 3) + [step_of(OUT, 1)], 4: steps_of(3, 2) + steps_of(1, 4)},
+        {2: [step_of(OUT, 2)], 4: steps_of(3, 3), 6: steps_of(2, 4), 7: [step_of(OUT, 3)]},
+        {2: [step_of(GROUP, 1)], 4: steps_of(3, 4), 6: [step_of(OUT, 4)]},
+        {0: [step_of(GROUP, 2)], 2: [step_of(GROUP + 1, 1)], 5: [step_of(GROUP, 3)]},
+    ]
+
+    def store_turned(kind, p, rows, value):
+        g, c, j = place_of(kind, p)
+        if kind < 2:
+            value = turned(value, m["cos"][rows, :], -m["sin"][rows, :])
+        dp[g, c, rows, j * 128 : (j + 1) * 128] = value.astype(BF16)
+
+    backs = []
+    for p in range(PAIRS):
+        dkx, dvx = m["dkx"], m["dvx"]
+        dkx[...] = jnp.zeros_like(dkx)
+        dvx[...] = jnp.zeros_like(dvx)
+
+        def probe(b, p=p):
+            spare(b % 4)[...] = dot_t(
+                m["vx"][p, block_window(b), :], two_heads(m["dox"][p, block_rows(b), :])
+            )
+
+        def weigh(b, p=p):
+            probs = m["probs"][p, b].astype(F32)
+            heads = (pl.ds(p * 128, 128), block_rows(b))
+            shared = m["n2t"][heads].astype(F32) * m["ot"][heads].astype(F32)
+            balance = jnp.concatenate(
+                [
+                    jnp.sum(shared[:HD], axis=0, keepdims=True),
+                    jnp.sum(shared[HD:], axis=0, keepdims=True),
+                ],
+                axis=1,
+            )
+            spare_low(b % 4)[...] = (probs * (spare(b % 4)[...] - balance)).astype(BF16)
+
+        def gather_back(b, p=p):
+            window, rows = block_window(b), block_rows(b)
+            dscores = spare_low(b % 4)[...]
+            dvx[window, :] = dvx[window, :] + dot(
+                m["probs"][p, b], two_heads(m["dox"][p, rows, :])
+            )
+            dkx[window, :] = dkx[window, :] + dot(dscores, two_heads(m["qx"][p, rows, :]))
+            joined = heads_joined(dot(m["kt"][p, :, window], dscores)).T * factor
+            store_turned(0, p, rows, joined)
+
+        h_out, h_in = m["h_out"], m["h_in"]
+        halo_back = links.single(h_out.at[p], h_in.at[p], "s")
+        backs.append(halo_back)
+
+        def send_back(p=p, halo_back=halo_back):
+            h_out[p, 0] = dkx[0:REACH, :].astype(BF16)
+            h_out[p, 1] = dvx[0:REACH, :].astype(BF16)
+            halo_back.start()
+
+        events = dict(plan[p])
+        events[4] = [send_back] + events.get(4, [])
+        in_turn(blocks, (probe, weigh, gather_back), events)
+        halo_back.wait_recv()
+        dkx[tail, :] = dkx[tail, :] + h_in[p, 0].astype(F32)
+        dvx[tail, :] = dvx[tail, :] + h_in[p, 1].astype(F32)
+
+        def finish(t, _, p=p):
+            rows = start_of(t, TILE)
+            placed = pl.ds(pl.multiple_of(REACH + t * TILE, TILE), TILE)
+            store_turned(1, p, rows, dkx[placed, :])
+            store_turned(2, p, rows, dvx[placed, :])
+
+        run(0, tiles, finish)
+        if p > 0:
+            unit_grads(GROUP + p - 1, m["n1t"], dp.at[p - 1])
+
+    sums[GROUP + 1].step(2)
+
+    def first(t, _):
+        rows = start_of(t, TILE)
+        sides = [(g, c) for g in range(3) for c in range(2)]
+        grad = dot_t(
+            jnp.concatenate([dp[g, c, rows, :] for g, c in sides], axis=1),
+            jnp.concatenate([w[g, c].reshape(width, COLUMNS) for g, c in sides], axis=1),
+        )
+        unit, scale = normalized(x_ref[0, rows, :].astype(F32))
+        add_to(0, grad * unit)
+        add_to(1, grad)
+        ig_ref[0, rows, :] = (
+            m["dx1"][rows, :] + norm_back(unit, scale, gain_one, grad)
+        ).astype(BF16)
+
+    run(
+        0,
+        tiles,
+        first,
+        {1: [step_of(GROUP + 2, 1)], 3: [step_of(GROUP, 4)]},
+    )
+
+    v_out, v_in, v_z = m["v_out"], m["v_in"], m["v_z"]
+    here, there = start_of(core, width // 2), start_of(other, width // 2)
+    v_out[0] = acc[:, there]
+    hops = [links.single(v_out.at[i], v_in.at[i], peer) for i, peer in enumerate(("s", "y", "x"))]
+    hops[0].start()
+    hops[0].wait_recv()
+    v_out[1] = acc[:, here] + v_in[0]
+    hops[1].start()
+    sums[GROUP + 2].step(2)
+    sums[GROUP + 1].step(3)
+    for j in range(2):
+        for a in range(4):
+            gu[:, (4 * j + a) * 128 : (4 * j + a + 1) * 128] = regroup(
+                [m["up_sums"][q, :, j * 128 : (j + 1) * 128] for q in range(4)], a, True
+            )
+    hops[1].wait_recv()
+    v_out[2] = v_out[1] + v_in[1]
+    hops[2].start()
+    sums[GROUP + 2].step(3)
+    hops[2].wait_recv()
+    v_z[z] = v_out[2] + v_in[2]
+    spread_send, spread_recv = links.slot(), links.slot()
+    spreads = [links.copy(v_z.at[z], v_z.at[z], k, spread_send, spread_recv) for k in (1, 2, 3)]
+    for each in spreads:
+        each.start()
+    sums[GROUP + 1].step(4)
+    sums[GROUP + 2].step(4)
+    await_bytes(v_z.at[0:3], spread_recv)
+    gv[...] = (v_z[0] + v_z[1]) + (v_z[2] + v_z[3])
+    await_bytes(v_z.at[0:3], spread_send)
+    for i, each in sums.items():
+        if i not in DOWN[:3]:
+            each.drain()
+    for each in [vec_copy, seg_copy, *halos.values(), *backs, *hops]:
+        each.wait_send()
+
+
+def write_kernel(*refs):
+    for source, target in zip(refs[:6], refs[7:13]):
+        target[...] = source[...]
+    for i, vector in enumerate(refs[13:]):
+        vector[...] = refs[6][i : i + 1, :]
+
+
+def local_staged(
+    inputs,
+    cotangent,
+    segment_ids,
+    qkv_weight,
+    out_weight,
+    up_weight,
+    down_weight,
+    *vectors,
+):
+    frames, width = inputs.shape[1:]
+    items = scratch_list(frames, width)
+    whole = pl.BlockSpec(memory_space=pltpu.VMEM)
+    shapes = [
+        jax.ShapeDtypeStruct(inputs.shape, BF16),
+        jax.ShapeDtypeStruct(inputs.shape, BF16),
+        *[
+            jax.ShapeDtypeStruct(weight.shape, F32)
+            for weight in (qkv_weight, out_weight, up_weight, down_weight)
+        ],
+    ]
+    results = pl.pallas_call(
+        functools.partial(layer_kernel, [name for name, _, _ in items]),
+        out_shape=shapes + [jax.ShapeDtypeStruct((8, width // 2), F32)],
+        in_specs=[whole] * 13,
+        out_specs=[whole] * 7,
+        scratch_shapes=[pltpu.VMEM(shape, kind) for _, shape, kind in items]
+        + [pltpu.SemaphoreType.DMA((SLOTS,))],
+        compiler_params=pltpu.CompilerParams(
+            collective_id=0, has_side_effects=True, vmem_limit_bytes=VMEM_LIMIT
+        ),
+    )(
+        inputs,
+        cotangent,
+        segment_ids,
+        qkv_weight,
+        out_weight,
+        up_weight,
+        down_weight,
+        *[v.reshape(1, -1) for v in vectors],
+    )
+    written = pl.pallas_call(
+        write_kernel,
+        out_shape=shapes + [jax.ShapeDtypeStruct((1, width // 2), F32)] * 6,
+        in_specs=[whole] * 7,
+        out_specs=[whole] * 12,
+    )(*results)
+    return (*written[:6], *[v.reshape(-1) for v in written[6:]])
+
+
+VMEM_LIMIT = 64 * 2**20
+
+
 def solution(mesh):
     placed = (
         P("rows", "tm", None),
@@ -344,8 +1266,9 @@
         P("tm"),
         P("tm"),
     )
+    staged = mesh.shape["rows"] == 16 and mesh.shape["tm"] == 2
     return jax.shard_map(
-        local,
+        local_staged if staged else local,
         mesh=mesh,
         in_specs=placed,
         out_specs=(

time: 720 us -> 113 us (0.16); the launches traced: 712 us -> 113 us
  waiting for transfers between devices: 334 us -> 0 us
  matrix products: 135 us -> 0 us
  blocking collectives: 121 us -> 0 us
  Pallas kernels: 0 us -> 112 us
  local copies, waits for them, and re-layouts: 48.8 us -> 0 us
  other arithmetic: 46.8 us -> 0 us
  between operations: 15.8 us -> 0.83 us
  starting transfers between devices: 11.2 us -> 0 us
    reduce_scatter x8 -> x0, waiting for transfers between devices: 321 us -> none  [the longest x1 127 us: local(): lax.psum_scatter(reduced[0], 'rows', scatter_dimension=0, tiled=True)]
    dot_general x24 -> x0, matrix products: 135 us -> none  [the longest x1 24.8 us: local(): hidden = jnp.dot(normed_two_low, w_up, preferred_element_type=jnp.float32)]
    pallas_call x0 -> x2, Pallas kernels: none -> 112 us  [the longest x1 109 us: local_staged(): pl.pallas_call(functools.partial(layer_kernel, [name for name, _, _ in it...]
    all_gather x11 -> x0, blocking collectives: 72.6 us -> none  [the longest x1 49.6 us: local(): lax.all_gather(gathered[1], 'rows', axis=0, tiled=True)]
    psum x1 -> x0, blocking collectives: 43.2 us -> none  [local(): lax.psum((reduced[4], reduced[5], reduced[6], reduced[7], reduced[8], red...]
    unnamed x145 -> x0, local copies, waits for them, and re-layouts: 23.2 us -> none
    convert_element_type x20 -> x0, other arithmetic: 18.1 us -> none  [the longest x2 14 us: local(): grad_scores = (probs_full * (grad_probs - balance)).astype(low_type)]
    slice x21 -> x0, local copies, waits for them, and re-layouts: 17.8 us -> none  [the longest x2 5.35 us: local(): projected[:, width:2 * width].reshape(frames, H, HD)]
  transfers between devices with their start and end apart: 16 -> 0, of which waited for: 8 -> 0; matrix products, arithmetic and copies ran while one was open for 25% -> 0% of each run, Pallas kernels for 0% -> 0%
where the time goes in v3:
time: 113 us
  Pallas kernels  112 us (99%)
    pallas_call x1, Pallas kernels, local_staged(): pl.pallas_call(functools.partial(layer_kernel, [name for name, _, _ in it...  109 us
    pallas_call x1, Pallas kernels, local_staged(): pl.pallas_call(write_kernel, out_shape=shapes + [jax.ShapeDtypeStruct((1,...  3.18 us

profile of v3, /device:TPU:0, one launch (start us, length us, event | category | flops | bytes accessed | tf_op | source)
XLA Modules:
  0.0 113.2 jit_solution(2058118719415019025)
XLA Ops:
  0.6 109.2 %shard_map.220 = (bf16[1,1024,512]{2,1,0:T(8,128)(2,1)}, bf16[1,1024,512]{2,1,0:T(8,128)(2,1)}, f32[32,768]{1,0:T(8,128)}, f32[32,256]{1,0:T(8,128)}, f32[32,102...) custom-call(bf16[1,1024,512]{2,1,0:T(8,128)(2,1)} %refs_0_.1, bf16[1,1024,512]{2,1,0:T(8,128)(2,1)} %refs_1_.1, ...), custom_call_target="tpu_custom_call" | custom-call | tf_op jit(solution)/shard_map/pallas_call | solution.py:1221
  109.8 3.2 %shard_map.221 = (bf16[1,1024,512]{2,1,0:T(8,128)(2,1)}, bf16[1,1024,512]{2,1,0:T(8,128)(2,1)}, f32[32,768]{1,0:T(8,128)}, f32[32,256]{1,0:T(8,128)}, f32[32,102...) custom-call(bf16[1,1024,512]{2,1,0:T(8,128)(2,1)} %get-tuple-element, ...), custom_call_target="tpu_custom_call" | custom-call | tf_op jit(solution)/shard_map/pallas_call | solution.py:1241

commit v4 on v3

--- a/solution.py
+++ b/solution.py
@@ -362,14 +362,21 @@
     }
     for k in (1, 2, 3):
         found[k] = (lax.rem(z + k, 4) * 4 + lax.rem(row, 4), core)
+    found["xy"] = (row + 3 - 2 * x - 4 * y, core)
+    for k in range(1, 16):
+        found["r", k] = (lax.rem(row + k, 16), core)
     return found
 
 
-def enter(peers):
-    barrier = pltpu.get_barrier_semaphore()
-    for peer in peers.values():
-        pl.semaphore_signal(barrier, inc=1, device_id=peer, device_id_type=MESH_IDS)
-    pl.semaphore_wait(barrier, len(peers))
+def greet(peers):
+    for name in ["s"] + [("r", k) for k in range(1, 16)]:
+        pl.semaphore_signal(
+            pltpu.get_barrier_semaphore(), inc=1, device_id=peers[name], device_id_type=MESH_IDS
+        )
+
+
+def be_greeted():
+    pl.semaphore_wait(pltpu.get_barrier_semaphore(), 16)
 
 
 class Links:
@@ -436,6 +443,74 @@
             (full.at[core, :, y, x], got[1]),
             (full.at[core, :, y], got[2]),
             (full.at[1 - core], got[3]),
+        )
+        self.sent = ((full.at[core, 0:3, y, x], near), (units.at[0:7, 0, 0], far))
+
+    def step(self, number):
+        if number > 0:
+            await_bytes(*self.waits[number])
+        for copy in self.starts[number]:
+            copy.start()
+
+    def drain(self):
+        for like, sem in self.sent:
+            await_bytes(like, sem)
+
+
+class GatherDirect:
+    def __init__(self, units, i, links, at):
+        full = units.at[i]
+        row, core, x, y, z = at
+        piece = full.at[core, z, y, x]
+        self.sent, self.got, passed, self.whole = [links.slot() for _ in range(4)]
+        self.starts = [
+            links.copy(piece, piece, ("r", k), self.sent, self.got) for k in range(1, 16)
+        ]
+        self.over = links.copy(full.at[core], full.at[core], "s", passed, self.whole)
+        self.fifteen = units.at[0:5, 0, 0:3, 0, 0]
+
+    def step(self, number):
+        if number == 0:
+            for copy in self.starts:
+                copy.start()
+        if number == 1:
+            await_bytes(self.fifteen, self.got)
+            self.over.start()
+        if number == 2:
+            self.over.wait_recv()
+
+    def drain(self):
+        await_bytes(self.fifteen, self.sent)
+        self.over.wait_send()
+
+
+class GatherPlane:
+    def __init__(self, units, i, links, at):
+        full = units.at[i]
+        row, core, x, y, z = at
+        every = slice(None)
+        near, far = links.slot(), links.slot()
+        got = [links.slot() for _ in range(3)]
+
+        def copy(where, peer, send, recv):
+            return links.copy(full.at[where], full.at[where], peer, send, recv)
+
+        column = (core, every, y, x)
+        self.starts = (
+            [copy((core, z, y, x), k, near, got[0]) for k in (1, 2, 3)],
+            [copy(column, peer, far, got[1]) for peer in ("xy", "x", "y")]
+            + [copy(column, "s", far, got[2])],
+            [
+                copy((core, every, y, 1 - x), "s", far, got[2]),
+                copy((core, every, 1 - y), "s", far, got[2]),
+            ],
+            [],
+        )
+        self.waits = (
+            None,
+            (full.at[core, 0:3, y, x], got[0]),
+            (units.at[0:3, 0, :, 0, 0], got[1]),
+            (full.at[1 - core], got[2]),
         )
         self.sent = ((full.at[core, 0:3, y, x], near), (units.at[0:7, 0, 0], far))
 
@@ -538,6 +613,44 @@
         await_bytes(self.units.at[0:5, 0:3, 0, 0], self.far)
 
 
+class ScatterDirect(Scatter):
+    def __init__(self, own, out, arrived, result, links, at, units):
+        self.own, self.out, self.result, self.at = own, out, result, at
+        self.s_in, self.pieces = arrived
+        row, core, x, y, z = at
+        self.rows = out.shape[3]
+        self.half = self.rows // 2
+        self.units = units
+        self.d = links.single(out, self.s_in, "s")
+        self.far, self.got = links.slot(), links.slot()
+        self.copies = []
+        for k in range(1, 16):
+            there = lax.rem(row + k, 16)
+            where = (lax.div(there, 4), lax.rem(lax.div(there, 2), 2), lax.rem(there, 2))
+            made = links.copy(out.at[where], self.pieces.at[k - 1], ("r", k), self.far, self.got)
+            self.copies.append((where, made))
+
+    def whole(self, z, y, x):
+        return jnp.concatenate([self.mine(z, y, x, part) for part in range(2)], axis=0)
+
+    def step(self, number):
+        row, core, x, y, z = self.at
+        if number == 0:
+            self.d.start()
+        if number == 1:
+            self.d.wait()
+            for where, copy in self.copies:
+                self.out[where] = self.whole(*where).astype(BF16)
+                copy.start()
+            self.own[: self.rows, :] = self.whole(z, y, x)
+        if number == 2:
+            await_bytes(self.pieces, self.got)
+            total = self.own[: self.rows, :]
+            for k in range(15):
+                total = total + self.pieces[k].astype(F32)
+            self.result(total)
+
+
 def gelu_and_slope(values):
     cdf = 0.5 + 0.5 * lax.erf(values * math.sqrt(0.5))
     bell = jnp.exp2((values * values) * (-0.5 * math.log2(math.e)))
@@ -549,9 +662,16 @@
 
 
 def turned(values, cosine, sine):
-    first = lane_pattern(values.shape, HD) < HD // 2
-    swapped = jnp.where(first, pltpu.roll(values, 96, 1), pltpu.roll(values, 32, 1))
-    return values * cosine + swapped * sine
+    return values * cosine + pltpu.roll(values, 64, 1) * sine
+
+
+def swap_middle(values):
+    group = lane_pattern((1, 128), 128) // 32
+    return jnp.where(
+        group == 1,
+        pltpu.roll(values, 96, 1),
+        jnp.where(group == 2, pltpu.roll(values, 32, 1), values),
+    )
 
 
 TILE = 256
@@ -561,7 +681,30 @@
 COLUMNS = 256
 UNITS = 12
 GROUP, OUT, DOWN, UP = 0, 3, (4, 6, 8, 10), (5, 7, 9, 11)
-OFFSETS = (0, 2, 4, 6, 7)
+D0, U0, D1, U1, D2, U2, D3, U3 = range(4, 12)
+DUE = {
+    "tables": ((1, 1),),
+    "masks": ((0, 1), (2, 1), (OUT, 0), (D0, 0), (0, 2)),
+    ("before", 0): ((OUT, 1), (U0, 0)),
+    ("during", 0): ((1, 2),),
+    ("after", 0): ((1, 3), (D0, 1), (D1, 0)),
+    ("before", 1): ((2, 2), (OUT, 2), (U0, 1), (U1, 0)),
+    ("after", 1): ((2, 3), (D0, 2), (D1, 1), (D2, 0)),
+    ("before", 2): ((OUT, 3), (U0, 2), (U1, 1), (U2, 0)),
+    ("after", 2): ((OUT, 4), (D0, 3), (D1, 2), (D2, 1), (D3, 0)),
+    ("after", 3): ((D0, 4), (U0, 3), (U1, 2), (U2, 1), (U3, 0)),
+    ("norm", 2): ((D2, 2),),
+    ("feed", 0, 0): ((U0, 4), (D1, 3), (D3, 1)),
+    ("feed", 0, 1): ((D1, 4), (U1, 3), (U2, 2), (U3, 1)),
+    ("feed", 0, 2): ((D2, 3), (D3, 2)),
+    ("feed", 1, 0): ((U1, 4), (D2, 4)),
+    ("feed", 1, 1): ((U2, 3), (U3, 2)),
+    ("feed", 1, 2): ((D3, 3), (U2, 4)),
+    ("feed", 2, 0): ((D3, 4),),
+    ("feed", 2, 1): ((U3, 3),),
+    ("feed", 2, 2): ((U3, 4),),
+}
+LAST = 2
 CHUNKS = (
     (((0, 0), (1, 0)), ((2, 0), (2, 1))),
     (((0, 1), (1, 1)), ((2, 2), (1, 2))),
@@ -614,7 +757,15 @@
     unit = (4, 2, 2, width // 16, COLUMNS)
     half = width // 32
     return [
+        ("x", (frames, width), BF16),
+        ("dy", (frames, width), BF16),
+        ("y", (frames, width), BF16),
+        ("mixed", (frames, width), BF16),
+        ("wo", (width // 16, width // 2), F32),
+        ("wu", (width // 16, 2 * width), F32),
+        ("wd", (width // 4, width // 2), F32),
         ("w", (UNITS, 2) + unit, BF16),
+        ("pos", (8, frames), F32),
         ("vecs", (2, 8, width // 2), F32),
         ("segs", (2, 8, frames), F32),
         ("n1t", (width, frames), BF16),
@@ -643,32 +794,47 @@
         ("h_out", (PAIRS, 2, REACH, 128), BF16),
         ("h_in", (PAIRS, 2, REACH, 128), BF16),
         ("acc", (8, width), F32),
-        ("v_out", (3, 8, width // 2), F32),
-        ("v_in", (3, 8, width // 2), F32),
-        ("v_z", (4, 8, width // 2), F32),
+        ("v_out", (8, width // 2), F32),
+        ("v_in", (8, width // 2), F32),
+        ("v_all", (16, 8, width // 2), F32),
+        ("pieces", (15, width // 16, COLUMNS), BF16),
         ("own", (UNITS - 3, width, COLUMNS), F32),
         ("up_sums", (4, width // 16, COLUMNS), F32),
         ("s_in", (UNITS,) + unit, BF16),
-        ("c_in", (UNITS, 2, 4, 2, half, COLUMNS), BF16),
-        ("b_in", (UNITS, 2, 4, half, COLUMNS), BF16),
-        ("a_in", (UNITS, 3, width // 16, COLUMNS), BF16),
+        ("c_in", (UNITS - 1, 2, 4, 2, half, COLUMNS), BF16),
+        ("b_in", (UNITS - 1, 2, 4, half, COLUMNS), BF16),
+        ("a_in", (UNITS - 1, 3, width // 16, COLUMNS), BF16),
     ]
 
 
-SLOTS = 12 * UNITS + 2 * (2 + 2 * PAIRS + PAIRS + 3) + 4
+SLOTS = 12 * UNITS + 2 * (2 + 2 * PAIRS + PAIRS) + 4
 
 
 def layer_kernel(names, *refs):
-    x_ref, dy_ref, seg_ref = refs[:3]
-    wq_shard, wo_shard, wu_shard, wd_shard = refs[3:7]
+    seg_ref, wq_shard = refs[2:4]
     vectors = refs[7:13]
-    y_ref, ig_ref, gq, go, gu, gd, gv = refs[13:20]
-    m = dict(zip(names, refs[20:-1]))
+    y_out, ig_out, gq, go, gu, gd, gv = refs[13:20]
+    m = dict(zip(names, refs[20:-2]))
+    x_ref, dy_ref, y_ref, mixed = m["x"], m["dy"], m["y"], m["mixed"]
+    wo_shard, wu_shard, wd_shard = m["wo"], m["wu"], m["wd"]
+    moves = refs[-2]
+    loads = [
+        pltpu.make_async_copy(source, target, moves.at[i])
+        for i, (source, target) in enumerate(
+            (
+                (refs[0].at[0], x_ref),
+                (refs[4], wo_shard),
+                (refs[5], wu_shard),
+                (refs[6], wd_shard),
+                (refs[1].at[0], dy_ref),
+            )
+        )
+    ]
     at = coordinates()
     row, core, x, y, z = at
     peers = peers_of(at)
     links = Links(refs[-1], peers)
-    frames, width = x_ref.shape[1:]
+    frames, width = x_ref.shape
     piece = width // 16
     blocks, tiles = frames // BLOCK, frames // TILE
     factor = 1.0 / math.sqrt(HD)
@@ -683,30 +849,45 @@
         begin = offsets[0] + core * (offsets[1] - offsets[0])
         return pl.ds(pl.multiple_of(begin, 128), 128)
 
+    def ordered(g, j, value):
+        kinds = [CHUNKS[g][c][j][0] for c in range(2)]
+        if kinds == [2, 2]:
+            return value
+        swapped = swap_middle(value)
+        if 2 not in kinds:
+            return swapped
+        return jnp.where(core == kinds.index(2), value, swapped)
+
+    greet(peers)
+    for load in loads:
+        load.start()
     for g in range(3):
         for j in range(2):
-            w[g, core, z, y, x, :, j * 128 : (j + 1) * 128] = wq_shard[
-                :, chunk_columns(g, j)
-            ].astype(BF16)
+            w[g, core, z, y, x, :, j * 128 : (j + 1) * 128] = ordered(
+                g, j, wq_shard[:, chunk_columns(g, j)]
+            ).astype(BF16)
     m["vecs"][core] = jnp.concatenate(
         [v[...].astype(BF16).astype(F32) for v in vectors]
         + [jnp.zeros((2, width // 2), F32)],
         axis=0,
     )
     m["segs"][core] = jnp.broadcast_to(seg_ref[...].astype(F32), (8, frames))
-    enter(peers)
+    be_greeted()
     vec_copy = links.single(m["vecs"].at[core], m["vecs"].at[core], "s")
     seg_copy = links.single(m["segs"].at[core], m["segs"].at[core], "s")
-    gathers = [Gather(w, i, links, at) for i in range(UNITS)]
-
-    def tick(k):
-        for step in (4, 3, 2, 1, 0):
-            if 0 <= k - OFFSETS[step] < UNITS:
-                gathers[k - OFFSETS[step]].step(step)
+    kinds = [GatherDirect, GatherPlane, GatherPlane] + [Gather] * (UNITS - 3)
+    gathers = [kind(w, i, links, at) for i, kind in enumerate(kinds)]
+
+    def due(*where):
+        for i, step in DUE.get(where if len(where) > 1 else where[0], ()):
+            gathers[i].step(step)
 
     vec_copy.start()
     seg_copy.start()
-    tick(0)
+    for i in (1, 0, 2):
+        gathers[i].step(0)
+    for load in loads:
+        load.wait()
     w[OUT, core, z, y, x] = wo_shard[...].astype(BF16)
     for q in range(4):
         w[DOWN[q], core, z, y, x] = wd_shard[q * piece : (q + 1) * piece, :].astype(BF16)
@@ -733,55 +914,73 @@
 
     def norm_one(t, _):
         rows = start_of(t, TILE)
-        unit, _scale = normalized(x_ref[0, rows, :].astype(F32))
+        unit, _scale = normalized(x_ref[rows, :].astype(F32))
         low = (unit * gain_one + bias_one).astype(BF16)
-        n1[0, rows, :] = low
+        n1[rows, :] = low
         m["n1t"][:, rows] = low.T
 
-    tick(1)
     run(0, tiles, norm_one)
-    tick(2)
 
     seg_copy.wait_recv()
     segs = m["segs"]
+    index = lax.broadcasted_iota(jnp.int32, (8, frames), 1)
+    order = index.astype(F32)
+
+    def starts_in(which):
+        line = segs[which]
+        change = (line != pltpu.roll(line, 1, 1)) | (index == 0)
+        begun = jnp.where(change, order, 0.0)
+        reach = 1
+        while reach < frames:
+            begun = jnp.maximum(begun, jnp.where(index >= reach, pltpu.roll(begun, reach, 1), 0.0))
+            reach *= 2
+        return begun
+
+    running = (core > 0) & (segs[core] == segs[other][:, frames - 1 :])
+    before = starts_in(other)[:, frames - 1 :]
+    m["pos"][...] = order - jnp.where(
+        running, before - (core * frames).astype(F32), starts_in(core)
+    )
+    seg_blocks = m["own"]
+
+    def across(line):
+        return jnp.broadcast_to(line, (BLOCK, BLOCK)).T
 
     def spread(which, begin):
-        line = segs[which, 0:1, pl.ds(pl.multiple_of(begin, BLOCK), BLOCK)]
-        return jnp.broadcast_to(line, (BLOCK, BLOCK)).T
-
-    seg_blocks = m["own"]
+        return across(segs[which, 0:1, begin : begin + BLOCK])
 
     def seg_place(e):
         return (e // 8, pl.ds((e % 8) // 2 * BLOCK, BLOCK), pl.ds(e % 2 * BLOCK, BLOCK))
+
+    group = lane_pattern((1, 128), 128) // 32
+    lanes = lane_pattern((1, 128), HD // 2).astype(F32)
+    frequency = jnp.exp(lanes * (-2.0 * math.log(10000.0) / HD))
+    near_half = lane_pattern((1, 128), 128) < HD
+    quarter = frames // 4
+    for i in range(quarter // BLOCK):
+        position = across(m["pos"][0:1, i * BLOCK : (i + 1) * BLOCK])
+        for a in range(1, 4):
+            begin = a * quarter + i * BLOCK
+            position = jnp.where(
+                group == a, across(m["pos"][0:1, begin : begin + BLOCK]), position
+            )
+        angle = position * frequency
+        for name, table in (("cos", jnp.cos(angle)), ("sin", jnp.sin(angle))):
+            for a in range(4):
+                begin = a * quarter + i * BLOCK
+                wide = jnp.where(group == a, table, 0.0)
+                wide = wide + pltpu.roll(wide, 32, 1)
+                wide = wide + pltpu.roll(wide, 64, 1)
+                if name == "sin":
+                    wide = jnp.where(near_half, -wide, wide)
+                m[name][begin : begin + BLOCK, :] = wide
 
     for e in range(REACH // BLOCK):
         halo = spread(other, frames - REACH + e * BLOCK)
         seg_blocks[seg_place(e)] = jnp.where(core > 0, halo, -1.0)
-
-    lanes = lane_pattern((1, 128), HD // 2).astype(F32)
-    frequency = jnp.exp(lanes * (-2.0 * math.log(10000.0) / HD))
-    first_half = lane_pattern((BLOCK, 128), HD) < HD // 2
-
-    def tables(b, _):
-        rows = start_of(b, BLOCK)
-        here = spread(core, b * BLOCK)
-        count = jnp.zeros((BLOCK, BLOCK), F32)
-        for which in range(2):
-            for k in range(blocks):
-                line = segs[which, 0:1, k * BLOCK : (k + 1) * BLOCK]
-                count = count + jnp.where(line < here, 1.0, 0.0)
-        began = jnp.sum(count, axis=1, keepdims=True)
-        frame = lax.broadcasted_iota(jnp.int32, (BLOCK, 1), 0) + (core * frames + b * BLOCK)
-        angle = (frame.astype(F32) - began) * frequency
-        m["cos"][rows, :] = jnp.cos(angle)
-        sine = jnp.sin(angle)
-        m["sin"][rows, :] = jnp.where(first_half, -sine, sine)
-
-    run(0, blocks, tables, {blocks // 2: [lambda: tick(3)]})
-    tick(4)
-
     for b in range(blocks):
         seg_blocks[seg_place(REACH // BLOCK + b)] = spread(core, b * BLOCK)
+    due("tables")
     distance = (
         lax.broadcasted_iota(jnp.int32, (SPAN, BLOCK), 1)
         - lax.broadcasted_iota(jnp.int32, (SPAN, BLOCK), 0)
@@ -792,22 +991,20 @@
         keys = jnp.concatenate([seg_blocks[seg_place(b + i)] for i in range(SPAN // BLOCK)], axis=0)
         line = segs[core, 0:1, b * BLOCK : (b + 1) * BLOCK]
         m["bias"][b] = jnp.where(near & (keys == line), 0.0, NEGATIVE).astype(BF16)
-    for k in (5, 6, 7):
-        tick(k)
-
-    low_lanes = lane_pattern((1, 128), 128) < HD
-
-    def two_heads(value):
+    due("masks")
+
+    def two_heads(value, swapped=False):
+        first = lax.rem(group, 2) == 0 if swapped else group < 2
         zero = jnp.zeros_like(value)
         return jnp.concatenate(
-            [jnp.where(low_lanes, value, zero), jnp.where(low_lanes, zero, value)], axis=0
+            [jnp.where(first, value, zero), jnp.where(first, zero, value)], axis=0
         )
 
     def projection(g):
         def project(t, _):
             rows = start_of(t, TILE)
             placed = pl.ds(pl.multiple_of(REACH + t * TILE, TILE), TILE)
-            left = n1[0, rows, :]
+            left = n1[rows, :]
             cosine, sine = m["cos"][rows, :], m["sin"][rows, :]
             for c in range(2):
                 wide = dot(left, w[g, c].reshape(width, COLUMNS))
@@ -829,10 +1026,16 @@
         return project
 
     tail, head = pl.ds(frames, REACH), pl.ds(0, REACH)
-    mixed = ig_ref
-
-    def heads_joined(both):
-        return jnp.concatenate([both[:HD, :BLOCK], both[HD:, BLOCK:]], axis=0)
+
+    def heads_joined(both, swapped=False):
+        step = HD // 2 if swapped else HD
+        return jnp.concatenate(
+            [
+                both[i : i + step, i // step % 2 * BLOCK : (i // step % 2 + 1) * BLOCK]
+                for i in range(0, 2 * HD, step)
+            ],
+            axis=0,
+        )
 
     unit_rows = lax.broadcasted_iota(jnp.int32, (2 * BLOCK, BLOCK), 0)
     unit_lanes = lax.broadcasted_iota(jnp.int32, (2 * BLOCK, BLOCK), 1)
@@ -853,7 +1056,7 @@
     def attend(p, events):
         def score(b):
             left = jnp.concatenate([m["kx"][p, block_window(b), :], m["bias"][b]], axis=1)
-            right = jnp.concatenate([two_heads(m["qx"][p, block_rows(b), :]), picks], axis=1)
+            right = jnp.concatenate([two_heads(m["qx"][p, block_rows(b), :], True), picks], axis=1)
             spare(b % 4)[...] = dot_t(left, right)
 
         def soften(b):
@@ -866,7 +1069,7 @@
         def mix(b):
             joined = heads_joined(dot(m["vt"][p, :, block_window(b)], m["probs"][p, b]))
             m["ot"][p * 128 : (p + 1) * 128, block_rows(b)] = joined.astype(BF16)
-            mixed[0, block_rows(b), p * 128 : (p + 1) * 128] = joined.T.astype(BF16)
+            mixed[block_rows(b), p * 128 : (p + 1) * 128] = joined.T.astype(BF16)
 
         in_turn(blocks, (score, soften, mix), events)
 
@@ -890,11 +1093,9 @@
                     if kind > 0:
                         send_halo(kind, q)
         take_halo(p)
-        due = {
-            2: [functools.partial(tick, 8 + 2 * p)],
-            6: [functools.partial(tick, 9 + 2 * p)],
-        }
-        attend(p, due)
+        due("before", p)
+        attend(p, {7: [functools.partial(due, "during", p)]} if p == 0 else {})
+        due("after", p)
 
     m["acc"][...] = jnp.zeros_like(m["acc"])
     acc = m["acc"]
@@ -916,28 +1117,30 @@
 
     def norm_two(t, _):
         rows = start_of(t, TILE)
-        both = mixed[0, rows, :]
+        both = mixed[rows, :]
         branch = jnp.concatenate(
             [dot(both, w[OUT, c].reshape(width, COLUMNS)) for c in range(2)], axis=1
         )
         m["branch"][rows, :] = branch.astype(BF16)
-        after = x_ref[0, rows, :].astype(F32) + scale_one * branch
+        after = x_ref[rows, :].astype(F32) + scale_one * branch
         m["after"][rows, :] = after
         unit, _scale = normalized(after)
         low = (unit * gain_two + bias_two).astype(BF16)
-        n2[0, rows, :] = low
+        n2[rows, :] = low
         m["n2t"][:, rows] = low.T
-        dbm = (dy_ref[0, rows, :].astype(F32) * scale_two).astype(BF16)
+        dbm = (dy_ref[rows, :].astype(F32) * scale_two).astype(BF16)
         dba[0, rows, :] = dbm[:, : width // 2]
         dba[1, rows, :] = dbm[:, width // 2 :]
 
-    run(0, tiles, norm_two)
+    run(0, tiles, norm_two, {2: [functools.partial(due, "norm", 2)]})
 
     def result_of(i):
         def keep(value):
             if i < OUT:
                 for j in range(2):
-                    gq[:, chunk_columns(i, j)] = value[:, j * 128 : (j + 1) * 128]
+                    gq[:, chunk_columns(i, j)] = ordered(
+                        i, j, value[:, j * 128 : (j + 1) * 128]
+                    )
             elif i == OUT:
                 go[...] = value
             elif i in DOWN:
@@ -956,8 +1159,13 @@
             sums[DOWN[i]].drain()
         place = DOWN[i] if i < OUT else i
         out, own = w.at[place, 0], m["own"].at[place - 3]
-        arrived = [m[name].at[i] for name in ("s_in", "c_in", "b_in", "a_in")]
-        sums[i] = Scatter(own, out, arrived, result_of(i), links, at, m["s_in"])
+        if i == LAST:
+            arrived, kind = [m["s_in"].at[i], m["pieces"]], ScatterDirect
+        else:
+            at_unit = i - (i > LAST)
+            arrived = [m["s_in"].at[i]] + [m[n].at[at_unit] for n in ("c_in", "b_in", "a_in")]
+            kind = Scatter
+        sums[i] = kind(own, out, arrived, result_of(i), links, at, m["s_in"])
         own[...] = dot(left[...], right[core])
         out[...] = dot(left[...], right[other]).astype(BF16).reshape(4, 2, 2, piece, COLUMNS)
         sums[i].step(0)
@@ -966,13 +1174,17 @@
         return lambda: sums[i].step(number)
 
     def feed(q):
-        def middle(t, _):
+        def middle(pair, _):
+            for t in range(2):
+                one(2 * pair + t)
+
+        def one(t):
             rows = start_of(t, TILE)
             ups = [w[UP[q], h].reshape(width, COLUMNS) for h in range(2)]
             dbm = jnp.concatenate([dba[c, rows, :] for c in range(2)], axis=1)
             acts, dus = [], []
             for h in range(2):
-                value, slope = gelu_and_slope(dot(n2[0, rows, :], ups[h]))
+                value, slope = gelu_and_slope(dot(n2[rows, :], ups[h]))
                 act = value.astype(BF16)
                 m["actt"][h * COLUMNS : (h + 1) * COLUMNS, rows] = act.T
                 down = jnp.concatenate(
@@ -1005,29 +1217,22 @@
             action()
 
     for q in range(4):
-        events = {i: [] for i in range(tiles)}
-        if q == 0:
-            events[1] += [functools.partial(tick, 16)]
-            events[3] += [functools.partial(tick, 17)]
-        if q == 1:
-            events[2] += [functools.partial(tick, 18)]
+        due("feed", q, 0)
+        events = {1: [functools.partial(due, "feed", q, 1)]}
         if q > 0:
             events[1] += steps_of(q - 1, 1)
+        run(0, tiles // 2, feed(q), events)
+        due("feed", q, 2)
         if q > 1:
-            events[0] += steps_of(q - 2, 2)
-        if q > 2:
-            events[2] += steps_of(q - 3, 4)
-        run(0, tiles, feed(q), events)
-        if q > 1:
-            do(steps_of(q - 2, 3))
+            do(steps_of(q - 2, 2))
         unit_grads(DOWN[q], m["actt"], dba)
         unit_grads(UP[q], m["n2t"], m["du"])
 
     def norm_two_back(t, _):
         rows = start_of(t, TILE)
         after, branch_two = m["after"][rows, :], m["branch_two"][rows, :]
-        y_ref[0, rows, :] = (after + scale_two * branch_two).astype(BF16)
-        upstream = dy_ref[0, rows, :].astype(F32)
+        y_ref[rows, :] = (after + scale_two * branch_two).astype(BF16)
+        upstream = dy_ref[rows, :].astype(F32)
         add_to(5, upstream * branch_two)
         unit, scale = normalized(after)
         grad = m["dx1"][rows, :]
@@ -1048,20 +1253,31 @@
         for p in range(PAIRS):
             m["dox"][p, rows, :] = dmixed[:, p * 128 : (p + 1) * 128]
 
+    do(steps_of(0, 3))
     run(
         0,
         tiles,
         norm_two_back,
-        {0: steps_of(2, 2), 1: steps_of(3, 1)},
-    )
+        {2: steps_of(3, 1)},
+    )
+    y_send = pltpu.make_async_copy(y_ref, y_out.at[0], moves.at[5])
+    y_send.start()
+    do(steps_of(2, 2))
     unit_grads(OUT, m["ot"], dba)
+    do(steps_of(1, 3))
 
     dp = m["dp"]
-    plan = [
-        {2: steps_of(2, 3) + [step_of(OUT, 1)], 4: steps_of(3, 2) + steps_of(1, 4)},
-        {2: [step_of(OUT, 2)], 4: steps_of(3, 3), 6: steps_of(2, 4), 7: [step_of(OUT, 3)]},
-        {2: [step_of(GROUP, 1)], 4: steps_of(3, 4), 6: [step_of(OUT, 4)]},
-        {0: [step_of(GROUP, 2)], 2: [step_of(GROUP + 1, 1)], 5: [step_of(GROUP, 3)]},
+    halfway = [
+        [step_of(OUT, 1)],
+        steps_of(2, 3) + steps_of(3, 2),
+        [step_of(GROUP, 1)],
+        [step_of(GROUP + 1, 1)],
+    ]
+    after_pair = [
+        steps_of(0, 4),
+        steps_of(1, 4) + [step_of(OUT, 2)],
+        steps_of(2, 4) + steps_of(3, 3) + [step_of(OUT, 3)],
+        [step_of(GROUP, 2)],
     ]
 
     def store_turned(kind, p, rows, value):
@@ -1100,8 +1316,8 @@
             dvx[window, :] = dvx[window, :] + dot(
                 m["probs"][p, b], two_heads(m["dox"][p, rows, :])
             )
-            dkx[window, :] = dkx[window, :] + dot(dscores, two_heads(m["qx"][p, rows, :]))
-            joined = heads_joined(dot(m["kt"][p, :, window], dscores)).T * factor
+            dkx[window, :] = dkx[window, :] + dot(dscores, two_heads(m["qx"][p, rows, :], True))
+            joined = heads_joined(dot(m["kt"][p, :, window], dscores), True).T * factor
             store_turned(0, p, rows, joined)
 
         h_out, h_in = m["h_out"], m["h_in"]
@@ -1113,8 +1329,7 @@
             h_out[p, 1] = dvx[0:REACH, :].astype(BF16)
             halo_back.start()
 
-        events = dict(plan[p])
-        events[4] = [send_back] + events.get(4, [])
+        events = {4: [send_back] + halfway[p]}
         in_turn(blocks, (probe, weigh, gather_back), events)
         halo_back.wait_recv()
         dkx[tail, :] = dkx[tail, :] + h_in[p, 0].astype(F32)
@@ -1127,10 +1342,10 @@
             store_turned(2, p, rows, dvx[placed, :])
 
         run(0, tiles, finish)
+        do(after_pair[p])
         if p > 0:
             unit_grads(GROUP + p - 1, m["n1t"], dp.at[p - 1])
 
-    sums[GROUP + 1].step(2)
 
     def first(t, _):
         rows = start_of(t, TILE)
@@ -1139,55 +1354,51 @@
             jnp.concatenate([dp[g, c, rows, :] for g, c in sides], axis=1),
             jnp.concatenate([w[g, c].reshape(width, COLUMNS) for g, c in sides], axis=1),
         )
-        unit, scale = normalized(x_ref[0, rows, :].astype(F32))
+        unit, scale = normalized(x_ref[rows, :].astype(F32))
         add_to(0, grad * unit)
         add_to(1, grad)
-        ig_ref[0, rows, :] = (
+        mixed[rows, :] = (
             m["dx1"][rows, :] + norm_back(unit, scale, gain_one, grad)
         ).astype(BF16)
 
-    run(
-        0,
-        tiles,
-        first,
-        {1: [step_of(GROUP + 2, 1)], 3: [step_of(GROUP, 4)]},
-    )
-
-    v_out, v_in, v_z = m["v_out"], m["v_in"], m["v_z"]
-    here, there = start_of(core, width // 2), start_of(other, width // 2)
-    v_out[0] = acc[:, there]
-    hops = [links.single(v_out.at[i], v_in.at[i], peer) for i, peer in enumerate(("s", "y", "x"))]
-    hops[0].start()
-    hops[0].wait_recv()
-    v_out[1] = acc[:, here] + v_in[0]
-    hops[1].start()
-    sums[GROUP + 2].step(2)
-    sums[GROUP + 1].step(3)
+    late = {1: [step_of(LAST, 1)], 3: [*steps_of(3, 4), step_of(OUT, 4), step_of(GROUP + 1, 2)]}
+    run(0, tiles, first, late)
+    sends = [pltpu.make_async_copy(mixed, ig_out.at[0], moves.at[6])]
+    sends[0].start()
+
+    v_out, v_in, v_all = m["v_out"], m["v_in"], m["v_all"]
+    v_out[...] = acc[:, start_of(other, width // 2)]
+    vector_hop = links.single(v_out, v_in, "s")
+    vector_hop.start()
+    sums[GROUP].step(3)
+    vector_hop.wait_recv()
+    v_all[row] = acc[:, start_of(core, width // 2)] + v_in[...]
+    spread_send, spread_recv = links.slot(), links.slot()
+    for k in range(1, 16):
+        links.copy(v_all.at[row], v_all.at[row], ("r", k), spread_send, spread_recv).start()
     for j in range(2):
         for a in range(4):
             gu[:, (4 * j + a) * 128 : (4 * j + a + 1) * 128] = regroup(
                 [m["up_sums"][q, :, j * 128 : (j + 1) * 128] for q in range(4)], a, True
             )
-    hops[1].wait_recv()
-    v_out[2] = v_out[1] + v_in[1]
-    hops[2].start()
-    sums[GROUP + 2].step(3)
-    hops[2].wait_recv()
-    v_z[z] = v_out[2] + v_in[2]
-    spread_send, spread_recv = links.slot(), links.slot()
-    spreads = [links.copy(v_z.at[z], v_z.at[z], k, spread_send, spread_recv) for k in (1, 2, 3)]
-    for each in spreads:
-        each.start()
+    sums[GROUP + 1].step(3)
+    sums[GROUP].step(4)
+    await_bytes(v_all.at[0:15], spread_recv)
+    total = v_all[0]
+    for r in range(1, 16):
+        total = total + v_all[r]
+    gv[...] = total
+    sums[LAST].step(2)
     sums[GROUP + 1].step(4)
-    sums[GROUP + 2].step(4)
-    await_bytes(v_z.at[0:3], spread_recv)
-    gv[...] = (v_z[0] + v_z[1]) + (v_z[2] + v_z[3])
-    await_bytes(v_z.at[0:3], spread_send)
+    await_bytes(v_all.at[0:15], spread_send)
     for i, each in sums.items():
         if i not in DOWN[:3]:
             each.drain()
-    for each in [vec_copy, seg_copy, *halos.values(), *backs, *hops]:
+    for each in [vec_copy, seg_copy, *halos.values(), *backs, vector_hop]:
         each.wait_send()
+    y_send.wait()
+    for each in sends:
+        each.wait()
 
 
 def write_kernel(*refs):
@@ -1210,6 +1421,7 @@
     frames, width = inputs.shape[1:]
     items = scratch_list(frames, width)
     whole = pl.BlockSpec(memory_space=pltpu.VMEM)
+    anywhere = pl.BlockSpec(memory_space=pl.ANY)
     shapes = [
         jax.ShapeDtypeStruct(inputs.shape, BF16),
         jax.ShapeDtypeStruct(inputs.shape, BF16),
@@ -1221,10 +1433,10 @@
     results = pl.pallas_call(
         functools.partial(layer_kernel, [name for name, _, _ in items]),
         out_shape=shapes + [jax.ShapeDtypeStruct((8, width // 2), F32)],
-        in_specs=[whole] * 13,
-        out_specs=[whole] * 7,
+        in_specs=[anywhere] * 2 + [whole] * 2 + [anywhere] * 3 + [whole] * 6,
+        out_specs=[anywhere] * 2 + [whole] * 5,
         scratch_shapes=[pltpu.VMEM(shape, kind) for _, shape, kind in items]
-        + [pltpu.SemaphoreType.DMA((SLOTS,))],
+        + [pltpu.SemaphoreType.DMA((7,)), pltpu.SemaphoreType.DMA((SLOTS,))],
         compiler_params=pltpu.CompilerParams(
             collective_id=0, has_side_effects=True, vmem_limit_bytes=VMEM_LIMIT
         ),

time: 113 us -> 97.2 us (0.86)
  Pallas kernels: 112 us -> 96.2 us
    pallas_call x1, Pallas kernels: 109 us -> 93 us  [local_staged(): pl.pallas_call(functools.partial(layer_kernel, [name for name, _, _ in it...]
where the time goes in v4:
time: 97.2 us; the launch traced here: 97 us
  Pallas kernels  96.2 us (99%)
    pallas_call x1, Pallas kernels, local_staged(): pl.pallas_call(functools.partial(layer_kernel, [name for name, _, _ in it...  93 us
    pallas_call x1, Pallas kernels, local_staged(): pl.pallas_call(write_kernel, out_shape=shapes + [jax.ShapeDtypeStruct((1,...  3.18 us

profile of v4, /device:TPU:0, one launch (start us, length us, event | category | flops | bytes accessed | tf_op | source)
XLA Modules:
  0.0 97.0 jit_solution(16938497017590831028)
XLA Ops:
  0.6 93.0 %shard_map.220 = (bf16[1,1024,512]{2,1,0:T(8,128)(2,1)}, bf16[1,1024,512]{2,1,0:T(8,128)(2,1)}, f32[32,768]{1,0:T(8,128)}, f32[32,256]{1,0:T(8,128)}, f32[32,102...) custom-call(bf16[1,1024,512]{2,1,0:T(8,128)(2,1)} %refs_0_.1, bf16[1,1024,512]{2,1,0:T(8,128)(2,1)} %refs_1_.1, ...), custom_call_target="tpu_custom_call" | custom-call | tf_op jit(solution)/shard_map/pallas_call | solution.py:1433
  93.6 3.2 %shard_map.221 = (bf16[1,1024,512]{2,1,0:T(8,128)(2,1)}, bf16[1,1024,512]{2,1,0:T(8,128)(2,1)}, f32[32,768]{1,0:T(8,128)}, f32[32,256]{1,0:T(8,128)}, f32[32,102...) custom-call(bf16[1,1024,512]{2,1,0:T(8,128)(2,1)} %get-tuple-element, ...), custom_call_target="tpu_custom_call" | custom-call | tf_op jit(solution)/shard_map/pallas_call | solution.py:1453

commit v5 on v4

--- a/solution.py
+++ b/solution.py
@@ -734,13 +734,21 @@
     lax.fori_loop(begin, end, with_events, 0)
 
 
-def in_turn(count, stages, events):
-    for i in range(count + len(stages) - 1):
+def in_turn(items, stages, events):
+    for i in range(len(items) + len(stages) - 1):
         for action in events.get(i, []):
             action()
         for late, stage in enumerate(stages):
-            if 0 <= i - late < count:
-                stage(i - late)
+            if 0 <= i - late < len(items):
+                stage(items[i - late])
+
+
+def in_pairs(body):
+    def both(i, carried):
+        body(2 * i, carried)
+        body(2 * i + 1, carried)
+
+    return both
 
 
 def regroup(tiles, quarter, back=False):
@@ -884,7 +892,7 @@
 
     vec_copy.start()
     seg_copy.start()
-    for i in (1, 0, 2):
+    for i in (0, 1, 2):
         gathers[i].step(0)
     for load in loads:
         load.wait()
@@ -1071,7 +1079,7 @@
             m["ot"][p * 128 : (p + 1) * 128, block_rows(b)] = joined.astype(BF16)
             mixed[block_rows(b), p * 128 : (p + 1) * 128] = joined.T.astype(BF16)
 
-        in_turn(blocks, (score, soften, mix), events)
+        in_turn([*range(2, blocks), 0, 1], (score, soften, mix), events)
 
     halos = {}
 
@@ -1087,14 +1095,18 @@
 
     for p in range(PAIRS):
         if p < 3:
-            run(0, tiles, projection(p))
+            run(0, tiles // 2, in_pairs(projection(p)))
             for pair in CHUNKS[p]:
                 for kind, q in pair:
                     if kind > 0:
                         send_halo(kind, q)
-        take_halo(p)
         due("before", p)
-        attend(p, {7: [functools.partial(due, "during", p)]} if p == 0 else {})
+        take = functools.partial(take_halo, p)
+        if p < 2:
+            attend(p, {blocks - 2: [functools.partial(due, "during", p), take]})
+        else:
+            take()
+            attend(p, {})
         due("after", p)
 
     m["acc"][...] = jnp.zeros_like(m["acc"])
@@ -1132,7 +1144,7 @@
         dba[0, rows, :] = dbm[:, : width // 2]
         dba[1, rows, :] = dbm[:, width // 2 :]
 
-    run(0, tiles, norm_two, {2: [functools.partial(due, "norm", 2)]})
+    run(0, tiles // 2, in_pairs(norm_two), {1: [functools.partial(due, "norm", 2)]})
 
     def result_of(i):
         def keep(value):
@@ -1256,9 +1268,9 @@
     do(steps_of(0, 3))
     run(
         0,
-        tiles,
-        norm_two_back,
-        {2: steps_of(3, 1)},
+        tiles // 2,
+        in_pairs(norm_two_back),
+        {1: steps_of(3, 1)},
     )
     y_send = pltpu.make_async_copy(y_ref, y_out.at[0], moves.at[5])
     y_send.start()
@@ -1330,7 +1342,7 @@
             halo_back.start()
 
         events = {4: [send_back] + halfway[p]}
-        in_turn(blocks, (probe, weigh, gather_back), events)
+        in_turn(range(blocks), (probe, weigh, gather_back), events)
         halo_back.wait_recv()
         dkx[tail, :] = dkx[tail, :] + h_in[p, 0].astype(F32)
         dvx[tail, :] = dvx[tail, :] + h_in[p, 1].astype(F32)

time: 97.2 us -> 94.7 us (0.974)
  Pallas kernels: 96.2 us -> 93.7 us
    pallas_call x1, Pallas kernels: 93 us -> 90.5 us  [local_staged(): pl.pallas_call(functools.partial(layer_kernel, [name for name, _, _ in it...]
where the time goes in v5:
time: 94.7 us; the launch traced here: 94.5 us
  Pallas kernels  93.7 us (99%)
    pallas_call x1, Pallas kernels, local_staged(): pl.pallas_call(functools.partial(layer_kernel, [name for name, _, _ in it...  90.5 us
    pallas_call x1, Pallas kernels, local_staged(): pl.pallas_call(write_kernel, out_shape=shapes + [jax.ShapeDtypeStruct((1,...  3.18 us

profile of v5, /device:TPU:0, one launch (start us, length us, event | category | flops | bytes accessed | tf_op | source)
XLA Modules:
  0.0 94.5 jit_solution(12035259042868778666)
XLA Ops:
  0.6 90.5 %shard_map.220 = (bf16[1,1024,512]{2,1,0:T(8,128)(2,1)}, bf16[1,1024,512]{2,1,0:T(8,128)(2,1)}, f32[32,768]{1,0:T(8,128)}, f32[32,256]{1,0:T(8,128)}, f32[32,102...) custom-call(bf16[1,1024,512]{2,1,0:T(8,128)(2,1)} %refs_0_.1, bf16[1,1024,512]{2,1,0:T(8,128)(2,1)} %refs_1_.1, ...), custom_call_target="tpu_custom_call" | custom-call | tf_op jit(solution)/shard_map/pallas_call | solution.py:1445
  91.2 3.2 %shard_map.221 = (bf16[1,1024,512]{2,1,0:T(8,128)(2,1)}, bf16[1,1024,512]{2,1,0:T(8,128)(2,1)}, f32[32,768]{1,0:T(8,128)}, f32[32,256]{1,0:T(8,128)}, f32[32,102...) custom-call(bf16[1,1024,512]{2,1,0:T(8,128)(2,1)} %get-tuple-element, ...), custom_call_target="tpu_custom_call" | custom-call | tf_op jit(solution)/shard_map/pallas_call | solution.py:1465

commit v6 on v5

--- a/solution.py
+++ b/solution.py
@@ -1289,7 +1289,7 @@
         steps_of(0, 4),
         steps_of(1, 4) + [step_of(OUT, 2)],
         steps_of(2, 4) + steps_of(3, 3) + [step_of(OUT, 3)],
-        [step_of(GROUP, 2)],
+        [],
     ]
 
     def store_turned(kind, p, rows, value):
@@ -1357,6 +1357,7 @@
         do(after_pair[p])
         if p > 0:
             unit_grads(GROUP + p - 1, m["n1t"], dp.at[p - 1])
+    sums[GROUP].step(2)
 
 
     def first(t, _):

time: 94.7 us -> 94.7 us (level)
  no operation moved by 1% of the time
where the time goes in v6:
time: 94.7 us; the launch traced here: 94.5 us
  Pallas kernels  93.6 us (99%)
    pallas_call x1, Pallas kernels, local_staged(): pl.pallas_call(functools.partial(layer_kernel, [name for name, _, _ in it...  90.5 us
    pallas_call x1, Pallas kernels, local_staged(): pl.pallas_call(write_kernel, out_shape=shapes + [jax.ShapeDtypeStruct((1,...  3.18 us

profile of v6, /device:TPU:0, one launch (start us, length us, event | category | flops | bytes accessed | tf_op | source)
XLA Modules:
  0.0 94.5 jit_solution(4774623344160930104)
XLA Ops:
  0.6 90.5 %shard_map.220 = (bf16[1,1024,512]{2,1,0:T(8,128)(2,1)}, bf16[1,1024,512]{2,1,0:T(8,128)(2,1)}, f32[32,768]{1,0:T(8,128)}, f32[32,256]{1,0:T(8,128)}, f32[32,102...) custom-call(bf16[1,1024,512]{2,1,0:T(8,128)(2,1)} %refs_0_.1, bf16[1,1024,512]{2,1,0:T(8,128)(2,1)} %refs_1_.1, ...), custom_call_target="tpu_custom_call" | custom-call | tf_op jit(solution)/shard_map/pallas_call | solution.py:1446
  91.1 3.2 %shard_map.221 = (bf16[1,1024,512]{2,1,0:T(8,128)(2,1)}, bf16[1,1024,512]{2,1,0:T(8,128)(2,1)}, f32[32,768]{1,0:T(8,128)}, f32[32,256]{1,0:T(8,128)}, f32[32,102...) custom-call(bf16[1,1024,512]{2,1,0:T(8,128)(2,1)} %get-tuple-element, ...), custom_call_target="tpu_custom_call" | custom-call | tf_op jit(solution)/shard_map/pallas_call | solution.py:1466
